TPU v7x, 32 devices: a whole 2x2x4 slice. The times are simulated.
32 devices in a mesh: groups: 2 (over x), req: 4 (over y, core), tp: 4 (over z).
Axes of the slice: x: 2, y: 2, z: 4, core: 2. Of those that a mesh axis runs over, the one named last changes fastest.
Arguments:
- ssm_input: bfloat16 [4096, 8192], P(('groups', 'req'), 'tp'), parts along dimension 0, may hold values from -6 to 6
- gate_input: bfloat16 [4096, 8192], P(('groups', 'req'), 'tp'), parts along dimension 0, may hold values from -6 to 6
- bc_input: bfloat16 [4096, 1024], P(('groups', 'req')), parts along dimension 0, may hold values from -6 to 6
- dt_input: float32 [4096, 128], P(('groups', 'req'), 'tp'), parts along dimension 0, may hold values from -6 to 6
- decay_rate: float32 [128], P('tp'), may hold values from 0.002 to 0.15
- skip_gain: float32 [128], P('tp'), may hold values from 0.5 to 1.5
- norm_gain: float32 [8192], P('tp'), may hold values from 0.1 to 1.9
- conv_x_weight: bfloat16 [4, 8192], P(None, 'tp'), may hold values from -3 to 3
- conv_bc_weight: bfloat16 [4, 1024], replicated, may hold values from -3 to 3
- out_weight: bfloat16 [8192, 4096], P('tp'), may hold values from -0.0625 to 0.0625
- pool_states: float32 [16, 128, 64, 128], P(('groups', 'req'), 'tp'), parts along dimension 0, may hold values from -24 to 24
- pool_conv_x: bfloat16 [16, 3, 8192], P(('groups', 'req'), None, 'tp'), parts along dimension 0, may hold values from -6 to 6
- pool_conv_bc: bfloat16 [16, 3, 1024], P(('groups', 'req')), parts along dimension 0, may hold values from -6 to 6
- prefix_slot: int32 [8], P('groups'), parts along dimension 0, may hold values from 0 to 7
- prefix_spans: int32 [8], P('groups'), parts along dimension 0, may hold values from 0 to 3
- dest_slot: int32 [8], P('groups'), parts along dimension 0, may hold values from 0 to 3, each once
- suffix_len: int32 [8], P('groups'), parts along dimension 0, may hold values from 1 to 512, 1280 in all
Outputs:
- mixed: bfloat16 [4096, 4096], P(('groups', 'req'), 'tp'), parts along dimension 0
- ckpt_states: float32 [8, 128, 64, 128], P(('groups', 'req'), 'tp'), parts along dimension 0
- ckpt_conv_x: bfloat16 [8, 3, 8192], P(('groups', 'req'), None, 'tp'), parts along dimension 0
- ckpt_conv_bc: bfloat16 [8, 3, 1024], P(('groups', 'req')), parts along dimension 0
There are 2 independent parts, one for each index of `groups`. A program takes and returns all parts, laid end to end along the dimension named above; an argument that names none is the same for every part. Nothing has to cross between parts.
Inputs may be any that keep to these rules, and one draw needn't show every extreme that they name: `prefix_slot`: slot s of the pool lives on req index s // 2; several requests may share one slot. `prefix_spans`: 0 means the request has no cached prefix. `dest_slot`: all different; store slot s lives on req index s. `suffix_len`: they sum to 1280 and one equals 512.
All inputs are finite; a program needn't handle non-finite values.
Results may differ from a plain program's by a relative error of at most 0.012.
Values may be sent and summed in bfloat16 or wider, within the bound.
No kernel may reach another device: no remote copies, remote signals or barrier semaphores. Data moves between devices by JAX's collectives and lax.ppermute only.
A program may use at most 192 MiB of HBM per device.

v0:
```python
import jax
import jax.numpy as jnp
from jax import lax
from jax.sharding import PartitionSpec as P

HDIM = 64
STATE = 128
GHEADS = 32
CONV = 4
SPAN = 128
SUF = 512
REQ_DEV = 1
INNER = 8192
BCG = 4
BCW = 1024
NCH = 4


HIGH = lax.Precision.HIGHEST


def as_sent(shard):

    def short(part):
        return part.astype(jnp.bfloat16) if part.dtype == jnp.float32 else part

    return jax.tree.map(short, shard)


def causal_conv(sequence, carried, weight):
    extended = jnp.concatenate([carried, sequence.astype(jnp.float32)], axis=1)
    summed = jnp.zeros(sequence.shape, jnp.float32)
    for tap_index in range(CONV):
        summed = (
            summed
            + extended[:, tap_index : tap_index + SUF, :]
            * weight[tap_index].astype(jnp.float32)[None, None, :]
        )
    return (summed, extended)


def ssd_spans(values, step_sizes, input_map, output_map, initial, decay_rate, skip_gain):
    log_steps = -step_sizes * decay_rate[None, None, :]
    cumulative = jnp.cumsum(log_steps, axis=1)
    by_head = jnp.transpose(cumulative, (0, 2, 1))
    spread = by_head[:, :, :, None] - by_head[:, :, None, :]
    length = values.shape[1]
    causal = jnp.arange(length)[:, None] >= jnp.arange(length)[None, :]
    decay_table = jnp.where(causal, jnp.exp(jnp.where(causal, spread, 0.0)), 0.0)
    scores = jnp.einsum("cthn,cshn->chts", output_map, input_map, precision=HIGH)
    mixing = scores * decay_table * jnp.transpose(step_sizes, (0, 2, 1))[:, :, None, :]
    inside = jnp.einsum("chts,cshp->cthp", mixing, values, precision=HIGH)
    tail_weights = jnp.exp(cumulative[:, -1:, :] - cumulative) * step_sizes
    local_states = jnp.einsum(
        "cthp,cthn->chpn", values * tail_weights[..., None], input_map, precision=HIGH
    )
    span_decay = jnp.exp(cumulative[:, -1, :])

    def advance(carried, pair_in):
        advanced = pair_in[1][:, None, None] * carried + pair_in[0]
        return (advanced, carried)

    final_state, starts = lax.scan(advance, initial, (local_states, span_decay))
    across = jnp.einsum(
        "cthn,chpn->cthp", output_map * jnp.exp(cumulative)[..., None], starts, precision=HIGH
    )
    output = inside + across + skip_gain[None, None, :, None] * values
    return (output, final_state)


def per_device(
    ssm_input,
    gate_input,
    bc_input,
    dt_input,
    decay_rate,
    skip_gain,
    norm_gain,
    conv_x_weight,
    conv_bc_weight,
    out_weight,
    pool_states,
    pool_conv_x,
    pool_conv_bc,
    prefix_slot,
    prefix_spans,
    dest_slot,
    suffix_len,
):
    num_req = lax.axis_size("req")
    my_index = lax.axis_index("req")
    heads_dev = dt_input.shape[1]
    inner_dev = ssm_input.shape[1]
    first_mine = my_index * REQ_DEV
    my_len = lax.dynamic_slice_in_dim(suffix_len, first_mine, REQ_DEV, 0)
    my_slot = lax.dynamic_slice_in_dim(prefix_slot, first_mine, REQ_DEV, 0)
    my_present = lax.dynamic_slice_in_dim(prefix_spans, first_mine, REQ_DEV, 0) > 0
    my_dest = lax.dynamic_slice_in_dim(dest_slot, first_mine, REQ_DEV, 0)
    pool_x_f = pool_conv_x.astype(jnp.float32)
    pool_bc_f = pool_conv_bc.astype(jnp.float32)
    empty = (
        jnp.zeros((REQ_DEV,) + pool_states.shape[1:], jnp.float32),
        jnp.zeros((REQ_DEV,) + pool_x_f.shape[1:], jnp.float32),
        jnp.zeros((REQ_DEV,) + pool_bc_f.shape[1:], jnp.float32),
    )
    pieces = (
        lax.all_gather(pool_states.astype(jnp.bfloat16), "req", axis=0, tiled=True).astype(
            jnp.float32
        ),
        lax.all_gather(pool_x_f.astype(jnp.bfloat16), "req", axis=0, tiled=True).astype(
            jnp.float32
        ),
        lax.all_gather(pool_bc_f.astype(jnp.bfloat16), "req", axis=0, tiled=True).astype(
            jnp.float32
        ),
    )
    row_count = pieces[0].shape[0]
    hits = (my_slot[:, None] == jnp.arange(row_count)[None, :]).astype(jnp.float32)
    new_states = empty[0] + jnp.einsum("rs,shpn->rhpn", hits, pieces[0], precision=HIGH)
    new_x = empty[1] + jnp.einsum("rs,skc->rkc", hits, pieces[1], precision=HIGH)
    new_bc = empty[2] + jnp.einsum("rs,skc->rkc", hits, pieces[2], precision=HIGH)
    start_states = jnp.where(my_present[:, None, None, None], new_states, 0.0)
    start_x = jnp.where(my_present[:, None, None], new_x, 0.0)
    start_bc = jnp.where(my_present[:, None, None], new_bc, 0.0)
    positions = jnp.arange(SUF, dtype=jnp.int32)
    live_mask = (positions[None, :] < my_len[:, None]).astype(jnp.float32)
    conv_x, extended_x = causal_conv(
        ssm_input.reshape(REQ_DEV, SUF, inner_dev), start_x, conv_x_weight
    )
    values = jax.nn.silu(conv_x).astype(jnp.bfloat16)
    conv_bc, extended_bc = causal_conv(
        bc_input.reshape(REQ_DEV, SUF, BCW), start_bc, conv_bc_weight
    )
    maps = jax.nn.silu(conv_bc).astype(jnp.bfloat16)

    def tail_rows(extended, count):
        return lax.dynamic_slice_in_dim(extended, count, CONV - 1, 0)

    new_conv_x = jax.vmap(tail_rows)(extended_x, my_len)
    new_conv_bc = jax.vmap(tail_rows)(extended_bc, my_len)
    step_sizes = jax.nn.softplus(dt_input).reshape(REQ_DEV, SUF, heads_dev) * live_mask[:, :, None]
    head_ids = lax.axis_index("tp") * heads_dev + jnp.arange(heads_dev)
    group_pick = (head_ids[:, None] // GHEADS == jnp.arange(BCG)[None, :]).astype(jnp.float32)
    maps_f = maps.astype(jnp.float32).reshape(REQ_DEV, NCH, SPAN, 2, BCG, STATE)
    input_map = jnp.einsum("rclgn,hg->rclhn", maps_f[:, :, :, 0], group_pick, precision=HIGH)
    output_map = jnp.einsum("rclgn,hg->rclhn", maps_f[:, :, :, 1], group_pick, precision=HIGH)
    values_f = values.astype(jnp.float32).reshape(REQ_DEV, NCH, SPAN, heads_dev, HDIM)
    steps_c = step_sizes.reshape(REQ_DEV, NCH, SPAN, heads_dev)

    def one_request(values_r, steps_r, input_r, output_r, initial_r):
        return ssd_spans(values_r, steps_r, input_r, output_r, initial_r, decay_rate, skip_gain)

    outputs, finals = jax.vmap(one_request)(values_f, steps_c, input_map, output_map, start_states)
    total_rows = REQ_DEV * SUF
    placer = (my_dest[None, :] == jnp.arange(num_req * REQ_DEV)[:, None]).astype(jnp.float32)
    out_states = jnp.einsum("tr,rhpn->thpn", placer, finals, precision=HIGH).reshape(
        (num_req, REQ_DEV) + finals.shape[1:]
    )
    out_x = jnp.einsum("tr,rkc->tkc", placer, new_conv_x, precision=HIGH).reshape(
        (num_req, REQ_DEV) + new_conv_x.shape[1:]
    )
    out_bc = jnp.einsum("tr,rkc->tkc", placer, new_conv_bc, precision=HIGH).reshape(
        (num_req, REQ_DEV) + new_conv_bc.shape[1:]
    )
    landed_states, landed_x, landed_bc = (
        lax.all_to_all(as_sent(out_states), "req", split_axis=0, concat_axis=0, tiled=True).astype(
            out_states.dtype
        ),
        lax.all_to_all(as_sent(out_x), "req", split_axis=0, concat_axis=0, tiled=True).astype(
            out_x.dtype
        ),
        lax.all_to_all(as_sent(out_bc), "req", split_axis=0, concat_axis=0, tiled=True).astype(
            out_bc.dtype
        ),
    )
    ckpt_states = jnp.sum(landed_states, axis=0)
    ckpt_conv_x = jnp.sum(landed_x, axis=0).astype(jnp.bfloat16)
    ckpt_conv_bc = jnp.sum(landed_bc, axis=0).astype(jnp.bfloat16)
    gated = outputs.reshape(total_rows, inner_dev) * jax.nn.silu(gate_input.astype(jnp.float32))
    square_total = lax.psum(jnp.sum(gated * gated, axis=1), "tp")
    normed = (gated * lax.rsqrt(square_total / INNER + 1e-05)[:, None] * norm_gain[None, :]).astype(
        jnp.bfloat16
    )
    reduced = lax.psum_scatter(
        lax.dot_general(
            out_weight, normed, (((0,), (1,)), ((), ())), preferred_element_type=jnp.float32
        ).astype(jnp.bfloat16),
        "tp",
        scatter_dimension=0,
        tiled=True,
    ).astype(jnp.float32)
    mixed = (reduced.T * live_mask.reshape(total_rows)[:, None]).astype(jnp.bfloat16)
    return (mixed, ckpt_states, ckpt_conv_x, ckpt_conv_bc)


def solution(mesh):
    return jax.shard_map(
        per_device,
        mesh=mesh,
        in_specs=(
            P(("groups", "req"), "tp"),
            P(("groups", "req"), "tp"),
            P(("groups", "req"), None),
            P(("groups", "req"), "tp"),
            P("tp"),
            P("tp"),
            P("tp"),
            P(None, "tp"),
            P(),
            P("tp", None),
            P(("groups", "req"), "tp", None, None),
            P(("groups", "req"), None, "tp"),
            P(("groups", "req"), None, None),
            P("groups"),
            P("groups"),
            P("groups"),
            P("groups"),
        ),
        out_specs=(
            P(("groups", "req"), "tp"),
            P(("groups", "req"), "tp", None, None),
            P(("groups", "req"), None, "tp"),
            P(("groups", "req"), None, None),
        ),
        check_vma=False,
    )
```

profile of v0, /device:TPU:0, one launch (start us, length us, event | category | flops | bytes accessed | tf_op | source)
XLA Modules:
  0.0 287.4 jit_solution(12276298086072607401)
XLA Ops:
  7.3 2.9 %convert_element_type.197 = bf16[2,32,64,128]{3,2,1,0:T(8,128)(2,1)} convert(f32[2,32,64,128]{3,2,1,0:T(8,128)} %param.29) | non-fusion elementwise | flops 524288 | bytes 3145728 | tf_op jit(solution)/shard_map/convert_element_type | solution.py:107
  12.9 6.5 %all_gather.9 = bf16[8,3,2048]{2,1,0:T(4,128)(2,1)S(1)} all-gather(bf16[2,3,2048]{2,1,0:T(4,128)(2,1)S(1)} %copy.53), channel_id=1, replica_groups=mesh['groups'=2,'req'=4,'tp'=4] {'req'}, dimensions={0}, use_global_device_ids=true | all-gather | bytes 122880 | tf_op jit(solution)/shard_map/all_gather | solution.py:110
  22.2 2.7 multiply_convert_fusion.2
  25.7 3.0 %copy.65 = f32[1,512,2048]{1,2,0:T(8,128)} copy(bf16[1,512,2048]{2,1,0:T(8,128)(2,1)S(1)} %multiply_convert_fusion.2) | data formatting | bytes 6291456 | tf_op jit(solution)/shard_map/convert_element_type | solution.py:147
  28.7 5.3 %reshape.461 = bf16[4,128,32,64]{3,2,1,0:T(8,128)(2,1)} reshape(bf16[1,512,2048]{2,1,0:T(8,128)(2,1)S(1)} %multiply_convert_fusion.2) | data formatting | bytes 4194304 | tf_op jit(solution)/shard_map/reshape.44
  34.6 6.9 %copy.73 = f32[1,512,2048]{1,0,2:T(1,128)} copy(bf16[1,512,2048]{2,1,0:T(8,128)(2,1)S(1)} %multiply_convert_fusion.2) | data formatting | bytes 6291456 | tf_op jit(solution)/shard_map/convert_element_type | solution.py:147
  41.7 5.4 %reshape.386 = f32[4,128,32,64]{1,0,3,2:T(4,128)} reshape(f32[1,512,2048]{1,2,0:T(8,128)} %copy.65) | data formatting | bytes 8388608 | tf_op jit(solution)/shard_map/reshape | solution.py:147
  47.0 5.6 %all_gather.10 = bf16[8,3,1024]{2,1,0:T(4,128)(2,1)S(1)} all-gather(bf16[2,3,1024]{2,1,0:T(4,128)(2,1)S(1)} %copy.55), channel_id=1, replica_groups=mesh['groups'=2,'req'=4,'tp'=4] {'req'}, dimensions={0}, use_global_device_ids=true | all-gather | bytes 61440 | tf_op jit(solution)/shard_map/all_gather | solution.py:113
  53.7 2.2 multiply_convert_fusion.5
  55.9 1.8 reshape.380
  58.5 3.9 %copy.76 = bf16[512,2048]{0,1:T(8,128)(2,1)} copy(bf16[512,2048]{1,0:T(8,128)(2,1)} %param.20) | data formatting | bytes 4194304 | tf_op args[1]
  62.4 3.1 %broadcast_multiply_fusion = f32[4,128,32,64]{1,0,3,2:T(4,128)S(1)} fusion(f32[4,128,32,64]{1,0,3,2:T(4,128)} %reshape.386, f32[4,128,32]{1,0,2:T(4,128)S(1)} %copy.67), kind=kLoop, calls=%fused_computation.84 | loop fusion | flops 1048576 | bytes 8454144 | tf_op jit(solution)/shard_map/vmap()/mul | solution.py:55
  68.2 12.6 %fusion.41 = f32[4,1,32,64,128]{4,3,2,1,0:T(8,128)} fusion(f32[4,128,32,128]{3,2,1,0:T(8,128)S(1)} %convolution_bitcast_fusion, f32[4,128,32,64]{1,0,3,2:T(4,128)S(1)} %broadcast_multiply_fusion), kind=kOutput, calls=%fused_computation.69 | convolution fusion | flops 1610612736 | bytes 16777216 | tf_op jit(solution)/shard_map/vmap(cthp,cthn->chpn)/dot_general | solution.py:54
  80.8 4.6 %fusion.1 = f32[4,128,32,128]{3,2,1,0:T(8,128)} fusion(f32[32,4,128,128]{3,0,2,1:T(8,128)S(1)} %fusion.64, f32[4,128,32]{2,1,0:T(8,128)S(1)} %copy-done.6), kind=kLoop, calls=%fused_computation.9 | loop fusion | flops 2097152 | bytes 16842752 | tf_op jit(solution)/shard_map/reshape.58
  85.4 25.8 %fusion.4 = f32[4,32,128,128]{3,2,1,0:T(8,128)} fusion(f32[4,128,32,128]{3,2,1,0:T(8,128)S(1)} %bitcast.172, f32[4,128,32,128]{3,2,1,0:T(8,128)S(1)} %convolution_bitcast_fusion), kind=kOutput, calls=%fused_computation.12 | convolution fusion | flops 3221225472 | bytes 25165824 | tf_op jit(solution)/shard_map/vmap(cthn,cshn->chts)/dot_general | solution.py:50
  111.2 16.1 %fusion.6 = f32[4,32,64,128]{3,2,1,0:T(8,128)} fusion(f32[4,32,128,128]{3,2,1,0:T(8,128)} %fusion.4, bf16[4,128,32,64]{3,2,1,0:T(8,128)(2,1)} %reshape.461, f32[4,32,128]{2,1,0:T(8,128)S(1)} %bitcast.180, f32[4,32,128]{2,1,0:T(8,128)S(1)} %copy-done.7, pred[128,128]{1,0:T(8,128)(4,1)S(1)} %iota_compare_fusion), kind=kOutput, calls=%fused_computation.14 | convolution fusion | flops 1621098496 | bytes 14827520 | tf_op jit(solution)/shard_map/vmap(chts,cshp->cthp)/dot_general | solution.py:52
  127.4 5.6 %fusion.33 = f32[1,32,64,128]{3,0,2,1:T(1,128)S(1)} fusion(bf16[8,32,64,128]{3,2,1,0:T(8,128)(2,1)} %all-gather.2.cloned.1.call-done, s32[]{:T(128)} %bitcast.4), kind=kOutput, calls=%fused_computation.51 | convolution fusion | flops 4194312 | bytes 5242884 | tf_op jit(solution)/shard_map/rs,shpn->rhpn/dot_general | solution.py:119
  133.1 10.2 %while.14 = (s32[]{:T(128)}, f32[1,32,64,128]{3,2,1,0:T(8,128)S(1)}, f32[4,1,32,64,128]{4,3,2,1,0:T(8,128)}, f32[4,1,32]{2,1,0:T(1,128)S(1)}, f32[4,1,32,64,128]{4,3,2,1,0:T(8,128)}, /*index=5*/s32[]{:T(128)}) while((s32[]{:T(128)}, f32[1,32,64,128]{3,2,1,0:T(8,128)S(1)}, f32[4,1,32,64,128]{4,3,2,1,0:T(8,128)}, f32[4,1,32]{2,1,0:T(1,128)S(1)}, ...), condition=%wide.region_2.3_spmd, body=%wide.region_1.2_spmd.sunk | while | flops 524290 | bytes 5243853 | solution.py:63
  143.2 23.0 %bitcast_add_fusion.1 = f32[1,4,128,32,64]{2,4,3,1,0:T(8,128)S(1)} fusion(f32[1,4,128,32,64]{2,1,0,4,3:T(4,128)} %bitcast.173, f32[4,32,64,128]{3,2,1,0:T(8,128)} %fusion.6, f32[4,128,32,128]{3,2,1,0:T(8,128)} %fusion.1, f32[4,1,32,64,128]{4,3,2,1,0:T(8,128)} %get-tuple-element.32, f32[32]{0:T(128)S(1)} %copy-done.14), kind=kOutput, calls=%fused_computation.48 | convolution fusion | flops 1613758464 | bytes 25165952 | tf_op jit(solution)/shard_map/vmap(cthn,chpn->cthp)/dot_general | solution.py:64
  166.2 3.6 %copy.75 = f32[1,4,128,32,64]{2,1,4,3,0:T(4,128)S(1)} copy(f32[1,4,128,32,64]{2,4,3,1,0:T(8,128)S(1)} %bitcast_add_fusion.1) | data formatting | bytes 8388608 | tf_op jit(solution)/shard_map/vmap()/add | solution.py:67
  169.9 2.1 copy-done.1
  173.3 12.1 %psum.7 = f32[512]{0:T(512)S(1)} all-reduce(f32[512]{0:T(512)S(1)} %multiply_reduce_fusion), channel_id=1, replica_groups=mesh['groups'=2,'req'=4,'tp'=4] {'tp'}, use_global_device_ids=true, to_apply=%region_4.5 | all-reduce | flops 512 | bytes 4096 | tf_op jit(solution)/shard_map/psum | solution.py:180
  185.5 17.2 %fusion.16 = bf16[4096,512]{0,1:T(8,128)(2,1)} fusion(bf16[2048,4096]{1,0:T(8,128)(2,1)} %param.28, f32[2048]{0:T(1024)S(1)} %copy-done.16, f32[512]{0:T(512)S(1)} %add_rsqrt_fusion, bf16[512,2048]{0,1:T(8,128)(2,1)} %copy.76, f32[256,8,4,128]{3,2,1,0:T(4,128)} %bitcast.175), kind=kOutput, calls=%fused_computation.25 | convolution fusion | flops 8601468928 | bytes 27273216 | tf_op jit(solution)/shard_map/dot_general | solution.py:185
  206.6 3.3 %all-to-all-start.2 = ((bf16[4,1,3,1024]{3,2,1,0:T(4,128)(2,1)}), bf16[4,1,3,1024]{3,2,1,0:T(4,128)(2,1)S(1)}, u32[]{:S(2)}, u32[]{:S(2)}) async-start(bf16[4,1,3,1024]{3,2,1,0:T(4,128)(2,1)} %fusion.74), calls=%async_computation.3 | async-start | bytes 65536 | tf_op jit(solution)/shard_map/all_to_all | solution.py:172
  211.5 2.2 all-to-all-done.2
  213.8 3.3 %all-to-all-start.1 = ((bf16[4,1,3,2048]{3,2,1,0:T(4,128)(2,1)}), bf16[4,1,3,2048]{3,2,1,0:T(4,128)(2,1)S(1)}, u32[]{:S(2)}, u32[]{:S(2)}) async-start(bf16[4,1,3,2048]{3,2,1,0:T(4,128)(2,1)} %fusion.69), calls=%async_computation.2 | async-start | bytes 131072 | tf_op jit(solution)/shard_map/all_to_all | solution.py:169
  217.1 2.0 fusion.52
  219.0 2.1 all-to-all-done.1
  221.1 3.6 %all-to-all-start = ((bf16[4,1,32,64,128]{4,3,2,1,0:T(8,128)(2,1)}), bf16[4,1,32,64,128]{4,3,2,1,0:T(8,128)(2,1)S(1)}, u32[]{:S(2)}, u32[]{:S(2)}) async-start(bf16[4,1,32,64,128]{4,3,2,1,0:T(8,128)(2,1)} %fusion.52), calls=%async_computation.1 | async-start | bytes 4194304 | tf_op jit(solution)/shard_map/all_to_all | solution.py:166
  226.0 24.4 %all-to-all-done = bf16[4,1,32,64,128]{4,3,2,1,0:T(8,128)(2,1)S(1)} async-done(((bf16[4,1,32,64,128]{4,3,2,1,0:T(8,128)(2,1)}), bf16[4,1,32,64,128]{4,3,2,1,0:T(8,128)(2,1)S(1)}, u32[]{:S(2)}, u32[]{:S(2)}) %all-to-all-start) | async-done | bytes 2097184 | tf_op jit(solution)/shard_map/all_to_all | solution.py:166
  251.8 26.1 %reduce-scatter.2.cloned.1.call-done = bf16[1024,512]{0,1:T(8,128)(2,1)} async-done(((bf16[4096,512]{0,1:T(8,128)(2,1)}), bf16[1024,512]{0,1:T(8,128)(2,1)}) %reduce-scatter.2.cloned.1.call-update) | async-done | bytes 1048592 | tf_op jit(solution)/shard_map/reduce_scatter | solution.py:184
  277.9 2.4 fusion.63
  (100 shorter events, 28.5 us)
Async XLA Ops:
  7.2 3.1 %copy-start.17 = (s32[4]{0:T(128)S(1)}, s32[4]{0:T(128)}, u32[]{:S(2)}) copy-start(s32[4]{0:T(128)} %param.35) | copy-start | bytes 52
  7.2 4.4 %copy-start.8 = (f32[512,32]{0,1:T(8,128)S(1)}, f32[512,32]{0,1:T(8,128)}, u32[]{:S(2)}) copy-start(f32[512,32]{0,1:T(8,128)} %param.22) | copy-start | bytes 196612
  7.2 4.7 %copy-start.15 = (f32[32]{0:T(128)S(1)}, f32[32]{0:T(128)}, u32[]{:S(2)}) copy-start(f32[32]{0:T(128)} %param.23) | copy-start | bytes 388
  7.2 5.0 %copy-start.18 = (s32[4]{0:T(128)S(1)}, s32[4]{0:T(128)}, u32[]{:S(2)}) copy-start(s32[4]{0:T(128)} %param.32) | copy-start | bytes 52
  7.2 5.6 %copy-start.12 = (bf16[2,3,2048]{2,0,1:T(2,128)(2,1)S(1)}, bf16[2,3,2048]{2,0,1:T(2,128)(2,1)}, u32[]{:S(2)}) copy-start(bf16[2,3,2048]{2,0,1:T(2,128)(2,1)} %param.30) | copy-start | bytes 73732
  7.2 12.2 %copy-start.19 = (s32[4]{0:T(128)S(1)}, s32[4]{0:T(128)}, u32[]{:S(2)}) copy-start(s32[4]{0:T(128)} %param.33) | copy-start | bytes 52
  7.2 12.7 %copy-start.10 = (bf16[4,2048]{1,0:T(4,128)(2,1)S(1)}, bf16[4,2048]{1,0:T(4,128)(2,1)}, u32[]{:S(2)}) copy-start(bf16[4,2048]{1,0:T(4,128)(2,1)} %param.26) | copy-start | bytes 49156
  7.2 12.8 %copy-start.2 = (bf16[512,2048]{1,0:T(8,128)(2,1)S(1)}, bf16[512,2048]{1,0:T(8,128)(2,1)}, u32[]{:S(2)}) copy-start(bf16[512,2048]{1,0:T(8,128)(2,1)} %param.19) | copy-start | bytes 6291460
  7.2 120.1 %all-gather.2.cloned.1.call-start = ((), (), s32[]{:S(2)}) async-start(), calls=%async_computation.4 | async-start | bytes 5242880 | tf_op jit(solution)/shard_map/all_gather | solution.py:107
  10.2 267.6 %reduce-scatter.2.cloned.1.call-start = ((), (), s32[]{:S(2)}) async-start(), calls=%async_computation.5 | async-start | bytes 5242880 | tf_op jit(solution)/shard_map/reduce_scatter | solution.py:184
  12.2 9.9 %copy-start.3 = (bf16[512,2048]{1,0:T(8,128)(2,1)S(1)}, bf16[512,2048]{1,0:T(8,128)(2,1)}, u32[]{:S(2)}) copy-start(bf16[512,2048]{1,0:T(8,128)(2,1)} %param.19) | copy-start | bytes 6291460
  20.6 4.4 %copy-start = (f32[1,512,2048]{2,1,0:T(8,128)}, f32[1,512,2048]{2,1,0:T(8,128)S(1)}, u32[]{:S(2)}) copy-start(f32[1,512,2048]{2,1,0:T(8,128)S(1)} %convert_bitcast_fusion) | copy-start | bytes 12582916
  41.6 5.4 %copy-start.13 = (bf16[2,3,1024]{2,0,1:T(2,128)(2,1)S(1)}, bf16[2,3,1024]{2,0,1:T(2,128)(2,1)}, u32[]{:S(2)}) copy-start(bf16[2,3,1024]{2,0,1:T(2,128)(2,1)} %param.31) | copy-start | bytes 36868
  41.6 11.0 %copy-start.11 = (bf16[4,1024]{1,0:T(4,128)(2,1)S(1)}, bf16[4,1024]{1,0:T(4,128)(2,1)}, u32[]{:S(2)}) copy-start(bf16[4,1024]{1,0:T(4,128)(2,1)} %param.27) | copy-start | bytes 24580
  41.6 11.8 %copy-start.5 = (bf16[512,1024]{1,0:T(8,128)(2,1)S(1)}, bf16[512,1024]{1,0:T(8,128)(2,1)}, u32[]{:S(2)}) copy-start(bf16[512,1024]{1,0:T(8,128)(2,1)} %param.21) | copy-start | bytes 3145732
  68.2 12.6 %copy-start.6 = (f32[4,128,32]{2,1,0:T(8,128)S(1)}, f32[4,128,32]{2,1,0:T(8,128)}, u32[]{:S(2)}) copy-start(f32[4,128,32]{2,1,0:T(8,128)} %get-tuple-element.82) | copy-start | bytes 196612
  85.4 25.8 %copy-start.7 = (f32[4,32,128]{2,1,0:T(8,128)S(1)}, f32[4,32,128]{2,1,0:T(8,128)}, u32[]{:S(2)}) copy-start(f32[4,32,128]{2,1,0:T(8,128)} %copy.61) | copy-start | bytes 196612
  85.4 25.8 %copy-start.9 = (f32[1,4,128,32]{2,3,1,0:T(8,128)S(1)}, f32[1,4,128,32]{2,3,1,0:T(8,128)}, u32[]{:S(2)}) copy-start(f32[1,4,128,32]{2,3,1,0:T(8,128)} %copy.126) | copy-start | bytes 196612
  133.0 10.2 %copy-start.14 = (f32[32]{0:T(128)S(1)}, f32[32]{0:T(128)}, u32[]{:S(2)}) copy-start(f32[32]{0:T(128)} %param.24) | copy-start | bytes 388
  166.2 5.7 %copy-start.4 = (bf16[512,2048]{0,1:T(8,128)(2,1)S(1)}, bf16[512,2048]{0,1:T(8,128)(2,1)}, u32[]{:S(2)}) copy-start(bf16[512,2048]{0,1:T(8,128)(2,1)} %copy.76) | copy-start | bytes 6291460
  169.8 2.1 copy-start.1
  169.8 15.6 %copy-start.16 = (f32[2048]{0:T(1024)S(1)}, f32[2048]{0:T(1024)}, u32[]{:S(2)}) copy-start(f32[2048]{0:T(1024)} %param.25) | copy-start | bytes 24580
  202.7 0.7 copy-start.20
  206.6 7.2 %all-to-all-start.2 = ((bf16[4,1,3,1024]{3,2,1,0:T(4,128)(2,1)}), bf16[4,1,3,1024]{3,2,1,0:T(4,128)(2,1)S(1)}, u32[]{:S(2)}, u32[]{:S(2)}) async-start(bf16[4,1,3,1024]{3,2,1,0:T(4,128)(2,1)} %fusion.74), calls=%async_computation.3 | async-start | bytes 65536 | tf_op jit(solution)/shard_map/all_to_all | solution.py:172
  213.8 7.4 %all-to-all-start.1 = ((bf16[4,1,3,2048]{3,2,1,0:T(4,128)(2,1)}), bf16[4,1,3,2048]{3,2,1,0:T(4,128)(2,1)S(1)}, u32[]{:S(2)}, u32[]{:S(2)}) async-start(bf16[4,1,3,2048]{3,2,1,0:T(4,128)(2,1)} %fusion.69), calls=%async_computation.2 | async-start | bytes 131072 | tf_op jit(solution)/shard_map/all_to_all | solution.py:169
  221.1 29.3 %all-to-all-start = ((bf16[4,1,32,64,128]{4,3,2,1,0:T(8,128)(2,1)}), bf16[4,1,32,64,128]{4,3,2,1,0:T(8,128)(2,1)S(1)}, u32[]{:S(2)}, u32[]{:S(2)}) async-start(bf16[4,1,32,64,128]{4,3,2,1,0:T(8,128)(2,1)} %fusion.52), calls=%async_computation.1 | async-start | bytes 4194304 | tf_op jit(solution)/shard_map/all_to_all | solution.py:166
Sparse Core Ops, SparseCore 0:
  10.4 37.1 all-gather.1
  202.8 74.9 reduce-scatter.1
where the time goes:
time: 293 us; the launch traced here: 287 us
  matrix products  105 us (36%)
  waiting for transfers between devices  54.9 us (19%)
  local copies, waits for them, and re-layouts  40.5 us (14%)
  other arithmetic  35.5 us (12%)
  blocking collectives  24.2 us (8%)
  between operations  17.3 us (6%)
  starting transfers between devices  10.2 us (3%)
    reduce_scatter x1, waiting for transfers between devices, per_device(): lax.psum_scatter(lax.dot_general(out_weight, normed, (((0,), (1,)), ((),...  26.1 us
    dot_general x1, matrix products, ssd_spans(): jnp.einsum('cthn,cshn->chts', output_map, input_map, precision=HIGH)  25.8 us
    all_to_all x1, waiting for transfers between devices, per_device(): lax.all_to_all(as_sent(out_states), 'req', split_axis=0, concat_axis=0, t...  24.4 us
    dot_general x1, matrix products, ssd_spans(): jnp.einsum('cthn,chpn->cthp', output_map * jnp.exp(cumulative)[..., None]...  23 us
    dot_general x1, matrix products, per_device(): lax.dot_general(out_weight, normed, (((0,), (1,)), ((), ())), preferred_e...  17.2 us
    dot_general x1, matrix products, ssd_spans(): inside = jnp.einsum('chts,cshp->cthp', mixing, values, precision=HIGH)  16.1 us
    dot_general x1, matrix products, ssd_spans(): jnp.einsum('cthp,cthn->chpn', values * tail_weights[..., None], input_map...  12.6 us
    psum x1, blocking collectives, per_device(): square_total = lax.psum(jnp.sum(gated * gated, axis=1), 'tp')  12.1 us
  transfers between devices with their start and end apart: 5, of which 4 were waited for; matrix products, arithmetic and copies ran while one was open for 39% of the time, Pallas kernels for 0%

commit v1 on v0

v1 whole, which is shorter than its diff:
```python
import functools

import jax
import jax.numpy as jnp
from jax import lax
from jax.experimental import pallas as pl
from jax.experimental.pallas import tpu as pltpu
from jax.sharding import PartitionSpec as P

HDIM = 64
STATE = 128
GHEADS = 32
CONV = 4
SPAN = 128
SUF = 512
INNER = 8192
BCG = 4
BCW = 1024
NCH = 4
LANES = 128
WIDE = 512

F32 = jnp.float32
BF16 = jnp.bfloat16
HIGH = lax.Precision.HIGHEST


def silu(x):
    half = 0.5 * x
    return half + half * jnp.tanh(half)


def split_pair(x, heads):
    lane = lax.broadcasted_iota(jnp.int32, x.shape, 1)
    high = x.astype(BF16).astype(F32)
    rest = jnp.where(lane < 2 * heads, x - high, 0.0)
    return jnp.where(lane < heads, high, rest).astype(BF16)


def dot(a, b):
    return jnp.dot(a, b, preferred_element_type=F32)


def dot_t(a, b):
    return lax.dot_general(a, b, (((1,), (1,)), ((), ())), preferred_element_type=F32)


def conv_taps(before, x, weight):
    extended = jnp.concatenate([before, x], axis=0)
    total = extended[8:] * weight[CONV - 1 :]
    for k in range(CONV - 1):
        total += extended[5 + k : 5 + k + SPAN] * weight[k : k + 1]
    return total


def scan_kernel(
    heads,
    meta,
    x_ref,
    b_ref,
    c_ref,
    dt_ref,
    rate_ref,
    skip_ref,
    wx_ref,
    wb_ref,
    wc_ref,
    sx_ref,
    sb_ref,
    sc_ref,
    pick_ref,
    y_ref,
    final_ref,
    cmap_ref,
    reach_ref,
    total_ref,
    state,
    tail_x,
    tail_m,
    left,
    bmap_t,
    fac_a,
    fac_b,
    fac_row,
    base,
):
    block = pl.program_id(0)
    c = pl.program_id(1)

    @pl.when(block == 0)
    def _():
        maps = []
        for k, (ref, w, s) in enumerate(((b_ref, wb_ref, sb_ref), (c_ref, wc_ref, sc_ref))):
            before = jnp.where(c == 0, s[...], tail_m[k])
            x = ref[...].astype(F32)
            maps.append(silu(conv_taps(before, x, w[...].astype(F32))).astype(BF16))
            tail_m[k] = x[SPAN - 8 :]
        bmap, cmap = maps
        row = lax.broadcasted_iota(jnp.int32, (SPAN, SPAN), 0)
        col = lax.broadcasted_iota(jnp.int32, (SPAN, SPAN), 1)
        scores = jnp.where(row >= col, dot_t(cmap, bmap), 0.0).astype(BF16)
        left[c, :, :SPAN] = scores
        left[c, :, SPAN:] = cmap
        cmap_ref[...] = cmap
        bmap_t[c] = jnp.transpose(bmap.astype(F32)).astype(BF16)

        @pl.when(c == 0)
        def _():
            base[...] = jnp.zeros_like(base)

        logit = dt_ref[...]
        live = (row + c * SPAN < meta[1]).astype(F32)
        step = (jnp.maximum(logit, 0.0) + jnp.log1p(jnp.exp(-jnp.abs(logit)))) * live
        cum = jnp.dot(
            (row >= col).astype(F32),
            -step * rate_ref[...],
            precision=HIGH,
            preferred_element_type=F32,
        )
        last = cum[SPAN - 1 :]
        mid = 0.5 * last
        fac_a[c] = split_pair(jnp.exp(cum - mid), heads)
        fac_b[c] = split_pair(jnp.exp(mid - cum) * step, heads)
        before = base[0:1]
        reach_ref[...] = split_pair(jnp.exp(before + cum), heads)
        which = lax.broadcasted_iota(jnp.int32, (16, LANES), 0)
        fac_row[c] = split_pair(
            jnp.where(which == 0, jnp.exp(mid), jnp.exp(last - mid)) + jnp.zeros((16, LANES), F32),
            heads,
        )
        base[...] = base[...] + last
        total_ref[...] = jnp.exp(base[...])

    @pl.when(c == 0)
    def _():
        state[...] = jnp.zeros_like(state)
        tail_x[...] = sx_ref[...]

    pick = pick_ref[...]
    x = x_ref[...].astype(F32)
    conv = conv_taps(tail_x[...], x, wx_ref[...].astype(F32))
    tail_x[...] = x[SPAN - 8 :]
    values = silu(conv).astype(BF16).astype(F32)
    scaled = (values * dot(fac_b[c], pick)).astype(BF16)
    rows = dot(fac_row[c], pick)
    held = state[...] * rows[0:1]
    right = jnp.concatenate([scaled, held.astype(BF16)], axis=0)
    y_ref[...] = dot(left[c], right) * dot(fac_a[c], pick) + skip_ref[...] * values
    state[...] = (held + dot(bmap_t[c], scaled)) * rows[1:2]

    @pl.when(c == NCH - 1)
    def _():
        final_ref[...] = jnp.transpose(state[...])


def run_scan(meta, x, bc, dt, rate, skip, wx, wbc, sx, sbc, pick, heads):
    inner = x.shape[1]
    blocks = inner // WIDE
    once = lambda b, c: jnp.where(b == 0, c, NCH - 1)
    in_specs = [
        pl.BlockSpec((SPAN, WIDE), lambda b, c, m: (c, b)),
        pl.BlockSpec((SPAN, LANES), lambda b, c, m: (once(b, c), m[0])),
        pl.BlockSpec((SPAN, LANES), lambda b, c, m: (once(b, c), m[0] + BCG)),
        pl.BlockSpec((SPAN, LANES), lambda b, c, m: (once(b, c), 0)),
        pl.BlockSpec((1, LANES), lambda b, c, m: (0, 0)),
        pl.BlockSpec((1, WIDE), lambda b, c, m: (0, b)),
        pl.BlockSpec((CONV, WIDE), lambda b, c, m: (0, b)),
        pl.BlockSpec((CONV, LANES), lambda b, c, m: (0, m[0])),
        pl.BlockSpec((CONV, LANES), lambda b, c, m: (0, m[0] + BCG)),
        pl.BlockSpec((8, WIDE), lambda b, c, m: (0, b)),
        pl.BlockSpec((8, LANES), lambda b, c, m: (0, m[0])),
        pl.BlockSpec((8, LANES), lambda b, c, m: (0, m[0] + BCG)),
        pl.BlockSpec((LANES, WIDE), lambda b, c, m: (0, b)),
    ]
    out_specs = [
        pl.BlockSpec((SPAN, WIDE), lambda b, c, m: (c, b)),
        pl.BlockSpec((WIDE, STATE), lambda b, c, m: (b, 0)),
        pl.BlockSpec((SPAN, LANES), lambda b, c, m: (once(b, c), 0)),
        pl.BlockSpec((SPAN, LANES), lambda b, c, m: (once(b, c), 0)),
        pl.BlockSpec((8, LANES), lambda b, c, m: (0, 0)),
    ]
    return pl.pallas_call(
        functools.partial(scan_kernel, heads),
        grid_spec=pltpu.PrefetchScalarGridSpec(
            num_scalar_prefetch=1,
            grid=(blocks, NCH),
            in_specs=in_specs,
            out_specs=out_specs,
            scratch_shapes=[
                pltpu.VMEM((STATE, WIDE), F32),
                pltpu.VMEM((8, WIDE), F32),
                pltpu.VMEM((2, 8, LANES), F32),
                pltpu.VMEM((NCH, SPAN, 2 * SPAN), BF16),
                pltpu.VMEM((NCH, STATE, SPAN), BF16),
                pltpu.VMEM((NCH, SPAN, LANES), BF16),
                pltpu.VMEM((NCH, SPAN, LANES), BF16),
                pltpu.VMEM((NCH, 16, LANES), BF16),
                pltpu.VMEM((8, LANES), F32),
            ],
        ),
        out_shape=[
            jax.ShapeDtypeStruct((SUF, inner), F32),
            jax.ShapeDtypeStruct((inner, STATE), F32),
            jax.ShapeDtypeStruct((SUF, LANES), BF16),
            jax.ShapeDtypeStruct((SUF, LANES), BF16),
            jax.ShapeDtypeStruct((8, LANES), F32),
        ],
        compiler_params=pltpu.CompilerParams(
            dimension_semantics=("arbitrary", "arbitrary"), vmem_limit_bytes=24 * 2**20
        ),
        cost_estimate=pl.CostEstimate(
            flops=8 * 10**9, bytes_accessed=12 * 2**20, transcendentals=SUF * inner
        ),
        name="local_scan",
    )(meta, x, bc, bc, dt, rate, skip, wx, wbc, wbc, sx, sbc, sbc, pick)


def project_kernel(
    y_ref, gate_ref, cmap_ref, reach_ref, start_ref, gain_ref, pick_ref, w_ref, out_ref, sq_ref, held
):
    @pl.when(pl.program_id(0) == 0)
    def _():
        inner = y_ref.shape[1]
        squares = jnp.zeros((SPAN, LANES), F32)
        for i in range(inner // WIDE):
            at = pl.ds(i * WIDE, WIDE)
            carried = dot_t(cmap_ref[...], start_ref[at, :])
            y = y_ref[:, at] + dot(reach_ref[...], pick_ref[:, at]) * carried
            gated = y * silu(gate_ref[:, at].astype(F32))
            held[:, at] = (gated * gain_ref[:, at]).astype(BF16)
            gated = gated * gated
            for j in range(WIDE // LANES):
                squares += gated[:, j * LANES : (j + 1) * LANES]
        sq_ref[...] = lax.dot_general(
            jnp.ones((8, LANES), F32),
            squares,
            (((1,), (1,)), ((), ())),
            precision=HIGH,
            preferred_element_type=F32,
        )

    out_ref[0] = dot(held[...], w_ref[...]).astype(BF16)


def run_project(piece, y, gate, cmap, reach, start, gain, pick, weight, shares):
    inner, width = weight.shape
    share = width // shares
    rows = lambda n: (piece, 0)
    whole = lambda n: (0, 0)
    return pl.pallas_call(
        project_kernel,
        grid=(shares,),
        in_specs=[
            pl.BlockSpec((SPAN, inner), rows),
            pl.BlockSpec((SPAN, inner), rows),
            pl.BlockSpec((SPAN, LANES), rows),
            pl.BlockSpec((SPAN, LANES), rows),
            pl.BlockSpec((inner, STATE), whole),
            pl.BlockSpec((1, inner), whole),
            pl.BlockSpec((LANES, inner), whole),
            pl.BlockSpec((inner, share), lambda n: (0, n)),
        ],
        out_specs=[
            pl.BlockSpec((1, SPAN, share), lambda n: (n, 0, 0)),
            pl.BlockSpec((8, LANES), whole),
        ],
        out_shape=[
            jax.ShapeDtypeStruct((shares, SPAN, share), BF16),
            jax.ShapeDtypeStruct((8, LANES), F32),
        ],
        scratch_shapes=[pltpu.VMEM((SPAN, inner), BF16)],
        compiler_params=pltpu.CompilerParams(
            dimension_semantics=("arbitrary",), vmem_limit_bytes=32 * 2**20
        ),
        cost_estimate=pl.CostEstimate(
            flops=2 * SPAN * inner * width,
            bytes_accessed=2 * inner * width + 3 * 2**20,
            transcendentals=SPAN * inner,
        ),
        name="project",
    )(y, gate, cmap, reach, start, gain, pick, weight)


def shifted(x, axis, size, by):
    return lax.ppermute(x, axis, [(i, (i + by) % size) for i in range(size)])


def swap_core(x, size):
    return lax.ppermute(x, "req", [(i, i ^ 1) for i in range(size)])


def per_device(
    ssm_input,
    gate_input,
    bc_input,
    dt_input,
    decay_rate,
    skip_gain,
    norm_gain,
    conv_x_weight,
    conv_bc_weight,
    out_weight,
    pool_states,
    pool_conv_x,
    pool_conv_bc,
    prefix_slot,
    prefix_spans,
    dest_slot,
    suffix_len,
):
    num_req = lax.axis_size("req")
    num_tp = lax.axis_size("tp")
    me = lax.axis_index("req")
    z = lax.axis_index("tp")
    mate = me ^ 1
    heads = dt_input.shape[1]
    inner = ssm_input.shape[1]
    slots = pool_states.shape[0]
    copies = LANES // heads

    my_len = suffix_len[me]
    my_slot = prefix_slot[me]
    my_present = prefix_spans[me] > 0

    pool_conv = jnp.concatenate([pool_conv_x, pool_conv_bc], axis=2)

    def conv_for(request):
        return lax.dynamic_index_in_dim(
            pool_conv, jnp.clip(prefix_slot[request] - slots * me, 0, slots - 1), 0, False
        )

    start_conv = conv_for(me)
    for by in range(1, num_req):
        got = shifted(conv_for((me + by) % num_req), "req", num_req, by)
        start_conv = jnp.where(my_slot // slots == (me - by) % num_req, got, start_conv)
    start_conv = jnp.where(my_present, start_conv, jnp.zeros_like(start_conv))

    pool_flat = pool_states.astype(BF16).reshape(slots, inner, STATE)
    pool_mate = swap_core(pool_flat, num_req)

    def state_for(request):
        slot = prefix_slot[request]
        mine = lax.dynamic_index_in_dim(
            pool_flat, jnp.clip(slot - slots * me, 0, slots - 1), 0, False
        )
        other = lax.dynamic_index_in_dim(
            pool_mate, jnp.clip(slot - slots * mate, 0, slots - 1), 0, False
        )
        return jnp.where(slot // slots == me, mine, other)

    start = state_for(me)
    for by in range(2, num_req, 2):
        got = shifted(state_for((me + by) % num_req), "req", num_req, by)
        start = jnp.where(my_slot // (2 * slots) == ((me - by) % num_req) // 2, got, start)
    start = jnp.where(my_present, start, jnp.zeros_like(start))

    before = jnp.pad(start_conv.astype(F32), ((8 - (CONV - 1), 0), (0, 0)))
    lane_head = jnp.arange(LANES)[:, None]
    pick = (
        (lane_head % heads == (jnp.arange(inner) // HDIM)[None, :]) & (lane_head < 2 * heads)
    ).astype(BF16)
    meta = jnp.stack([(z * heads) // GHEADS, my_len]).astype(jnp.int32)
    y_local, local_final, cmap, reach, total = run_scan(
        meta,
        ssm_input,
        bc_input,
        jnp.tile(dt_input, (1, copies)),
        jnp.tile(decay_rate, copies)[None, :],
        jnp.repeat(skip_gain, HDIM)[None, :],
        conv_x_weight,
        conv_bc_weight,
        before[:, :inner],
        before[:, inner:],
        pick,
        heads,
    )

    gain = norm_gain[None, :]
    to_right = [(i, i + 1) for i in range(num_tp - 1)]
    to_left = [(i + 1, i) for i in range(num_tp - 1)]
    squares, summed = [], []
    for piece in range(NCH):
        part, square = run_project(
            piece, y_local, gate_input, cmap, reach, start, gain, pick, out_weight, num_tp
        )
        squares.append(square[0])

        def share(at):
            return lax.dynamic_index_in_dim(part, jnp.clip(at, 0, num_tp - 1), 0, False)

        right = left = None
        for s in range(num_tp - 1):
            go_right = share(num_tp - 1 - s + z)
            go_left = share(s - (num_tp - 1) + z)
            if s:
                go_right = (go_right.astype(F32) + right.astype(F32)).astype(BF16)
                go_left = (go_left.astype(F32) + left.astype(F32)).astype(BF16)
            right = lax.ppermute(go_right, "tp", to_right[: s + 1])
            left = lax.ppermute(go_left, "tp", to_left[num_tp - 2 - s :])
        summed.append(share(z).astype(F32) + right.astype(F32) + left.astype(F32))

    square = jnp.concatenate(squares)
    square_total = square
    for by in range(1, num_tp):
        square_total = square_total + shifted(square, "tp", num_tp, by)
    scale = lax.rsqrt(square_total / INNER + 1e-05)
    scale = jnp.where(jnp.arange(SUF) < my_len, scale, 0.0)
    mixed = (jnp.concatenate(summed, axis=0) * scale[:, None]).astype(BF16)

    decay = jnp.repeat(total[0, :heads], HDIM)[:, None]
    final = (local_final + decay * start.astype(F32)).astype(BF16)
    source = jnp.argmax(dest_slot[None, :] == jnp.arange(num_req)[:, None], axis=1)
    for_me = for_mate = final
    for by in range(2, num_req, 2):
        got = shifted(final, "req", num_req, by)
        origin = (me - by) % num_req
        for_me = jnp.where(source[me] == origin, got, for_me)
        for_mate = jnp.where(source[mate] == origin, got, for_mate)
    crossed = swap_core(for_mate, num_req)
    ckpt = jnp.where(source[me] % 2 == me % 2, for_me, crossed)
    ckpt_states = ckpt.astype(F32).reshape((1, heads, HDIM, STATE))

    extended_x = jnp.concatenate([start_conv[:, :inner], ssm_input], axis=0)
    extended_bc = jnp.concatenate([start_conv[:, inner:], bc_input], axis=0)
    tail = jnp.concatenate(
        [
            lax.dynamic_slice_in_dim(extended_x, my_len, CONV - 1, 0),
            lax.dynamic_slice_in_dim(extended_bc, my_len, CONV - 1, 0),
        ],
        axis=1,
    )
    landed = tail
    for by in range(1, num_req):
        got = shifted(tail, "req", num_req, by)
        landed = jnp.where(source[me] == (me - by) % num_req, got, landed)
    return (mixed, ckpt_states, landed[None, :, :inner], landed[None, :, inner:])


def solution(mesh):
    return jax.shard_map(
        per_device,
        mesh=mesh,
        in_specs=(
            P(("groups", "req"), "tp"),
            P(("groups", "req"), "tp"),
            P(("groups", "req"), None),
            P(("groups", "req"), "tp"),
            P("tp"),
            P("tp"),
            P("tp"),
            P(None, "tp"),
            P(),
            P("tp", None),
            P(("groups", "req"), "tp", None, None),
            P(("groups", "req"), None, "tp"),
            P(("groups", "req"), None, None),
            P("groups"),
            P("groups"),
            P("groups"),
            P("groups"),
        ),
        out_specs=(
            P(("groups", "req"), "tp"),
            P(("groups", "req"), "tp", None, None),
            P(("groups", "req"), None, "tp"),
            P(("groups", "req"), None, None),
        ),
        check_vma=False,
    )
```

time: 293 us -> 200 us (0.68); the launches traced: 287 us -> 199 us
  matrix products: 105 us -> 0 us
  starting transfers between devices: 10.2 us -> 78.3 us
  Pallas kernels: 0 us -> 45.9 us
  local copies, waits for them, and re-layouts: 40.5 us -> 9.91 us
  blocking collectives: 24.2 us -> 0 us
  other arithmetic: 35.5 us -> 13.4 us
  waiting for transfers between devices: 54.9 us -> 34.1 us
    dot_general x10 -> x0, matrix products: 105 us -> none  [the longest x1 25.8 us: ssd_spans(): jnp.einsum('cthn,cshn->chts', output_map, input_map, precision=HIGH)]
    ppermute x0 -> x37, starting transfers between devices: none -> 78.3 us  [the longest x12 55.4 us: per_device(): right = lax.ppermute(go_right, 'tp', to_right[:s + 1])]
    pallas_call x0 -> x5, Pallas kernels: none -> 45.9 us  [the longest x4 32.6 us: run_project(): pl.pallas_call(project_kernel, grid=(shares,), in_specs=[pl.BlockSpec((SP...]
    ppermute x0 -> x37, waiting for transfers between devices: none -> 34.1 us  [the longest x11 12.7 us: shifted(): return lax.ppermute(x, axis, [(i, (i + by) % size) for i in range(size)])]
    all_to_all x3 -> x0, waiting for transfers between devices: 28.7 us -> none  [the longest x1 24.4 us: per_device(): lax.all_to_all(as_sent(out_states), 'req', split_axis=0, concat_axis=0, t...]
    reduce_scatter x1 -> x0, waiting for transfers between devices: 26.1 us -> none  [per_device(): lax.psum_scatter(lax.dot_general(out_weight, normed, (((0,), (1,)), ((),...]
    psum x1 -> x0, blocking collectives: 12.1 us -> none  [per_device(): square_total = lax.psum(jnp.sum(gated * gated, axis=1), 'tp')]
    all_gather x2 -> x0, blocking collectives: 12.1 us -> none  [the longest x1 6.51 us: per_device(): lax.all_gather(pool_x_f.astype(jnp.bfloat16), 'req', axis=0, tiled=True)]
  transfers between devices with their start and end apart: 5 -> 37, of which waited for: 4 -> 12; matrix products, arithmetic and copies ran while one was open for 39% -> 7% of each run, Pallas kernels for 0% -> 7%
where the time goes in v1:
time: 200 us; the launch traced here: 199 us
  starting transfers between devices  78.3 us (39%)
  Pallas kernels  45.9 us (23%)
  waiting for transfers between devices  34.1 us (17%)
  between operations  17.4 us (9%)
  other arithmetic  13.4 us (7%)
  local copies, waits for them, and re-layouts  9.91 us (5%)
    ppermute x12, starting transfers between devices, per_device(): right = lax.ppermute(go_right, 'tp', to_right[:s + 1])  55.4 us
    pallas_call x4, Pallas kernels, run_project(): pl.pallas_call(project_kernel, grid=(shares,), in_specs=[pl.BlockSpec((SP...  32.6 us
    pallas_call x1, Pallas kernels, run_scan(): pl.pallas_call(functools.partial(scan_kernel, heads), grid_spec=pltpu.Pre...  13.3 us
    ppermute x11, waiting for transfers between devices, shifted(): return lax.ppermute(x, axis, [(i, (i + by) % size) for i in range(size)])  12.7 us
    ppermute x11, starting transfers between devices, shifted(): return lax.ppermute(x, axis, [(i, (i + by) % size) for i in range(size)])  10.9 us
    ppermute x12, waiting for transfers between devices, per_device(): left = lax.ppermute(go_left, 'tp', to_left[num_tp - 2 - s:])  10.8 us
    ppermute x12, waiting for transfers between devices, per_device(): right = lax.ppermute(go_right, 'tp', to_right[:s + 1])  10.6 us
    ppermute x12, starting transfers between devices, per_device(): left = lax.ppermute(go_left, 'tp', to_left[num_tp - 2 - s:])  10.6 us
  transfers between devices with their start and end apart: 37, of which 12 were waited for; matrix products, arithmetic and copies ran while one was open for 7% of the time, Pallas kernels for 7%

profile of v1, /device:TPU:0, one launch (start us, length us, event | category | flops | bytes accessed | tf_op | source)
XLA Modules:
  0.0 199.0 jit_solution(17403069729763728517)
XLA Ops:
  1.5 1.4 fusion.32
  6.3 2.5 %collective-permute-start = (bf16[3,3072]{1,0:T(4,128)(2,1)S(1)}, bf16[3,3072]{1,0:T(4,128)(2,1)S(1)}, u32[]{:S(2)}, u32[]{:S(2)}) collective-permute-start(bf16[3,3072]{1,0:T(4,128)(2,1)S(1)} %bitcast.134), channel_id=1, source_target_pairs={{0,12},{4,0},{8,4},{12,8},{1,13},{5,1},{9,5},{13,9},{2,14},{6,2},{... | collective-permute-start | bytes 55304 | tf_op jit(solution)/shard_map/ppermute | solution.py:285
  9.8 2.8 %convert_element_type.268 = bf16[2,32,64,128]{3,2,1,0:T(8,128)(2,1)} convert(f32[2,32,64,128]{3,2,1,0:T(8,128)} %param.27) | non-fusion elementwise | flops 524288 | bytes 3145728 | tf_op jit(solution)/shard_map/convert_element_type | solution.py:338
  12.5 1.4 collective-permute-start.3
  32.4 1.5 collective-permute-start.35
  34.0 13.3 %local_scan.1 = (f32[512,2048]{1,0:T(8,128)S(1)}, f32[2048,128]{1,0:T(8,128)S(1)}, bf16[512,128]{1,0:T(8,128)(2,1)S(1)}, bf16[512,128]{1,0:T(8,128)(2,1)S(1)}, f32[8,128]{1,0:T(8,128)S(1)}) custom-call(s32[2]{0:T(128)S(1)} %pad_add_fusion.meta, bf16[512,2048]{1,0:T(8,128)(2,1)S(1)} %copy-done.4, bf16[512,1024]{1,0:T(8,128)(2,1)S(1)} %copy-done.7, ...), custom_call_target="tpu_custom_call" | custom-call | flops 8000000000 | bytes 12582912 | tf_op jit(solution)/shard_map/local_scan/pallas_call | solution.py:182
  47.4 2.0 copy-done
  50.6 1.4 select_bitcast_fusion
  53.9 12.7 %collective-permute-done.4 = bf16[2048,128]{1,0:T(8,128)(2,1)S(1)} collective-permute-done((bf16[2048,128]{1,0:T(8,128)(2,1)S(1)}, bf16[2048,128]{1,0:T(8,128)(2,1)S(1)}, u32[]{:S(2)}, u32[]{:S(2)}) %collective-permute-start.4) | collective-permute-done | bytes 524320 | tf_op jit(solution)/shard_map/ppermute | solution.py:285
  66.5 1.6 add_convert_fusion
  68.1 8.1 %project.7 = (bf16[4,128,1024]{2,1,0:T(8,128)(2,1)S(1)}, f32[8,128]{1,0:T(8,128)S(1)}) custom-call(f32[512,2048]{1,0:T(8,128)S(1)} %copy-done.1, bf16[512,2048]{1,0:T(8,128)(2,1)S(1)} %copy-done.2, bf16[512,128]{1,0:T(8,128)(2,1)S(1)} %get-tuple-element.19.cmap_ref, bf16[512,128]{1,0:T(8,128)(2,1)S(1)} %get-tuple-element.20.reach_ref, ...), custom_call_target="tpu_custom_call" | custom-call | flops 2147483648 | bytes 19922944 | tf_op jit(solution)/shard_map/project/pallas_call | solution.py:250
  76.3 8.1 %project.6 = (bf16[4,128,1024]{2,1,0:T(8,128)(2,1)S(1)}, f32[8,128]{1,0:T(8,128)S(1)}) custom-call(f32[512,2048]{1,0:T(8,128)S(1)} %copy-done.1, bf16[512,2048]{1,0:T(8,128)(2,1)S(1)} %copy-done.2, bf16[512,128]{1,0:T(8,128)(2,1)S(1)} %get-tuple-element.19.cmap_ref, bf16[512,128]{1,0:T(8,128)(2,1)S(1)} %get-tuple-element.20.reach_ref, ...), custom_call_target="tpu_custom_call" | custom-call | flops 2147483648 | bytes 19922944 | tf_op jit(solution)/shard_map/project/pallas_call | solution.py:250
  84.4 8.1 %project.5 = (bf16[4,128,1024]{2,1,0:T(8,128)(2,1)S(1)}, f32[8,128]{1,0:T(8,128)S(1)}) custom-call(f32[512,2048]{1,0:T(8,128)S(1)} %copy-done.1, bf16[512,2048]{1,0:T(8,128)(2,1)S(1)} %copy-done.2, bf16[512,128]{1,0:T(8,128)(2,1)S(1)} %get-tuple-element.19.cmap_ref, bf16[512,128]{1,0:T(8,128)(2,1)S(1)} %get-tuple-element.20.reach_ref, ...), custom_call_target="tpu_custom_call" | custom-call | flops 2147483648 | bytes 19922944 | tf_op jit(solution)/shard_map/project/pallas_call | solution.py:250
  92.6 8.1 %project.4 = (bf16[4,128,1024]{2,1,0:T(8,128)(2,1)S(1)}, f32[8,128]{1,0:T(8,128)S(1)}) custom-call(f32[512,2048]{1,0:T(8,128)S(1)} %copy-done.1, bf16[512,2048]{1,0:T(8,128)(2,1)S(1)} %copy-done.2, bf16[512,128]{1,0:T(8,128)(2,1)S(1)} %get-tuple-element.19.cmap_ref, bf16[512,128]{1,0:T(8,128)(2,1)S(1)} %get-tuple-element.20.reach_ref, ...), custom_call_target="tpu_custom_call" | custom-call | flops 2147483648 | bytes 19922944 | tf_op jit(solution)/shard_map/project/pallas_call | solution.py:250
  100.8 3.6 %collective-permute-start.31 = (f32[512]{0:T(512)S(1)}, f32[512]{0:T(512)S(1)}, u32[]{:S(2)}, u32[]{:S(2)}) collective-permute-start(f32[512]{0:T(512)S(1)} %pad_maximum_fusion.1), channel_id=1, source_target_pairs={{0,3},{1,0},{2,1},{3,2},{4,7},{5,4},{6,5},{7,6},{8,11},{9,8},{10,9... | collective-permute-start | bytes 6152 | tf_op jit(solution)/shard_map/ppermute | solution.py:285
  105.5 4.4 %collective-permute-start.23 = (bf16[128,1024]{1,0:T(8,128)(2,1)S(1)}, bf16[128,1024]{1,0:T(8,128)(2,1)S(1)}, u32[]{:S(2)}, u32[]{:S(2)}) collective-permute-start(bf16[128,1024]{1,0:T(8,128)(2,1)S(1)} %get-tuple-element.48), channel_id=1, source_target_pairs={{0,1},{4,5},{8,9},{12,13},{16,17},{20,21},{24,25},{28,29}} | collective-permute-start | bytes 786440 | tf_op jit(solution)/shard_map/ppermute | solution.py:398
  110.8 1.3 collective-permute-start.17
  112.8 1.3 collective-permute-start.11
  114.7 1.9 collective-permute-done.23
  117.4 4.9 %collective-permute-done.17 = bf16[128,1024]{1,0:T(8,128)(2,1)S(1)} collective-permute-done((bf16[128,1024]{1,0:T(8,128)(2,1)S(1)}, bf16[128,1024]{1,0:T(8,128)(2,1)S(1)}, u32[]{:S(2)}, u32[]{:S(2)}) %collective-permute-start.17) | collective-permute-done | bytes 262176 | tf_op jit(solution)/shard_map/ppermute | solution.py:398
  122.2 4.4 %collective-permute-start.5 = (bf16[128,1024]{1,0:T(8,128)(2,1)S(1)}, bf16[128,1024]{1,0:T(8,128)(2,1)S(1)}, u32[]{:S(2)}, u32[]{:S(2)}) collective-permute-start(bf16[128,1024]{1,0:T(8,128)(2,1)S(1)} %get-tuple-element.36), channel_id=1, source_target_pairs={{0,1},{4,5},{8,9},{12,13},{16,17},{20,21},{24,25},{28,29}} | collective-permute-start | bytes 786440 | tf_op jit(solution)/shard_map/ppermute | solution.py:398
  127.9 4.4 %collective-permute-start.24 = (bf16[128,1024]{1,0:T(8,128)(2,1)S(1)}, bf16[128,1024]{1,0:T(8,128)(2,1)S(1)}, u32[]{:S(2)}, u32[]{:S(2)}) collective-permute-start(bf16[128,1024]{1,0:T(8,128)(2,1)S(1)} %fusion.3), channel_id=1, source_target_pairs={{0,1},{1,2},{4,5},{5,6},{8,9},{9,10},{12,13},{13,14},{16,17},{17,1... | collective-permute-start | bytes 786440 | tf_op jit(solution)/shard_map/ppermute | solution.py:398
  133.5 4.4 %collective-permute-start.18 = (bf16[128,1024]{1,0:T(8,128)(2,1)S(1)}, bf16[128,1024]{1,0:T(8,128)(2,1)S(1)}, u32[]{:S(2)}, u32[]{:S(2)}) collective-permute-start(bf16[128,1024]{1,0:T(8,128)(2,1)S(1)} %fusion.8), channel_id=1, source_target_pairs={{0,1},{1,2},{4,5},{5,6},{8,9},{9,10},{12,13},{13,14},{16,17},{17,1... | collective-permute-start | bytes 786440 | tf_op jit(solution)/shard_map/ppermute | solution.py:398
  139.1 4.4 %collective-permute-start.12 = (bf16[128,1024]{1,0:T(8,128)(2,1)S(1)}, bf16[128,1024]{1,0:T(8,128)(2,1)S(1)}, u32[]{:S(2)}, u32[]{:S(2)}) collective-permute-start(bf16[128,1024]{1,0:T(8,128)(2,1)S(1)} %fusion.13), channel_id=1, source_target_pairs={{0,1},{1,2},{4,5},{5,6},{8,9},{9,10},{12,13},{13,14},{16,17},{17,1... | collective-permute-start | bytes 786440 | tf_op jit(solution)/shard_map/ppermute | solution.py:398
  144.7 4.4 %collective-permute-start.6 = (bf16[128,1024]{1,0:T(8,128)(2,1)S(1)}, bf16[128,1024]{1,0:T(8,128)(2,1)S(1)}, u32[]{:S(2)}, u32[]{:S(2)}) collective-permute-start(bf16[128,1024]{1,0:T(8,128)(2,1)S(1)} %fusion.18), channel_id=1, source_target_pairs={{0,1},{1,2},{4,5},{5,6},{8,9},{9,10},{12,13},{13,14},{16,17},{17,1... | collective-permute-start | bytes 786440 | tf_op jit(solution)/shard_map/ppermute | solution.py:398
  150.3 4.4 %collective-permute-start.25 = (bf16[128,1024]{1,0:T(8,128)(2,1)S(1)}, bf16[128,1024]{1,0:T(8,128)(2,1)S(1)}, u32[]{:S(2)}, u32[]{:S(2)}) collective-permute-start(bf16[128,1024]{1,0:T(8,128)(2,1)S(1)} %get-tuple-element.46), channel_id=1, source_target_pairs={{0,1},{1,2},{2,3},{4,5},{5,6},{6,7},{8,9},{9,10},{10,11},{12,13},{... | collective-permute-start | bytes 786440 | tf_op jit(solution)/shard_map/ppermute | solution.py:398
  156.0 4.4 %collective-permute-start.19 = (bf16[128,1024]{1,0:T(8,128)(2,1)S(1)}, bf16[128,1024]{1,0:T(8,128)(2,1)S(1)}, u32[]{:S(2)}, u32[]{:S(2)}) collective-permute-start(bf16[128,1024]{1,0:T(8,128)(2,1)S(1)} %get-tuple-element.42), channel_id=1, source_target_pairs={{0,1},{1,2},{2,3},{4,5},{5,6},{6,7},{8,9},{9,10},{10,11},{12,13},{... | collective-permute-start | bytes 786440 | tf_op jit(solution)/shard_map/ppermute | solution.py:398
  161.3 3.5 %collective-permute-start.13 = (bf16[128,1024]{1,0:T(8,128)(2,1)S(1)}, bf16[128,1024]{1,0:T(8,128)(2,1)S(1)}, u32[]{:S(2)}, u32[]{:S(2)}) collective-permute-start(bf16[128,1024]{1,0:T(8,128)(2,1)S(1)} %get-tuple-element.38), channel_id=1, source_target_pairs={{0,1},{1,2},{2,3},{4,5},{5,6},{6,7},{8,9},{9,10},{10,11},{12,13},{... | collective-permute-start | bytes 786440 | tf_op jit(solution)/shard_map/ppermute | solution.py:398
  168.5 14.1 %collective-permute-start.7 = (bf16[128,1024]{1,0:T(8,128)(2,1)S(1)}, bf16[128,1024]{1,0:T(8,128)(2,1)S(1)}, u32[]{:S(2)}, u32[]{:S(2)}) collective-permute-start(bf16[128,1024]{1,0:T(8,128)(2,1)S(1)} %get-tuple-element.34), channel_id=1, source_target_pairs={{0,1},{1,2},{2,3},{4,5},{5,6},{6,7},{8,9},{9,10},{10,11},{12,13},{... | collective-permute-start | bytes 786440 | tf_op jit(solution)/shard_map/ppermute | solution.py:398
  184.2 1.5 collective-permute-done.22
  187.1 4.6 %collective-permute-done.16 = bf16[128,1024]{1,0:T(8,128)(2,1)S(1)} collective-permute-done((bf16[128,1024]{1,0:T(8,128)(2,1)S(1)}, bf16[128,1024]{1,0:T(8,128)(2,1)S(1)}, u32[]{:S(2)}, u32[]{:S(2)}) %collective-permute-start.16) | collective-permute-done | bytes 262176 | tf_op jit(solution)/shard_map/ppermute | solution.py:399
  191.8 4.7 %collective-permute-done.10 = bf16[128,1024]{1,0:T(8,128)(2,1)S(1)} collective-permute-done((bf16[128,1024]{1,0:T(8,128)(2,1)S(1)}, bf16[128,1024]{1,0:T(8,128)(2,1)S(1)}, u32[]{:S(2)}, u32[]{:S(2)}) %collective-permute-start.10) | collective-permute-done | bytes 262176 | tf_op jit(solution)/shard_map/ppermute | solution.py:399
  (151 shorter events, 31.9 us)
Async XLA Ops:
  6.3 24.7 %collective-permute-start = (bf16[3,3072]{1,0:T(4,128)(2,1)S(1)}, bf16[3,3072]{1,0:T(4,128)(2,1)S(1)}, u32[]{:S(2)}, u32[]{:S(2)}) collective-permute-start(bf16[3,3072]{1,0:T(4,128)(2,1)S(1)} %bitcast.134), channel_id=1, source_target_pairs={{0,12},{4,0},{8,4},{12,8},{1,13},{5,1},{9,5},{13,9},{2,14},{6,2},{... | collective-permute-start | bytes 55304 | tf_op jit(solution)/shard_map/ppermute | solution.py:285
  8.8 22.3 %collective-permute-start.1 = (bf16[3,3072]{1,0:T(4,128)(2,1)S(1)}, bf16[3,3072]{1,0:T(4,128)(2,1)S(1)}, u32[]{:S(2)}, u32[]{:S(2)}) collective-permute-start(bf16[3,3072]{1,0:T(4,128)(2,1)S(1)} %bitcast.135), channel_id=1, source_target_pairs={{0,8},{4,12},{8,0},{12,4},{1,9},{5,13},{9,1},{13,5},{2,10},{6,14},... | collective-permute-start | bytes 55304 | tf_op jit(solution)/shard_map/ppermute | solution.py:285
  9.5 21.6 %collective-permute-start.2 = (bf16[3,3072]{1,0:T(4,128)(2,1)S(1)}, bf16[3,3072]{1,0:T(4,128)(2,1)S(1)}, u32[]{:S(2)}, u32[]{:S(2)}) collective-permute-start(bf16[3,3072]{1,0:T(4,128)(2,1)S(1)} %bitcast.136), channel_id=1, source_target_pairs={{0,4},{4,8},{8,12},{12,0},{1,5},{5,9},{9,13},{13,1},{2,6},{6,10},{... | collective-permute-start | bytes 55304 | tf_op jit(solution)/shard_map/ppermute | solution.py:285
  12.5 38.0 %collective-permute-start.3 = (bf16[2,2048,128]{2,1,0:T(8,128)(2,1)}, bf16[2,2048,128]{2,1,0:T(8,128)(2,1)}, u32[]{:S(2)}, u32[]{:S(2)}) collective-permute-start(bf16[2,2048,128]{2,1,0:T(8,128)(2,1)} %bitcast.7), channel_id=1, source_target_pairs={{0,4},{4,0},{8,12},{12,8},{1,5},{5,1},{9,13},{13,9},{2,6},{6,2},{1... | collective-permute-start | bytes 3145736 | tf_op jit(solution)/shard_map/ppermute | solution.py:289
  32.3 18.2 %collective-permute-start.34 = (bf16[3,3072]{1,0:T(4,128)(2,1)S(1)}, bf16[3,3072]{1,0:T(4,128)(2,1)S(1)}, u32[]{:S(2)}, u32[]{:S(2)}) collective-permute-start(bf16[3,3072]{1,0:T(4,128)(2,1)S(1)} %pad_maximum_fusion), channel_id=1, source_target_pairs={{0,12},{4,0},{8,4},{12,8},{1,13},{5,1},{9,5},{13,9},{2,14},{6,2},{... | collective-permute-start | bytes 55304 | tf_op jit(solution)/shard_map/ppermute | solution.py:285
  32.4 18.1 %collective-permute-start.35 = (bf16[3,3072]{1,0:T(4,128)(2,1)S(1)}, bf16[3,3072]{1,0:T(4,128)(2,1)S(1)}, u32[]{:S(2)}, u32[]{:S(2)}) collective-permute-start(bf16[3,3072]{1,0:T(4,128)(2,1)S(1)} %pad_maximum_fusion), channel_id=1, source_target_pairs={{0,8},{4,12},{8,0},{12,4},{1,9},{5,13},{9,1},{13,5},{2,10},{6,14},... | collective-permute-start | bytes 55304 | tf_op jit(solution)/shard_map/ppermute | solution.py:285
  34.0 16.5 %collective-permute-start.36 = (bf16[3,3072]{1,0:T(4,128)(2,1)S(1)}, bf16[3,3072]{1,0:T(4,128)(2,1)S(1)}, u32[]{:S(2)}, u32[]{:S(2)}) collective-permute-start(bf16[3,3072]{1,0:T(4,128)(2,1)S(1)} %pad_maximum_fusion), channel_id=1, source_target_pairs={{0,4},{4,8},{8,12},{12,0},{1,5},{5,9},{9,13},{13,1},{2,6},{6,10},{... | collective-permute-start | bytes 55304 | tf_op jit(solution)/shard_map/ppermute | solution.py:285
  52.0 14.5 %collective-permute-start.4 = (bf16[2048,128]{1,0:T(8,128)(2,1)S(1)}, bf16[2048,128]{1,0:T(8,128)(2,1)S(1)}, u32[]{:S(2)}, u32[]{:S(2)}) collective-permute-start(bf16[2048,128]{1,0:T(8,128)(2,1)S(1)} %select_bitcast_fusion), channel_id=1, source_target_pairs={{0,8},{4,12},{8,0},{12,4},{1,9},{5,13},{9,1},{13,5},{2,10},{6,14},... | collective-permute-start | bytes 1572872 | tf_op jit(solution)/shard_map/ppermute | solution.py:285
  100.8 9.9 %collective-permute-start.31 = (f32[512]{0:T(512)S(1)}, f32[512]{0:T(512)S(1)}, u32[]{:S(2)}, u32[]{:S(2)}) collective-permute-start(f32[512]{0:T(512)S(1)} %pad_maximum_fusion.1), channel_id=1, source_target_pairs={{0,3},{1,0},{2,1},{3,2},{4,7},{5,4},{6,5},{7,6},{8,11},{9,8},{10,9... | collective-permute-start | bytes 6152 | tf_op jit(solution)/shard_map/ppermute | solution.py:285
  105.5 11.1 %collective-permute-start.23 = (bf16[128,1024]{1,0:T(8,128)(2,1)S(1)}, bf16[128,1024]{1,0:T(8,128)(2,1)S(1)}, u32[]{:S(2)}, u32[]{:S(2)}) collective-permute-start(bf16[128,1024]{1,0:T(8,128)(2,1)S(1)} %get-tuple-element.48), channel_id=1, source_target_pairs={{0,1},{4,5},{8,9},{12,13},{16,17},{20,21},{24,25},{28,29}} | collective-permute-start | bytes 786440 | tf_op jit(solution)/shard_map/ppermute | solution.py:398
  109.9 28.1 %collective-permute-start.26 = (bf16[128,1024]{1,0:T(8,128)(2,1)S(1)}, bf16[128,1024]{1,0:T(8,128)(2,1)S(1)}, u32[]{:S(2)}, u32[]{:S(2)}) collective-permute-start(bf16[128,1024]{1,0:T(8,128)(2,1)S(1)} %get-tuple-element.49), channel_id=1, source_target_pairs={{3,2},{7,6},{11,10},{15,14},{19,18},{23,22},{27,26},{31,30}} | collective-permute-start | bytes 786440 | tf_op jit(solution)/shard_map/ppermute | solution.py:399
  110.8 11.5 %collective-permute-start.17 = (bf16[128,1024]{1,0:T(8,128)(2,1)S(1)}, bf16[128,1024]{1,0:T(8,128)(2,1)S(1)}, u32[]{:S(2)}, u32[]{:S(2)}) collective-permute-start(bf16[128,1024]{1,0:T(8,128)(2,1)S(1)} %get-tuple-element.44), channel_id=1, source_target_pairs={{0,1},{4,5},{8,9},{12,13},{16,17},{20,21},{24,25},{28,29}} | collective-permute-start | bytes 786440 | tf_op jit(solution)/shard_map/ppermute | solution.py:398
  112.1 31.6 %collective-permute-start.20 = (bf16[128,1024]{1,0:T(8,128)(2,1)S(1)}, bf16[128,1024]{1,0:T(8,128)(2,1)S(1)}, u32[]{:S(2)}, u32[]{:S(2)}) collective-permute-start(bf16[128,1024]{1,0:T(8,128)(2,1)S(1)} %get-tuple-element.45), channel_id=1, source_target_pairs={{3,2},{7,6},{11,10},{15,14},{19,18},{23,22},{27,26},{31,30}} | collective-permute-start | bytes 786440 | tf_op jit(solution)/shard_map/ppermute | solution.py:399
  112.8 15.1 %collective-permute-start.11 = (bf16[128,1024]{1,0:T(8,128)(2,1)S(1)}, bf16[128,1024]{1,0:T(8,128)(2,1)S(1)}, u32[]{:S(2)}, u32[]{:S(2)}) collective-permute-start(bf16[128,1024]{1,0:T(8,128)(2,1)S(1)} %get-tuple-element.40), channel_id=1, source_target_pairs={{0,1},{4,5},{8,9},{12,13},{16,17},{20,21},{24,25},{28,29}} | collective-permute-start | bytes 786440 | tf_op jit(solution)/shard_map/ppermute | solution.py:398
  116.6 32.7 %collective-permute-start.14 = (bf16[128,1024]{1,0:T(8,128)(2,1)S(1)}, bf16[128,1024]{1,0:T(8,128)(2,1)S(1)}, u32[]{:S(2)}, u32[]{:S(2)}) collective-permute-start(bf16[128,1024]{1,0:T(8,128)(2,1)S(1)} %get-tuple-element.41), channel_id=1, source_target_pairs={{3,2},{7,6},{11,10},{15,14},{19,18},{23,22},{27,26},{31,30}} | collective-permute-start | bytes 786440 | tf_op jit(solution)/shard_map/ppermute | solution.py:399
  122.2 11.2 %collective-permute-start.5 = (bf16[128,1024]{1,0:T(8,128)(2,1)S(1)}, bf16[128,1024]{1,0:T(8,128)(2,1)S(1)}, u32[]{:S(2)}, u32[]{:S(2)}) collective-permute-start(bf16[128,1024]{1,0:T(8,128)(2,1)S(1)} %get-tuple-element.36), channel_id=1, source_target_pairs={{0,1},{4,5},{8,9},{12,13},{16,17},{20,21},{24,25},{28,29}} | collective-permute-start | bytes 786440 | tf_op jit(solution)/shard_map/ppermute | solution.py:398
  127.9 11.2 %collective-permute-start.24 = (bf16[128,1024]{1,0:T(8,128)(2,1)S(1)}, bf16[128,1024]{1,0:T(8,128)(2,1)S(1)}, u32[]{:S(2)}, u32[]{:S(2)}) collective-permute-start(bf16[128,1024]{1,0:T(8,128)(2,1)S(1)} %fusion.3), channel_id=1, source_target_pairs={{0,1},{1,2},{4,5},{5,6},{8,9},{9,10},{12,13},{13,14},{16,17},{17,1... | collective-permute-start | bytes 786440 | tf_op jit(solution)/shard_map/ppermute | solution.py:398
  133.5 11.2 %collective-permute-start.18 = (bf16[128,1024]{1,0:T(8,128)(2,1)S(1)}, bf16[128,1024]{1,0:T(8,128)(2,1)S(1)}, u32[]{:S(2)}, u32[]{:S(2)}) collective-permute-start(bf16[128,1024]{1,0:T(8,128)(2,1)S(1)} %fusion.8), channel_id=1, source_target_pairs={{0,1},{1,2},{4,5},{5,6},{8,9},{9,10},{12,13},{13,14},{16,17},{17,1... | collective-permute-start | bytes 786440 | tf_op jit(solution)/shard_map/ppermute | solution.py:398
  138.0 17.0 %collective-permute-start.8 = (bf16[128,1024]{1,0:T(8,128)(2,1)S(1)}, bf16[128,1024]{1,0:T(8,128)(2,1)S(1)}, u32[]{:S(2)}, u32[]{:S(2)}) collective-permute-start(bf16[128,1024]{1,0:T(8,128)(2,1)S(1)} %get-tuple-element.37), channel_id=1, source_target_pairs={{3,2},{7,6},{11,10},{15,14},{19,18},{23,22},{27,26},{31,30}} | collective-permute-start | bytes 786440 | tf_op jit(solution)/shard_map/ppermute | solution.py:399
  139.1 11.2 %collective-permute-start.12 = (bf16[128,1024]{1,0:T(8,128)(2,1)S(1)}, bf16[128,1024]{1,0:T(8,128)(2,1)S(1)}, u32[]{:S(2)}, u32[]{:S(2)}) collective-permute-start(bf16[128,1024]{1,0:T(8,128)(2,1)S(1)} %fusion.13), channel_id=1, source_target_pairs={{0,1},{1,2},{4,5},{5,6},{8,9},{9,10},{12,13},{13,14},{16,17},{17,1... | collective-permute-start | bytes 786440 | tf_op jit(solution)/shard_map/ppermute | solution.py:398
  143.7 16.8 %collective-permute-start.32 = (bf16[2048,128]{1,0:T(8,128)(2,1)S(1)}, bf16[2048,128]{1,0:T(8,128)(2,1)S(1)}, u32[]{:S(2)}, u32[]{:S(2)}) collective-permute-start(bf16[2048,128]{1,0:T(8,128)(2,1)S(1)} %get-tuple-element.32), channel_id=1, source_target_pairs={{0,8},{4,12},{8,0},{12,4},{1,9},{5,13},{9,1},{13,5},{2,10},{6,14},... | collective-permute-start | bytes 1572872 | tf_op jit(solution)/shard_map/ppermute | solution.py:285
  144.7 11.2 %collective-permute-start.6 = (bf16[128,1024]{1,0:T(8,128)(2,1)S(1)}, bf16[128,1024]{1,0:T(8,128)(2,1)S(1)}, u32[]{:S(2)}, u32[]{:S(2)}) collective-permute-start(bf16[128,1024]{1,0:T(8,128)(2,1)S(1)} %fusion.18), channel_id=1, source_target_pairs={{0,1},{1,2},{4,5},{5,6},{8,9},{9,10},{12,13},{13,14},{16,17},{17,1... | collective-permute-start | bytes 786440 | tf_op jit(solution)/shard_map/ppermute | solution.py:398
  149.3 12.0 %collective-permute-start.27 = (bf16[128,1024]{1,0:T(8,128)(2,1)S(1)}, bf16[128,1024]{1,0:T(8,128)(2,1)S(1)}, u32[]{:S(2)}, u32[]{:S(2)}) collective-permute-start(bf16[128,1024]{1,0:T(8,128)(2,1)S(1)} %get-tuple-element.47), channel_id=1, source_target_pairs={{2,1},{3,2},{6,5},{7,6},{10,9},{11,10},{14,13},{15,14},{18,17},{19... | collective-permute-start | bytes 786440 | tf_op jit(solution)/shard_map/ppermute | solution.py:399
  150.3 18.1 %collective-permute-start.25 = (bf16[128,1024]{1,0:T(8,128)(2,1)S(1)}, bf16[128,1024]{1,0:T(8,128)(2,1)S(1)}, u32[]{:S(2)}, u32[]{:S(2)}) collective-permute-start(bf16[128,1024]{1,0:T(8,128)(2,1)S(1)} %get-tuple-element.46), channel_id=1, source_target_pairs={{0,1},{1,2},{2,3},{4,5},{5,6},{6,7},{8,9},{9,10},{10,11},{12,13},{... | collective-permute-start | bytes 786440 | tf_op jit(solution)/shard_map/ppermute | solution.py:398
  155.0 10.0 %collective-permute-start.21 = (bf16[128,1024]{1,0:T(8,128)(2,1)S(1)}, bf16[128,1024]{1,0:T(8,128)(2,1)S(1)}, u32[]{:S(2)}, u32[]{:S(2)}) collective-permute-start(bf16[128,1024]{1,0:T(8,128)(2,1)S(1)} %get-tuple-element.43), channel_id=1, source_target_pairs={{2,1},{3,2},{6,5},{7,6},{10,9},{11,10},{14,13},{15,14},{18,17},{19... | collective-permute-start | bytes 786440 | tf_op jit(solution)/shard_map/ppermute | solution.py:399
  156.0 28.1 %collective-permute-start.19 = (bf16[128,1024]{1,0:T(8,128)(2,1)S(1)}, bf16[128,1024]{1,0:T(8,128)(2,1)S(1)}, u32[]{:S(2)}, u32[]{:S(2)}) collective-permute-start(bf16[128,1024]{1,0:T(8,128)(2,1)S(1)} %get-tuple-element.42), channel_id=1, source_target_pairs={{0,1},{1,2},{2,3},{4,5},{5,6},{6,7},{8,9},{9,10},{10,11},{12,13},{... | collective-permute-start | bytes 786440 | tf_op jit(solution)/shard_map/ppermute | solution.py:398
  161.3 25.7 %collective-permute-start.13 = (bf16[128,1024]{1,0:T(8,128)(2,1)S(1)}, bf16[128,1024]{1,0:T(8,128)(2,1)S(1)}, u32[]{:S(2)}, u32[]{:S(2)}) collective-permute-start(bf16[128,1024]{1,0:T(8,128)(2,1)S(1)} %get-tuple-element.38), channel_id=1, source_target_pairs={{0,1},{1,2},{2,3},{4,5},{5,6},{6,7},{8,9},{9,10},{10,11},{12,13},{... | collective-permute-start | bytes 786440 | tf_op jit(solution)/shard_map/ppermute | solution.py:398
  165.7 16.9 %collective-permute-start.28 = (bf16[128,1024]{1,0:T(8,128)(2,1)S(1)}, bf16[128,1024]{1,0:T(8,128)(2,1)S(1)}, u32[]{:S(2)}, u32[]{:S(2)}) collective-permute-start(bf16[128,1024]{1,0:T(8,128)(2,1)S(1)} %fusion.2), channel_id=1, source_target_pairs={{1,0},{2,1},{3,2},{5,4},{6,5},{7,6},{9,8},{10,9},{11,10},{13,12},{... | collective-permute-start | bytes 786440 | tf_op jit(solution)/shard_map/ppermute | solution.py:399
  167.1 18.6 %collective-permute-start.22 = (bf16[128,1024]{1,0:T(8,128)(2,1)S(1)}, bf16[128,1024]{1,0:T(8,128)(2,1)S(1)}, u32[]{:S(2)}, u32[]{:S(2)}) collective-permute-start(bf16[128,1024]{1,0:T(8,128)(2,1)S(1)} %fusion.7), channel_id=1, source_target_pairs={{1,0},{2,1},{3,2},{5,4},{6,5},{7,6},{9,8},{10,9},{11,10},{13,12},{... | collective-permute-start | bytes 786440 | tf_op jit(solution)/shard_map/ppermute | solution.py:399
  168.5 23.3 %collective-permute-start.7 = (bf16[128,1024]{1,0:T(8,128)(2,1)S(1)}, bf16[128,1024]{1,0:T(8,128)(2,1)S(1)}, u32[]{:S(2)}, u32[]{:S(2)}) collective-permute-start(bf16[128,1024]{1,0:T(8,128)(2,1)S(1)} %get-tuple-element.34), channel_id=1, source_target_pairs={{0,1},{1,2},{2,3},{4,5},{5,6},{6,7},{8,9},{9,10},{10,11},{12,13},{... | collective-permute-start | bytes 786440 | tf_op jit(solution)/shard_map/ppermute | solution.py:398
  184.1 13.7 %collective-permute-start.33 = (bf16[2048,128]{1,0:T(8,128)(2,1)S(1)}, bf16[2048,128]{1,0:T(8,128)(2,1)S(1)}, u32[]{:S(2)}, u32[]{:S(2)}) collective-permute-start(bf16[2048,128]{1,0:T(8,128)(2,1)S(1)} %broadcast_select_fusion), channel_id=1, source_target_pairs={{0,4},{4,0},{8,12},{12,8},{1,5},{5,1},{9,13},{13,9},{2,6},{6,2},{1... | collective-permute-start | bytes 1572872 | tf_op jit(solution)/shard_map/ppermute | solution.py:289
  185.7 10.9 %collective-permute-start.10 = (bf16[128,1024]{1,0:T(8,128)(2,1)S(1)}, bf16[128,1024]{1,0:T(8,128)(2,1)S(1)}, u32[]{:S(2)}, u32[]{:S(2)}) collective-permute-start(bf16[128,1024]{1,0:T(8,128)(2,1)S(1)} %fusion.17), channel_id=1, source_target_pairs={{1,0},{2,1},{3,2},{5,4},{6,5},{7,6},{9,8},{10,9},{11,10},{13,12},{... | collective-permute-start | bytes 786440 | tf_op jit(solution)/shard_map/ppermute | solution.py:399
  (22 other events, 259.5 us)

commit v2 on v1

--- a/solution.py
+++ b/solution.py
@@ -53,9 +53,91 @@
     return total
 
 
+def pack_kernel(reqs, meta, pool_ref, px_ref, pb_ref, states_ref, conv_ref):
+    slots = pool_ref.shape[0]
+    inner = px_ref.shape[2]
+    me = meta[0]
+    for s in range(slots):
+        states_ref[s] = pool_ref[s].astype(BF16)
+    for by in range(reqs):
+        at = jnp.clip(meta[2 + (me + by) % reqs] - slots * me, 0, slots - 1)
+        conv_ref[by, :, :inner] = px_ref[at]
+        conv_ref[by, :, inner:] = pb_ref[at]
+
+
+def run_pack(meta, pool, px, pb, reqs):
+    slots, inner, _ = pool.shape
+    return pl.pallas_call(
+        functools.partial(pack_kernel, reqs),
+        grid_spec=pltpu.PrefetchScalarGridSpec(
+            num_scalar_prefetch=1,
+            grid=(1,),
+            in_specs=[
+                pl.BlockSpec(pool.shape, lambda i, m: (0, 0, 0)),
+                pl.BlockSpec(px.shape, lambda i, m: (0, 0, 0)),
+                pl.BlockSpec(pb.shape, lambda i, m: (0, 0, 0)),
+            ],
+            out_specs=[
+                pl.BlockSpec(pool.shape, lambda i, m: (0, 0, 0)),
+                pl.BlockSpec((reqs, CONV - 1, inner + BCW), lambda i, m: (0, 0, 0)),
+            ],
+        ),
+        out_shape=[
+            jax.ShapeDtypeStruct(pool.shape, BF16),
+            jax.ShapeDtypeStruct((reqs, CONV - 1, inner + BCW), BF16),
+        ],
+        compiler_params=pltpu.CompilerParams(vmem_limit_bytes=16 * 2**20),
+        cost_estimate=pl.CostEstimate(flops=10**6, bytes_accessed=3 * 2**20, transcendentals=0),
+        name="pack",
+    )(meta, pool, px, pb)
+
+
+def choose_kernel(reqs, slots, meta, mine_ref, mate_ref, out_ref):
+    slot = meta[2 + (meta[0] + 2 + 2 * pl.program_id(0)) % reqs]
+    out_ref[...] = jnp.where(slot // slots == meta[0], mine_ref[...], mate_ref[...])
+
+
+def run_choose(meta, mine, mate, reqs):
+    slots, inner, _ = mine.shape
+    shape = (1, inner, STATE)
+
+    def held(meta, by, owner):
+        return jnp.clip(meta[2 + (meta[0] + 2 + 2 * by) % reqs] - slots * owner, 0, slots - 1)
+
+    return pl.pallas_call(
+        functools.partial(choose_kernel, reqs, slots),
+        grid_spec=pltpu.PrefetchScalarGridSpec(
+            num_scalar_prefetch=1,
+            grid=(reqs // 2 - 1,),
+            in_specs=[
+                pl.BlockSpec(shape, lambda i, m: (held(m, i, m[0]), 0, 0)),
+                pl.BlockSpec(shape, lambda i, m: (held(m, i, m[0] ^ 1), 0, 0)),
+            ],
+            out_specs=pl.BlockSpec(shape, lambda i, m: (i, 0, 0)),
+        ),
+        out_shape=jax.ShapeDtypeStruct((reqs // 2 - 1, inner, STATE), BF16),
+        compiler_params=pltpu.CompilerParams(vmem_limit_bytes=16 * 2**20),
+        cost_estimate=pl.CostEstimate(flops=10**6, bytes_accessed=2 * 2**20, transcendentals=0),
+        name="choose",
+    )(meta, mine, mate)
+
+
 def scan_kernel(
     heads,
+    slots,
+    reqs,
     meta,
+    *refs,
+):
+    scan_body(heads, slots, reqs, meta, refs[:reqs], *refs[reqs:])
+
+
+def scan_body(
+    heads,
+    slots,
+    reqs,
+    meta,
+    conv_refs,
     x_ref,
     b_ref,
     c_ref,
@@ -65,15 +147,14 @@
     wx_ref,
     wb_ref,
     wc_ref,
-    sx_ref,
-    sb_ref,
-    sc_ref,
     pick_ref,
     y_ref,
     final_ref,
     cmap_ref,
     reach_ref,
     total_ref,
+    conv_ref,
+    start,
     state,
     tail_x,
     tail_m,
@@ -86,12 +167,29 @@
 ):
     block = pl.program_id(0)
     c = pl.program_id(1)
+    me = meta[0]
+    slot = meta[2 + me]
+    inner = conv_ref.shape[1] - BCW
+    group = (meta[1] * heads) // GHEADS
+
+    @pl.when((block == 0) & (c == 0))
+    def _():
+        away = (me - slot // slots + reqs) % reqs
+        taken = conv_refs[0][0].astype(F32)
+        for by in range(1, reqs):
+            taken = jnp.where(away == by, conv_refs[by][...].astype(F32), taken)
+        taken = jnp.where(meta[2 + reqs + me] > 0, taken, 0.0)
+        start[...] = jnp.concatenate(
+            [jnp.zeros((8 - (CONV - 1), inner + BCW), F32), taken], axis=0
+        )
+        conv_ref[...] = taken.astype(BF16)
 
     @pl.when(block == 0)
     def _():
         maps = []
-        for k, (ref, w, s) in enumerate(((b_ref, wb_ref, sb_ref), (c_ref, wc_ref, sc_ref))):
-            before = jnp.where(c == 0, s[...], tail_m[k])
+        for k, (ref, w) in enumerate(((b_ref, wb_ref), (c_ref, wc_ref))):
+            at = pl.multiple_of(inner + (group + k * BCG) * LANES, LANES)
+            before = jnp.where(c == 0, start[:, pl.ds(at, LANES)], tail_m[k])
             x = ref[...].astype(F32)
             maps.append(silu(conv_taps(before, x, w[...].astype(F32))).astype(BF16))
             tail_m[k] = x[SPAN - 8 :]
@@ -109,7 +207,7 @@
             base[...] = jnp.zeros_like(base)
 
         logit = dt_ref[...]
-        live = (row + c * SPAN < meta[1]).astype(F32)
+        live = (row + c * SPAN < meta[2 + 3 * reqs + me]).astype(F32)
         step = (jnp.maximum(logit, 0.0) + jnp.log1p(jnp.exp(-jnp.abs(logit)))) * live
         cum = jnp.dot(
             (row >= col).astype(F32),
@@ -134,7 +232,7 @@
     @pl.when(c == 0)
     def _():
         state[...] = jnp.zeros_like(state)
-        tail_x[...] = sx_ref[...]
+        tail_x[...] = start[:, pl.ds(pl.multiple_of(block * WIDE, WIDE), WIDE)]
 
     pick = pick_ref[...]
     x = x_ref[...].astype(F32)
@@ -153,23 +251,24 @@
         final_ref[...] = jnp.transpose(state[...])
 
 
-def run_scan(meta, x, bc, dt, rate, skip, wx, wbc, sx, sbc, pick, heads):
+def run_scan(meta, conv, x, bc, dt, rate, skip, wx, wbc, pick, heads, slots):
     inner = x.shape[1]
     blocks = inner // WIDE
+    reqs = len(conv)
     once = lambda b, c: jnp.where(b == 0, c, NCH - 1)
-    in_specs = [
+    group = lambda m: (m[1] * heads) // GHEADS
+    in_specs = [pl.BlockSpec((1, CONV - 1, inner + BCW), lambda b, c, m: (0, 0, 0))]
+    in_specs += [pl.BlockSpec((CONV - 1, inner + BCW), lambda b, c, m: (0, 0))] * (reqs - 1)
+    in_specs += [
         pl.BlockSpec((SPAN, WIDE), lambda b, c, m: (c, b)),
-        pl.BlockSpec((SPAN, LANES), lambda b, c, m: (once(b, c), m[0])),
-        pl.BlockSpec((SPAN, LANES), lambda b, c, m: (once(b, c), m[0] + BCG)),
+        pl.BlockSpec((SPAN, LANES), lambda b, c, m: (once(b, c), group(m))),
+        pl.BlockSpec((SPAN, LANES), lambda b, c, m: (once(b, c), group(m) + BCG)),
         pl.BlockSpec((SPAN, LANES), lambda b, c, m: (once(b, c), 0)),
         pl.BlockSpec((1, LANES), lambda b, c, m: (0, 0)),
         pl.BlockSpec((1, WIDE), lambda b, c, m: (0, b)),
         pl.BlockSpec((CONV, WIDE), lambda b, c, m: (0, b)),
-        pl.BlockSpec((CONV, LANES), lambda b, c, m: (0, m[0])),
-        pl.BlockSpec((CONV, LANES), lambda b, c, m: (0, m[0] + BCG)),
-        pl.BlockSpec((8, WIDE), lambda b, c, m: (0, b)),
-        pl.BlockSpec((8, LANES), lambda b, c, m: (0, m[0])),
-        pl.BlockSpec((8, LANES), lambda b, c, m: (0, m[0] + BCG)),
+        pl.BlockSpec((CONV, LANES), lambda b, c, m: (0, group(m))),
+        pl.BlockSpec((CONV, LANES), lambda b, c, m: (0, group(m) + BCG)),
         pl.BlockSpec((LANES, WIDE), lambda b, c, m: (0, b)),
     ]
     out_specs = [
@@ -178,15 +277,17 @@
         pl.BlockSpec((SPAN, LANES), lambda b, c, m: (once(b, c), 0)),
         pl.BlockSpec((SPAN, LANES), lambda b, c, m: (once(b, c), 0)),
         pl.BlockSpec((8, LANES), lambda b, c, m: (0, 0)),
+        pl.BlockSpec((CONV - 1, inner + BCW), lambda b, c, m: (0, 0)),
     ]
     return pl.pallas_call(
-        functools.partial(scan_kernel, heads),
+        functools.partial(scan_kernel, heads, slots, reqs),
         grid_spec=pltpu.PrefetchScalarGridSpec(
             num_scalar_prefetch=1,
             grid=(blocks, NCH),
             in_specs=in_specs,
             out_specs=out_specs,
             scratch_shapes=[
+                pltpu.VMEM((8, inner + BCW), F32),
                 pltpu.VMEM((STATE, WIDE), F32),
                 pltpu.VMEM((8, WIDE), F32),
                 pltpu.VMEM((2, 8, LANES), F32),
@@ -204,6 +305,7 @@
             jax.ShapeDtypeStruct((SUF, LANES), BF16),
             jax.ShapeDtypeStruct((SUF, LANES), BF16),
             jax.ShapeDtypeStruct((8, LANES), F32),
+            jax.ShapeDtypeStruct((CONV - 1, inner + BCW), BF16),
         ],
         compiler_params=pltpu.CompilerParams(
             dimension_semantics=("arbitrary", "arbitrary"), vmem_limit_bytes=24 * 2**20
@@ -212,22 +314,49 @@
             flops=8 * 10**9, bytes_accessed=12 * 2**20, transcendentals=SUF * inner
         ),
         name="local_scan",
-    )(meta, x, bc, bc, dt, rate, skip, wx, wbc, wbc, sx, sbc, sbc, pick)
-
-
-def project_kernel(
-    y_ref, gate_ref, cmap_ref, reach_ref, start_ref, gain_ref, pick_ref, w_ref, out_ref, sq_ref, held
-):
-    @pl.when(pl.program_id(0) == 0)
-    def _():
-        inner = y_ref.shape[1]
+    )(meta, *conv, x, bc, bc, dt, rate, skip, wx, wbc, wbc, pick)
+
+
+def project_kernel(reqs, slots, meta, *refs):
+    others = reqs // 2 - 1
+    mine_ref, mate_ref = refs[:2]
+    got_refs = refs[2 : 2 + others]
+    (
+        y_ref,
+        gate_ref,
+        cmap_ref,
+        reach_ref,
+        gain_ref,
+        pick_ref,
+        w_ref,
+        out_ref,
+        sq_ref,
+        start_ref,
+        held,
+    ) = refs[2 + others :]
+    step = pl.program_id(0)
+    me = meta[0]
+    inner = y_ref.shape[1]
+
+    @pl.when(step == 0)
+    def _():
+        owner = meta[2 + me] // slots
+        away = (me // 2 - owner // 2 + reqs // 2) % (reqs // 2)
+        taken = jnp.where(owner == me, mine_ref[0], mate_ref[0])
+        for k in range(others):
+            taken = jnp.where(away == k + 1, got_refs[k][0], taken)
+        start_ref[...] = jnp.where(meta[2 + reqs + me] > 0, taken, jnp.zeros_like(taken))
+
+    @pl.when(step < NCH)
+    def _():
         squares = jnp.zeros((SPAN, LANES), F32)
+        rows = pl.ds(pl.multiple_of(step * SPAN, SPAN), SPAN)
         for i in range(inner // WIDE):
             at = pl.ds(i * WIDE, WIDE)
             carried = dot_t(cmap_ref[...], start_ref[at, :])
             y = y_ref[:, at] + dot(reach_ref[...], pick_ref[:, at]) * carried
             gated = y * silu(gate_ref[:, at].astype(F32))
-            held[:, at] = (gated * gain_ref[:, at]).astype(BF16)
+            held[rows, at] = (gated * gain_ref[:, at]).astype(BF16)
             gated = gated * gated
             for j in range(WIDE // LANES):
                 squares += gated[:, j * LANES : (j + 1) * LANES]
@@ -239,46 +368,67 @@
             preferred_element_type=F32,
         )
 
-    out_ref[0] = dot(held[...], w_ref[...]).astype(BF16)
-
-
-def run_project(piece, y, gate, cmap, reach, start, gain, pick, weight, shares):
+    @pl.when(step >= NCH)
+    def _():
+        out_ref[0] = dot(held[...], w_ref[...]).astype(BF16)
+
+
+def run_project(meta, mine, mate, got, y, gate, cmap, reach, gain, pick, weight, shares):
+    slots = mine.shape[0]
+    reqs = 2 * len(got) + 2
     inner, width = weight.shape
     share = width // shares
-    rows = lambda n: (piece, 0)
-    whole = lambda n: (0, 0)
+    tile = min(share, WIDE)
+    per = share // tile
+    rows = lambda n, m: (jnp.minimum(n, NCH - 1), 0)
+    whole = lambda n, m: (0, 0)
+    column = lambda n: jnp.maximum(n - NCH, 0)
+    state = (1, inner, STATE)
+
+    def held(owner, m):
+        return jnp.clip(m[2 + m[0]] - slots * owner, 0, slots - 1)
+
     return pl.pallas_call(
-        project_kernel,
-        grid=(shares,),
-        in_specs=[
-            pl.BlockSpec((SPAN, inner), rows),
-            pl.BlockSpec((SPAN, inner), rows),
-            pl.BlockSpec((SPAN, LANES), rows),
-            pl.BlockSpec((SPAN, LANES), rows),
-            pl.BlockSpec((inner, STATE), whole),
-            pl.BlockSpec((1, inner), whole),
-            pl.BlockSpec((LANES, inner), whole),
-            pl.BlockSpec((inner, share), lambda n: (0, n)),
+        functools.partial(project_kernel, reqs, slots),
+        grid_spec=pltpu.PrefetchScalarGridSpec(
+            num_scalar_prefetch=1,
+            grid=(NCH + width // tile,),
+            in_specs=[
+                pl.BlockSpec(state, lambda n, m: (held(m[0], m), 0, 0)),
+                pl.BlockSpec(state, lambda n, m: (held(m[0] ^ 1, m), 0, 0)),
+            ]
+            + [pl.BlockSpec(state, lambda n, m: (0, 0, 0))] * len(got)
+            + [
+                pl.BlockSpec((SPAN, inner), rows),
+                pl.BlockSpec((SPAN, inner), rows),
+                pl.BlockSpec((SPAN, LANES), rows),
+                pl.BlockSpec((SPAN, LANES), rows),
+                pl.BlockSpec((1, inner), whole),
+                pl.BlockSpec((LANES, inner), whole),
+                pl.BlockSpec((inner, tile), lambda n, m: (0, column(n))),
+            ],
+            out_specs=[
+                pl.BlockSpec((1, SUF, tile), lambda n, m: (column(n) // per, 0, column(n) % per)),
+                pl.BlockSpec((8, LANES), lambda n, m: (0, jnp.minimum(n, NCH - 1))),
+                pl.BlockSpec((inner, STATE), whole),
+            ],
+            scratch_shapes=[pltpu.VMEM((SUF, inner), BF16)],
+        ),
+        out_shape=[
+            jax.ShapeDtypeStruct((shares, SUF, share), BF16),
+            jax.ShapeDtypeStruct((8, SUF), F32),
+            jax.ShapeDtypeStruct((inner, STATE), BF16),
         ],
-        out_specs=[
-            pl.BlockSpec((1, SPAN, share), lambda n: (n, 0, 0)),
-            pl.BlockSpec((8, LANES), whole),
-        ],
-        out_shape=[
-            jax.ShapeDtypeStruct((shares, SPAN, share), BF16),
-            jax.ShapeDtypeStruct((8, LANES), F32),
-        ],
-        scratch_shapes=[pltpu.VMEM((SPAN, inner), BF16)],
         compiler_params=pltpu.CompilerParams(
-            dimension_semantics=("arbitrary",), vmem_limit_bytes=32 * 2**20
+            dimension_semantics=("arbitrary",), vmem_limit_bytes=40 * 2**20
         ),
         cost_estimate=pl.CostEstimate(
-            flops=2 * SPAN * inner * width,
-            bytes_accessed=2 * inner * width + 3 * 2**20,
-            transcendentals=SPAN * inner,
+            flops=2 * SUF * inner * width,
+            bytes_accessed=2 * inner * width + 10 * 2**20,
+            transcendentals=SUF * inner,
         ),
         name="project",
-    )(y, gate, cmap, reach, start, gain, pick, weight)
+    )(meta, mine, mate, *got, y, gate, cmap, reach, gain, pick, weight)
 
 
 def shifted(x, axis, size, by):
@@ -317,51 +467,27 @@
     inner = ssm_input.shape[1]
     slots = pool_states.shape[0]
     copies = LANES // heads
-
-    my_len = suffix_len[me]
-    my_slot = prefix_slot[me]
-    my_present = prefix_spans[me] > 0
-
-    pool_conv = jnp.concatenate([pool_conv_x, pool_conv_bc], axis=2)
-
-    def conv_for(request):
-        return lax.dynamic_index_in_dim(
-            pool_conv, jnp.clip(prefix_slot[request] - slots * me, 0, slots - 1), 0, False
-        )
-
-    start_conv = conv_for(me)
-    for by in range(1, num_req):
-        got = shifted(conv_for((me + by) % num_req), "req", num_req, by)
-        start_conv = jnp.where(my_slot // slots == (me - by) % num_req, got, start_conv)
-    start_conv = jnp.where(my_present, start_conv, jnp.zeros_like(start_conv))
-
-    pool_flat = pool_states.astype(BF16).reshape(slots, inner, STATE)
-    pool_mate = swap_core(pool_flat, num_req)
-
-    def state_for(request):
-        slot = prefix_slot[request]
-        mine = lax.dynamic_index_in_dim(
-            pool_flat, jnp.clip(slot - slots * me, 0, slots - 1), 0, False
-        )
-        other = lax.dynamic_index_in_dim(
-            pool_mate, jnp.clip(slot - slots * mate, 0, slots - 1), 0, False
-        )
-        return jnp.where(slot // slots == me, mine, other)
-
-    start = state_for(me)
-    for by in range(2, num_req, 2):
-        got = shifted(state_for((me + by) % num_req), "req", num_req, by)
-        start = jnp.where(my_slot // (2 * slots) == ((me - by) % num_req) // 2, got, start)
-    start = jnp.where(my_present, start, jnp.zeros_like(start))
-
-    before = jnp.pad(start_conv.astype(F32), ((8 - (CONV - 1), 0), (0, 0)))
+    meta = jnp.concatenate(
+        [jnp.stack([me, z]), prefix_slot, prefix_spans, dest_slot, suffix_len]
+    ).astype(jnp.int32)
+
+    mine, conv = run_pack(
+        meta, pool_states.reshape(slots, inner, STATE), pool_conv_x, pool_conv_bc, num_req
+    )
+    other = swap_core(mine, num_req)
+    convs = [conv] + [shifted(conv[by], "req", num_req, by) for by in range(1, num_req)]
+    chosen = run_choose(meta, mine, other, num_req)
+    got = [
+        shifted(chosen[k : k + 1], "req", num_req, 2 * k + 2) for k in range(num_req // 2 - 1)
+    ]
+
     lane_head = jnp.arange(LANES)[:, None]
     pick = (
         (lane_head % heads == (jnp.arange(inner) // HDIM)[None, :]) & (lane_head < 2 * heads)
     ).astype(BF16)
-    meta = jnp.stack([(z * heads) // GHEADS, my_len]).astype(jnp.int32)
-    y_local, local_final, cmap, reach, total = run_scan(
+    y_local, local_final, cmap, reach, total, start_conv = run_scan(
         meta,
+        convs,
         ssm_input,
         bc_input,
         jnp.tile(dt_input, (1, copies)),
@@ -369,43 +495,34 @@
         jnp.repeat(skip_gain, HDIM)[None, :],
         conv_x_weight,
         conv_bc_weight,
-        before[:, :inner],
-        before[:, inner:],
         pick,
         heads,
+        slots,
     )
-
-    gain = norm_gain[None, :]
-    to_right = [(i, i + 1) for i in range(num_tp - 1)]
-    to_left = [(i + 1, i) for i in range(num_tp - 1)]
-    squares, summed = [], []
-    for piece in range(NCH):
-        part, square = run_project(
-            piece, y_local, gate_input, cmap, reach, start, gain, pick, out_weight, num_tp
-        )
-        squares.append(square[0])
-
-        def share(at):
-            return lax.dynamic_index_in_dim(part, jnp.clip(at, 0, num_tp - 1), 0, False)
-
-        right = left = None
-        for s in range(num_tp - 1):
-            go_right = share(num_tp - 1 - s + z)
-            go_left = share(s - (num_tp - 1) + z)
-            if s:
-                go_right = (go_right.astype(F32) + right.astype(F32)).astype(BF16)
-                go_left = (go_left.astype(F32) + left.astype(F32)).astype(BF16)
-            right = lax.ppermute(go_right, "tp", to_right[: s + 1])
-            left = lax.ppermute(go_left, "tp", to_left[num_tp - 2 - s :])
-        summed.append(share(z).astype(F32) + right.astype(F32) + left.astype(F32))
-
-    square = jnp.concatenate(squares)
+    part, square, start = run_project(
+        meta,
+        mine,
+        other,
+        got,
+        y_local,
+        gate_input,
+        cmap,
+        reach,
+        norm_gain[None, :],
+        pick,
+        out_weight,
+        num_tp,
+    )
+    summed = lax.psum_scatter(part, "tp", scatter_dimension=0, tiled=True)[0].astype(F32)
+
+    my_len = suffix_len[me]
+    square = square[0]
     square_total = square
     for by in range(1, num_tp):
         square_total = square_total + shifted(square, "tp", num_tp, by)
     scale = lax.rsqrt(square_total / INNER + 1e-05)
     scale = jnp.where(jnp.arange(SUF) < my_len, scale, 0.0)
-    mixed = (jnp.concatenate(summed, axis=0) * scale[:, None]).astype(BF16)
+    mixed = (summed * scale[:, None]).astype(BF16)
 
     decay = jnp.repeat(total[0, :heads], HDIM)[:, None]
     final = (local_final + decay * start.astype(F32)).astype(BF16)

time: 200 us -> 151 us (0.76)
  starting transfers between devices: 78.3 us -> 12.3 us
  waiting for transfers between devices: 34.1 us -> 56.6 us
  Pallas kernels: 45.9 us -> 35.9 us
  local copies, waits for them, and re-layouts: 9.91 us -> 17.5 us
  other arithmetic: 13.4 us -> 7.47 us
  between operations: 17.4 us -> 20.9 us
    ppermute x24 -> x0, starting transfers between devices: 65.9 us -> none  [the longest x12 55.4 us: per_device(): right = lax.ppermute(go_right, 'tp', to_right[:s + 1])]
    reduce_scatter x0 -> x1, waiting for transfers between devices: none -> 38.7 us  [per_device(): lax.psum_scatter(part, 'tp', scatter_dimension=0, tiled=True)[0].astype(F32)]
    ppermute x24 -> x0, waiting for transfers between devices: 21.4 us -> none  [the longest x12 10.8 us: per_device(): left = lax.ppermute(go_left, 'tp', to_left[num_tp - 2 - s:])]
    pallas_call x5 -> x4, Pallas kernels: 45.9 us -> 35.9 us  [the longest x1 17.8 us: run_project(): pl.pallas_call(functools.partial(project_kernel, reqs, slots), grid_spec=...]
    ppermute x11, waiting for transfers between devices: 12.7 us -> 17.9 us  [shifted(): return lax.ppermute(x, axis, [(i, (i + by) % size) for i in range(size)])]
    unnamed x38 -> x40, local copies, waits for them, and re-layouts: 3.84 us -> 8.76 us
    convert_element_type x14 -> x1, other arithmetic: 5.31 us -> 2.43 us  [per_device(): mixed = (summed * scale[:, None]).astype(BF16)]
    dynamic_slice x3 -> x0, local copies, waits for them, and re-layouts: 2.16 us -> none  [the longest x1 1.41 us: per_device(): my_slot = prefix_slot[me]]
  transfers between devices with their start and end apart: 37 -> 14, of which waited for: 12 -> 5; matrix products, arithmetic and copies ran while one was open for 7% -> 9% of each run, Pallas kernels for 7% -> 11%
where the time goes in v2:
time: 151 us
  waiting for transfers between devices  56.6 us (37%)
  Pallas kernels  35.9 us (24%)
  between operations  20.9 us (14%)
  local copies, waits for them, and re-layouts  17.5 us (12%)
  starting transfers between devices  12.3 us (8%)
  other arithmetic  7.47 us (5%)
    reduce_scatter x1, waiting for transfers between devices, per_device(): lax.psum_scatter(part, 'tp', scatter_dimension=0, tiled=True)[0].astype(F32)  38.7 us
    ppermute x11, waiting for transfers between devices, shifted(): return lax.ppermute(x, axis, [(i, (i + by) % size) for i in range(size)])  17.9 us
    pallas_call x1, Pallas kernels, run_project(): pl.pallas_call(functools.partial(project_kernel, reqs, slots), grid_spec=...  17.8 us
    pallas_call x1, Pallas kernels, run_scan(): pl.pallas_call(functools.partial(scan_kernel, heads, slots, reqs), grid_s...  14.5 us
    ppermute x11, starting transfers between devices, shifted(): return lax.ppermute(x, axis, [(i, (i + by) % size) for i in range(size)])  11.7 us
    unnamed x40, local copies, waits for them, and re-layouts  8.76 us
  transfers between devices with their start and end apart: 14, of which 5 were waited for; matrix products, arithmetic and copies ran while one was open for 9% of the time, Pallas kernels for 11%

profile of v2, /device:TPU:0, one launch (start us, length us, event | category | flops | bytes accessed | tf_op | source)
XLA Modules:
  0.0 150.6 jit_solution(15414566695534027834)
XLA Ops:
  7.2 0.8 copy.27.px_ref
  8.0 0.7 copy.28.pb_ref
  8.7 0.8 concatenate.12.meta
  9.5 1.6 %copy-done.1 = f32[2,32,64,128]{3,2,1,0:T(8,128)S(1)} copy-done((f32[2,32,64,128]{3,2,1,0:T(8,128)S(1)}, f32[2,32,64,128]{3,2,1,0:T(8,128)}, u32[]{:S(2)}) %copy-start.1) | copy-done | bytes 2097176
  11.1 1.6 %pack.1 = (bf16[2,2048,128]{2,1,0:T(8,128)(2,1)}, bf16[4,3,3072]{2,1,0:T(4,128)(2,1)S(1)}) custom-call(s32[18]{0:T(128)S(1)} %concatenate.12.meta, f32[2,2048,128]{2,1,0:T(8,128)S(1)} %bitcast.26, bf16[2,3,2048]{2,1,0:T(4,128)(2,1)S(1)} %copy.27.px_ref, bf16[2,3,1024]{2,1,0:T(4,128)(2,1)S(1)} %copy.28.pb_ref), custom_call_target="tpu_custom_call" | custom-call | flops 1000000 | bytes 3145728 | tf_op jit(solution)/shard_map/pack/pallas_call | solution.py:70
  13.9 3.0 %collective-permute-start.3 = (bf16[3,3072]{1,0:T(4,128)(2,1)}, bf16[3,3072]{1,0:T(4,128)(2,1)}, u32[]{:S(2)}, u32[]{:S(2)}) collective-permute-start(bf16[3,3072]{1,0:T(4,128)(2,1)} %get-tuple-element.29), channel_id=1, source_target_pairs={{0,8},{4,12},{8,0},{12,4},{1,9},{5,13},{9,1},{13,5},{2,10},{6,14},... | collective-permute-start | bytes 55304 | tf_op jit(solution)/shard_map/ppermute | solution.py:435
  16.8 1.0 collective-permute-start.4
  17.8 1.0 and_convert_fusion.refs_13_.refs_8_
  18.9 0.7 tile.6
  19.6 1.1 copy.29.refs_7_
  20.8 1.3 broadcast_in_dim.24
  22.1 0.8 broadcast_in_dim_reshape.4.refs_9_
  22.9 1.9 %choose.1 = bf16[1,2048,128]{2,1,0:T(8,128)(2,1)S(1)} custom-call(s32[18]{0:T(128)S(1)} %concatenate.12.meta, bf16[2,2048,128]{2,1,0:T(8,128)(2,1)} %get-tuple-element.16.mine_ref.refs_0_, bf16[2,2048,128]{2,1,0:T(8,128)(2,1)} %collective-permute-done.mate_ref.refs_1_), custom_call_target="tpu_custom_call" | custom-call | flops 1000000 | bytes 2097152 | tf_op jit(solution)/shard_map/choose/pallas_call | solution.py:107
  26.0 0.7 copy-done.10
  26.7 14.5 %local_scan.1 = (f32[512,2048]{1,0:T(8,128)S(1)}, f32[2048,128]{1,0:T(8,128)S(1)}, bf16[512,128]{1,0:T(8,128)(2,1)S(1)}, bf16[512,128]{1,0:T(8,128)(2,1)S(1)}, f...) custom-call(s32[18]{0:T(128)S(1)} %concatenate.12.meta, bf16[4,3,3072]{2,1,0:T(4,128)(2,1)S(1)} %get-tuple-element.17.refs_0_, ...), custom_call_target="tpu_custom_call" | custom-call | flops 8000000000 | bytes 12582912 | tf_op jit(solution)/shard_map/local_scan/pallas_call | solution.py:282
  41.3 1.0 copy-done.4
  42.3 17.8 %project.1 = (bf16[4,512,1024]{2,1,0:T(8,128)(2,1)S(1)}, f32[8,512]{1,0:T(8,128)S(1)}, bf16[2048,128]{1,0:T(8,128)(2,1)S(1)}) custom-call(s32[18]{0:T(128)S(1)} %concatenate.12.meta, bf16[2,2048,128]{2,1,0:T(8,128)(2,1)} %get-tuple-element.16.mine_ref.refs_0_, bf16[2,2048,128]{2,1,0:T(8,128)(2,1)} %collective-permute-done.mate_ref.refs_1_, ...), custom_call_target="tpu_custom_call" | custom-call | flops 8589934592 | bytes 27262976 | tf_op jit(solution)/shard_map/project/pallas_call | solution.py:391
  60.1 1.9 %copy-done = bf16[4,512,1024]{2,1,0:T(8,128)(2,1)} copy-done((bf16[4,512,1024]{2,1,0:T(8,128)(2,1)}, bf16[4,512,1024]{2,1,0:T(8,128)(2,1)S(1)}, u32[]{:S(2)}) %copy-start) | copy-done | bytes 4194328
  62.0 0.8 copy-done.7
  64.7 0.7 fusion.6
  72.6 1.2 collective-permute-start.11
  74.0 0.7 slice_bitcast_fusion.5
  74.8 1.4 add_convert_fusion
  76.2 0.7 collective-permute-start.8
  77.1 13.7 %collective-permute-done.8 = bf16[2048,128]{1,0:T(8,128)(2,1)S(1)} collective-permute-done((bf16[2048,128]{1,0:T(8,128)(2,1)S(1)}, bf16[2048,128]{1,0:T(8,128)(2,1)S(1)}, u32[]{:S(2)}, u32[]{:S(2)}) %collective-permute-start.8) | collective-permute-done | bytes 524320 | tf_op jit(solution)/shard_map/ppermute | solution.py:435
  91.6 3.6 %collective-permute-start.7 = (f32[512]{0:T(512)S(1)}, f32[512]{0:T(512)S(1)}, u32[]{:S(2)}, u32[]{:S(2)}) collective-permute-start(f32[512]{0:T(512)S(1)} %bitcast.30), channel_id=1, source_target_pairs={{0,3},{1,0},{2,1},{3,2},{4,7},{5,4},{6,5},{7,6},{8,11},{9,8},{10,9... | collective-permute-start | bytes 6152 | tf_op jit(solution)/shard_map/ppermute | solution.py:435
  95.2 1.0 collective-permute-start.5
  96.8 3.2 %collective-permute-done.6 = f32[512]{0:T(512)S(1)} collective-permute-done((f32[512]{0:T(512)S(1)}, f32[512]{0:T(512)S(1)}, u32[]{:S(2)}, u32[]{:S(2)}) %collective-permute-start.6) | collective-permute-done | bytes 2080 | tf_op jit(solution)/shard_map/ppermute | solution.py:435
  100.1 0.7 collective-permute-done.5
  101.5 1.1 convert.3
  102.6 38.7 %reduce-scatter.2.cloned.1.call-done = bf16[1,512,1024]{2,1,0:T(8,128)(2,1)} async-done(((bf16[4,512,1024]{2,1,0:T(8,128)(2,1)}), bf16[1,512,1024]{2,1,0:T(8,128)(2,1)}) %reduce-scatter.2.cloned.1.call-update) | async-done | bytes 1048592 | tf_op jit(solution)/shard_map/reduce_scatter | solution.py:516
  141.3 2.4 %fusion = bf16[512,1024]{1,0:T(8,128)(2,1)} fusion(bf16[1,512,1024]{2,1,0:T(8,128)(2,1)} %reduce-scatter.2.cloned.1.call-done, f32[512]{0:T(512)S(1)} %rsqrt_select_fusion), kind=kLoop, calls=%fused_computation.3 | loop fusion | flops 1572864 | bytes 2099200 | tf_op jit(solution)/shard_map/convert_element_type | solution.py:525
  (74 shorter events, 7.5 us)
Async XLA Ops:
  7.2 11.7 %copy-start.15 = (f32[512,32]{0,1:T(8,128)S(1)}, f32[512,32]{0,1:T(8,128)}, u32[]{:S(2)}) copy-start(f32[512,32]{0,1:T(8,128)} %param.20) | copy-start | bytes 196612
  7.2 13.5 %copy-start.16 = (f32[32]{0:T(128)S(1)}, f32[32]{0:T(128)}, u32[]{:S(2)}) copy-start(f32[32]{0:T(128)} %param.21) | copy-start | bytes 388
  7.2 134.1 %reduce-scatter.2.cloned.1.call-start = ((), (), s32[]{:S(2)}) async-start(), calls=%async_computation.1 | async-start | bytes 5242880 | tf_op jit(solution)/shard_map/reduce_scatter | solution.py:516
  9.5 1.6 %copy-start.1 = (f32[2,32,64,128]{3,2,1,0:T(8,128)S(1)}, f32[2,32,64,128]{3,2,1,0:T(8,128)}, u32[]{:S(2)}) copy-start(f32[2,32,64,128]{3,2,1,0:T(8,128)} %param.27) | copy-start | bytes 6291460
  12.7 10.2 %collective-permute-start = (bf16[2,2048,128]{2,1,0:T(8,128)(2,1)}, bf16[2,2048,128]{2,1,0:T(8,128)(2,1)}, u32[]{:S(2)}, u32[]{:S(2)}) collective-permute-start(bf16[2,2048,128]{2,1,0:T(8,128)(2,1)} %get-tuple-element.16.mine_ref.refs_0_), channel_id=1, source_target_pairs={{0,4},{4,0},{8,12},{12,8},{1,5},{5,1},{9,13},{13,9},{2,6},{6,2},{1... | collective-permute-start | bytes 3145736 | tf_op jit(solution)/shard_map/ppermute | solution.py:439
  13.2 12.8 %copy-start.2 = (bf16[512,2048]{1,0:T(8,128)(2,1)S(1)}, bf16[512,2048]{1,0:T(8,128)(2,1)}, u32[]{:S(2)}) copy-start(bf16[512,2048]{1,0:T(8,128)(2,1)} %refs_4_.2) | copy-start | bytes 6291460
  13.2 12.8 %copy-start.3 = (bf16[512,1024]{1,0:T(8,128)(2,1)S(1)}, bf16[512,1024]{1,0:T(8,128)(2,1)}, u32[]{:S(2)}) copy-start(bf16[512,1024]{1,0:T(8,128)(2,1)} %refs_6_.1) | copy-start | bytes 3145732
  13.2 12.8 %copy-start.12 = (bf16[4,1024]{1,0:T(4,128)(2,1)S(1)}, bf16[4,1024]{1,0:T(4,128)(2,1)}, u32[]{:S(2)}) copy-start(bf16[4,1024]{1,0:T(4,128)(2,1)} %refs_12_.1) | copy-start | bytes 24580
  13.8 11.5 %collective-permute-start.2 = (bf16[3,3072]{1,0:T(4,128)(2,1)}, bf16[3,3072]{1,0:T(4,128)(2,1)S(1)}, u32[]{:S(2)}, u32[]{:S(2)}) collective-permute-start(bf16[3,3072]{1,0:T(4,128)(2,1)} %get-tuple-element.30), channel_id=1, source_target_pairs={{0,4},{4,8},{8,12},{12,0},{1,5},{5,9},{9,13},{13,1},{2,6},{6,10},{... | collective-permute-start | bytes 55304 | tf_op jit(solution)/shard_map/ppermute | solution.py:435
  13.9 12.1 %collective-permute-start.3 = (bf16[3,3072]{1,0:T(4,128)(2,1)}, bf16[3,3072]{1,0:T(4,128)(2,1)}, u32[]{:S(2)}, u32[]{:S(2)}) collective-permute-start(bf16[3,3072]{1,0:T(4,128)(2,1)} %get-tuple-element.29), channel_id=1, source_target_pairs={{0,8},{4,12},{8,0},{12,4},{1,9},{5,13},{9,1},{13,5},{2,10},{6,14},... | collective-permute-start | bytes 55304 | tf_op jit(solution)/shard_map/ppermute | solution.py:435
  16.8 9.1 %collective-permute-start.4 = (bf16[3,3072]{1,0:T(4,128)(2,1)}, bf16[3,3072]{1,0:T(4,128)(2,1)}, u32[]{:S(2)}, u32[]{:S(2)}) collective-permute-start(bf16[3,3072]{1,0:T(4,128)(2,1)} %get-tuple-element.28), channel_id=1, source_target_pairs={{0,12},{4,0},{8,4},{12,8},{1,13},{5,1},{9,5},{13,9},{2,14},{6,2},{... | collective-permute-start | bytes 55304 | tf_op jit(solution)/shard_map/ppermute | solution.py:435
  22.9 3.1 %copy-start.6 = (bf16[128,2048]{1,0:T(8,128)(2,1)S(1)}, bf16[128,2048]{1,0:T(8,128)(2,1)}, u32[]{:S(2)}) copy-start(bf16[128,2048]{1,0:T(8,128)(2,1)} %and_convert_fusion.refs_13_.refs_8_) | copy-start | bytes 1572868
  22.9 3.1 %copy-start.11 = (bf16[4,2048]{1,0:T(4,128)(2,1)S(1)}, bf16[4,2048]{1,0:T(4,128)(2,1)}, u32[]{:S(2)}) copy-start(bf16[4,2048]{1,0:T(4,128)(2,1)} %refs_10_.1) | copy-start | bytes 49156
  22.9 19.3 %copy-start.13 = (f32[2048]{0:T(1024)S(1)}, f32[2048]{0:T(1024)}, u32[]{:S(2)}) copy-start(f32[2048]{0:T(1024)} %param.23) | copy-start | bytes 24580
  24.8 17.4 %copy-start.8 = (bf16[512,2048]{1,0:T(8,128)(2,1)S(1)}, bf16[512,2048]{1,0:T(8,128)(2,1)}, u32[]{:S(2)}) copy-start(bf16[512,2048]{1,0:T(8,128)(2,1)} %refs_4_.3) | copy-start | bytes 6291460
  24.9 17.4 %collective-permute-start.1 = (bf16[1,2048,128]{2,1,0:T(8,128)(2,1)S(1)}, bf16[1,2048,128]{2,1,0:T(8,128)(2,1)S(1)}, u32[]{:S(2)}, u32[]{:S(2)}) collective-permute-start(bf16[1,2048,128]{2,1,0:T(8,128)(2,1)S(1)} %choose.1), channel_id=1, source_target_pairs={{0,8},{4,12},{8,0},{12,4},{1,9},{5,13},{9,1},{13,5},{2,10},{6,14},... | collective-permute-start | bytes 1572872 | tf_op jit(solution)/shard_map/ppermute | solution.py:435
  26.0 0.7 copy-start.10
  41.3 1.0 copy-start.4
  42.2 17.8 %copy-start.14 = (f32[8,128]{1,0:T(8,128)}, f32[8,128]{1,0:T(8,128)S(1)}, u32[]{:S(2)}) copy-start(f32[8,128]{1,0:T(8,128)S(1)} %get-tuple-element.25) | copy-start | bytes 12292
  60.1 1.9 %copy-start = (bf16[4,512,1024]{2,1,0:T(8,128)(2,1)}, bf16[4,512,1024]{2,1,0:T(8,128)(2,1)S(1)}, u32[]{:S(2)}) copy-start(bf16[4,512,1024]{2,1,0:T(8,128)(2,1)S(1)} %get-tuple-element.21) | copy-start | bytes 12582916
  62.0 0.8 copy-start.7
  62.8 0.7 copy-start.17
  62.8 1.2 copy-start.18
  72.0 2.9 %copy-start.5 = (f32[2048,128]{1,0:T(8,128)S(1)}, f32[2048,128]{1,0:T(8,128)}, u32[]{:S(2)}) copy-start(f32[2048,128]{1,0:T(8,128)} %copy-done.4) | copy-start | bytes 3145732
  72.0 4.9 %collective-permute-start.10 = (bf16[3,3072]{1,0:T(4,128)(2,1)S(1)}, bf16[3,3072]{1,0:T(4,128)(2,1)S(1)}, u32[]{:S(2)}, u32[]{:S(2)}) collective-permute-start(bf16[3,3072]{1,0:T(4,128)(2,1)S(1)} %pad_maximum_fusion), channel_id=1, source_target_pairs={{0,12},{4,0},{8,4},{12,8},{1,13},{5,1},{9,5},{13,9},{2,14},{6,2},{... | collective-permute-start | bytes 55304 | tf_op jit(solution)/shard_map/ppermute | solution.py:435
  72.6 4.3 %collective-permute-start.11 = (bf16[3,3072]{1,0:T(4,128)(2,1)S(1)}, bf16[3,3072]{1,0:T(4,128)(2,1)S(1)}, u32[]{:S(2)}, u32[]{:S(2)}) collective-permute-start(bf16[3,3072]{1,0:T(4,128)(2,1)S(1)} %pad_maximum_fusion), channel_id=1, source_target_pairs={{0,8},{4,12},{8,0},{12,4},{1,9},{5,13},{9,1},{13,5},{2,10},{6,14},... | collective-permute-start | bytes 55304 | tf_op jit(solution)/shard_map/ppermute | solution.py:435
  73.8 3.3 %collective-permute-start.12 = (bf16[3,3072]{1,0:T(4,128)(2,1)S(1)}, bf16[3,3072]{1,0:T(4,128)(2,1)S(1)}, u32[]{:S(2)}, u32[]{:S(2)}) collective-permute-start(bf16[3,3072]{1,0:T(4,128)(2,1)S(1)} %pad_maximum_fusion), channel_id=1, source_target_pairs={{0,4},{4,8},{8,12},{12,0},{1,5},{5,9},{9,13},{13,1},{2,6},{6,10},{... | collective-permute-start | bytes 55304 | tf_op jit(solution)/shard_map/ppermute | solution.py:435
  76.2 14.6 %collective-permute-start.8 = (bf16[2048,128]{1,0:T(8,128)(2,1)S(1)}, bf16[2048,128]{1,0:T(8,128)(2,1)S(1)}, u32[]{:S(2)}, u32[]{:S(2)}) collective-permute-start(bf16[2048,128]{1,0:T(8,128)(2,1)S(1)} %add_convert_fusion), channel_id=1, source_target_pairs={{0,8},{4,12},{8,0},{12,4},{1,9},{5,13},{9,1},{13,5},{2,10},{6,14},... | collective-permute-start | bytes 1572872 | tf_op jit(solution)/shard_map/ppermute | solution.py:435
  90.9 10.5 %collective-permute-start.9 = (bf16[2048,128]{1,0:T(8,128)(2,1)S(1)}, bf16[2048,128]{1,0:T(8,128)(2,1)S(1)}, u32[]{:S(2)}, u32[]{:S(2)}) collective-permute-start(bf16[2048,128]{1,0:T(8,128)(2,1)S(1)} %broadcast_select_fusion), channel_id=1, source_target_pairs={{0,4},{4,0},{8,12},{12,8},{1,5},{5,1},{9,13},{13,9},{2,6},{6,2},{1... | collective-permute-start | bytes 1572872 | tf_op jit(solution)/shard_map/ppermute | solution.py:439
  91.6 5.2 %collective-permute-start.7 = (f32[512]{0:T(512)S(1)}, f32[512]{0:T(512)S(1)}, u32[]{:S(2)}, u32[]{:S(2)}) collective-permute-start(f32[512]{0:T(512)S(1)} %bitcast.30), channel_id=1, source_target_pairs={{0,3},{1,0},{2,1},{3,2},{4,7},{5,4},{6,5},{7,6},{8,11},{9,8},{10,9... | collective-permute-start | bytes 6152 | tf_op jit(solution)/shard_map/ppermute | solution.py:435
  95.2 4.9 %collective-permute-start.6 = (f32[512]{0:T(512)S(1)}, f32[512]{0:T(512)S(1)}, u32[]{:S(2)}, u32[]{:S(2)}) collective-permute-start(f32[512]{0:T(512)S(1)} %bitcast.31), channel_id=1, source_target_pairs={{0,2},{1,3},{2,0},{3,1},{4,6},{5,7},{6,4},{7,5},{8,10},{9,11},{10,... | collective-permute-start | bytes 6152 | tf_op jit(solution)/shard_map/ppermute | solution.py:435
  95.2 5.6 %collective-permute-start.5 = (f32[512]{0:T(512)S(1)}, f32[512]{0:T(512)S(1)}, u32[]{:S(2)}, u32[]{:S(2)}) collective-permute-start(f32[512]{0:T(512)S(1)} %bitcast.32), channel_id=1, source_target_pairs={{0,1},{1,2},{2,3},{3,0},{4,5},{5,6},{6,7},{7,4},{8,9},{9,10},{10,1... | collective-permute-start | bytes 6152 | tf_op jit(solution)/shard_map/ppermute | solution.py:435
  (1 other events, 0.6 us)
Sparse Core Ops, SparseCore 0:
  63.0 78.2 reduce-scatter.1

commit v3 on v2

v3 whole, which is shorter than its diff:
```python
import functools

import jax
import jax.numpy as jnp
from jax import lax
from jax.experimental import pallas as pl
from jax.experimental.pallas import tpu as pltpu
from jax.sharding import PartitionSpec as P

HDIM = 64
STATE = 128
GHEADS = 32
CONV = 4
SPAN = 128
SUF = 512
INNER = 8192
BCG = 4
BCW = 1024
NCH = 4
LANES = 128
WIDE = 512
SCAN_WIDE = 1024
PIECES = (2, 2)
VMEM_LIMIT = 56 * 2**20

F32 = jnp.float32
BF16 = jnp.bfloat16
HIGH = lax.Precision.HIGHEST


def wrap(x, n):
    return x & (n - 1) if n & (n - 1) == 0 else x % n


def over(x, n):
    return x >> (n.bit_length() - 1) if n & (n - 1) == 0 else x // n


def silu(x):
    half = 0.5 * x
    return half + half * jnp.tanh(half)


def split_pair(x, heads):
    lane = lax.broadcasted_iota(jnp.int32, x.shape, 1)
    high = x.astype(BF16).astype(F32)
    rest = jnp.where(lane < 2 * heads, x - high, 0.0)
    return jnp.where(lane < heads, high, rest).astype(BF16)


def dot(a, b):
    return jnp.dot(a, b, preferred_element_type=F32)


def dot_t(a, b):
    return lax.dot_general(a, b, (((1,), (1,)), ((), ())), preferred_element_type=F32)


def conv_taps(before, x, weight):
    extended = jnp.concatenate([before, x], axis=0)
    total = extended[8:] * weight[CONV - 1 :]
    for k in range(CONV - 1):
        total += extended[5 + k : 5 + k + SPAN] * weight[k : k + 1]
    return total


def pack_kernel(reqs, meta, px_ref, pb_ref, *conv_refs):
    slots = px_ref.shape[1]
    inner = px_ref.shape[2]
    me = meta[0]
    px = px_ref[...].astype(F32)
    pb = pb_ref[...].astype(F32)
    for by in range(reqs):
        at = jnp.clip(meta[2 + wrap(me + by, reqs)] - slots * me, 0, slots - 1)
        sent_x, sent_b = px[:, 0], pb[:, 0]
        for s in range(1, slots):
            sent_x = jnp.where(at == s, px[:, s], sent_x)
            sent_b = jnp.where(at == s, pb[:, s], sent_b)
        conv_refs[by][:, :inner] = sent_x.astype(BF16)
        conv_refs[by][:, inner:] = sent_b.astype(BF16)


def run_pack(meta, px, pb, reqs):
    taps, _, inner = px.shape
    return pl.pallas_call(
        functools.partial(pack_kernel, reqs),
        grid_spec=pltpu.PrefetchScalarGridSpec(
            num_scalar_prefetch=1,
            grid=(1,),
            in_specs=[
                pl.BlockSpec(px.shape, lambda i, m: (0, 0, 0)),
                pl.BlockSpec(pb.shape, lambda i, m: (0, 0, 0)),
            ],
            out_specs=[pl.BlockSpec((taps, inner + BCW), lambda i, m: (0, 0))] * reqs,
        ),
        out_shape=[jax.ShapeDtypeStruct((taps, inner + BCW), BF16)] * reqs,
        compiler_params=pltpu.CompilerParams(vmem_limit_bytes=VMEM_LIMIT),
        cost_estimate=pl.CostEstimate(flops=10**6, bytes_accessed=2**18, transcendentals=0),
        name="pack",
    )(meta, px, pb)


def choose_kernel(reqs, slots, meta, mine_ref, mate_ref, out_ref, mark_ref):
    slot = meta[2 + wrap(meta[0] + 2 + 2 * pl.program_id(0), reqs)]
    out_ref[...] = jnp.where(over(slot, slots) == meta[0], mine_ref[...], mate_ref[...]).astype(BF16)
    mark_ref[...] = jnp.zeros_like(mark_ref)


def run_choose(meta, mine, mate, reqs):
    slots, inner, _ = mine.shape
    shape = (1, WIDE, STATE)

    def held(meta, by, owner):
        return jnp.clip(meta[2 + wrap(meta[0] + 2 + 2 * by, reqs)] - slots * owner, 0, slots - 1)

    return pl.pallas_call(
        functools.partial(choose_kernel, reqs, slots),
        grid_spec=pltpu.PrefetchScalarGridSpec(
            num_scalar_prefetch=1,
            grid=(reqs // 2 - 1, inner // WIDE),
            in_specs=[
                pl.BlockSpec(shape, lambda i, j, m: (held(m, i, m[0]), j, 0)),
                pl.BlockSpec(shape, lambda i, j, m: (held(m, i, m[0] ^ 1), j, 0)),
            ],
            out_specs=[
                pl.BlockSpec(shape, lambda i, j, m: (i, j, 0)),
                pl.BlockSpec((8, LANES), lambda i, j, m: (0, 0)),
            ],
        ),
        out_shape=[
            jax.ShapeDtypeStruct((reqs // 2 - 1, inner, STATE), BF16),
            jax.ShapeDtypeStruct((8, LANES), F32),
        ],
        compiler_params=pltpu.CompilerParams(vmem_limit_bytes=VMEM_LIMIT),
        cost_estimate=pl.CostEstimate(flops=10**6, bytes_accessed=2 * 2**20, transcendentals=0),
        name="choose",
    )(meta, mine, mate)


def scan_kernel(
    heads,
    slots,
    reqs,
    meta,
    *refs,
):
    scan_body(heads, slots, reqs, meta, refs[:reqs], *refs[reqs + 1 :])


def scan_body(
    heads,
    slots,
    reqs,
    meta,
    conv_refs,
    x_ref,
    b_ref,
    c_ref,
    dt_ref,
    rate_ref,
    skip_ref,
    wx_ref,
    wb_ref,
    wc_ref,
    y_ref,
    final_ref,
    cmap_ref,
    reach_ref,
    total_ref,
    conv_ref,
    pick_ref,
    start,
    state,
    tail_x,
    tail_m,
    left,
    bmap_t,
    factors,
    base,
):
    block = pl.program_id(0)
    c = pl.program_id(1)
    me = meta[0]
    slot = meta[2 + me]
    inner = conv_ref.shape[1] - BCW
    group = over(meta[1] * heads, GHEADS)

    @pl.when((block == 0) & (c == 0))
    def _():
        away = wrap(me - over(slot, slots) + reqs, reqs)
        taken = conv_refs[0][...].astype(F32)
        for by in range(1, reqs):
            taken = jnp.where(away == by, conv_refs[by][...].astype(F32), taken)
        taken = jnp.where(meta[2 + reqs + me] > 0, taken, 0.0)
        start[...] = jnp.concatenate(
            [jnp.zeros((8 - (CONV - 1), inner + BCW), F32), taken], axis=0
        )
        conv_ref[...] = taken.astype(BF16)

    @pl.when(block == 0)
    def _():
        maps = []
        for k, (ref, w) in enumerate(((b_ref, wb_ref), (c_ref, wc_ref))):
            at = pl.multiple_of(inner + (group + k * BCG) * LANES, LANES)
            before = jnp.where(c == 0, start[:, pl.ds(at, LANES)], tail_m[k])
            x = ref[...].astype(F32)
            maps.append(silu(conv_taps(before, x, w[...].astype(F32))).astype(BF16))
            tail_m[k] = x[SPAN - 8 :]
        bmap, cmap = maps
        row = lax.broadcasted_iota(jnp.int32, (SPAN, SPAN), 0)
        col = lax.broadcasted_iota(jnp.int32, (SPAN, SPAN), 1)
        scores = jnp.where(row >= col, dot_t(cmap, bmap), 0.0).astype(BF16)
        left[c, :, :SPAN] = scores
        left[c, :, SPAN:] = cmap
        cmap_ref[...] = cmap
        bmap_t[c] = jnp.transpose(bmap.astype(F32)).astype(BF16)

        @pl.when(c == 0)
        def _():
            base[...] = jnp.zeros_like(base)

        copies = LANES // heads
        logit = jnp.transpose(jnp.concatenate([dt_ref[...]] * copies, axis=0))
        rate = jnp.concatenate([rate_ref[...].reshape(1, heads)] * copies, axis=1)
        skip = jnp.concatenate([skip_ref[...].reshape(1, heads)] * copies, axis=1)
        live = (row + c * SPAN < meta[2 + 3 * reqs + me]).astype(F32)
        step = (jnp.maximum(logit, 0.0) + jnp.log1p(jnp.exp(-jnp.abs(logit)))) * live
        cum = jnp.dot(
            (row >= col).astype(F32),
            -step * rate,
            precision=HIGH,
            preferred_element_type=F32,
        )
        last = cum[SPAN - 1 :]
        mid = 0.5 * last
        factors[c, :SPAN] = split_pair(jnp.exp(cum - mid), heads)
        factors[c, SPAN : 2 * SPAN] = split_pair(jnp.exp(mid - cum) * step, heads)
        before = base[0:1]
        reach_ref[...] = split_pair(jnp.exp(before + cum), heads)
        which = lax.broadcasted_iota(jnp.int32, (16, LANES), 0)
        singles = jnp.where(which == 1, jnp.exp(last - mid), skip)
        factors[c, 2 * SPAN :] = split_pair(jnp.where(which == 0, jnp.exp(mid), singles), heads)
        base[...] = base[...] + last
        total_ref[...] = split_pair(jnp.exp(base[...]), heads)

    @pl.when(c == 0)
    def _():
        state[...] = jnp.zeros_like(state)
        lane = lax.broadcasted_iota(jnp.int32, (LANES, SCAN_WIDE), 0)
        channel = lax.broadcasted_iota(jnp.int32, (LANES, SCAN_WIDE), 1) + block * SCAN_WIDE
        pick_ref[...] = ((wrap(lane, heads) == over(channel, HDIM)) & (lane < 2 * heads)).astype(BF16)
        tail_x[...] = start[:, pl.ds(pl.multiple_of(block * SCAN_WIDE, SCAN_WIDE), SCAN_WIDE)]

    x = x_ref[...].astype(F32)
    conv = conv_taps(tail_x[...], x, wx_ref[...].astype(F32))
    tail_x[...] = x[SPAN - 8 :]
    values = silu(conv).astype(BF16).astype(F32)
    spread = dot(factors[c], pick_ref[...])
    rows = spread[2 * SPAN :]
    scaled = (values * spread[SPAN : 2 * SPAN]).astype(BF16)
    held = state[...] * rows[0:1]
    right = jnp.concatenate([scaled, held.astype(BF16)], axis=0)
    y_ref[...] = dot(left[c], right) * spread[:SPAN] + rows[2:3] * values
    state[...] = (held + dot(bmap_t[c], scaled)) * rows[1:2]

    @pl.when(c == NCH - 1)
    def _():
        final_ref[...] = jnp.transpose(state[...])


def run_scan(meta, conv, mark, x, bc, dt, rate, skip, wx, wbc, heads, slots):
    inner = x.shape[1]
    blocks = inner // SCAN_WIDE
    reqs = len(conv)
    once = lambda b, c: jnp.where(b == 0, c, NCH - 1)
    group = lambda m: over(m[1] * heads, GHEADS)
    in_specs = [pl.BlockSpec((CONV - 1, inner + BCW), lambda b, c, m: (0, 0))] * reqs
    in_specs += [
        pl.BlockSpec((8, LANES), lambda b, c, m: (0, 0)),
        pl.BlockSpec((SPAN, SCAN_WIDE), lambda b, c, m: (c, b)),
        pl.BlockSpec((SPAN, LANES), lambda b, c, m: (once(b, c), group(m))),
        pl.BlockSpec((SPAN, LANES), lambda b, c, m: (once(b, c), group(m) + BCG)),
        pl.BlockSpec((heads, SPAN), lambda b, c, m: (0, once(b, c))),
        pl.BlockSpec((heads,), lambda b, c, m: (0,)),
        pl.BlockSpec((heads,), lambda b, c, m: (0,)),
        pl.BlockSpec((CONV, SCAN_WIDE), lambda b, c, m: (0, b)),
        pl.BlockSpec((CONV, LANES), lambda b, c, m: (0, group(m))),
        pl.BlockSpec((CONV, LANES), lambda b, c, m: (0, group(m) + BCG)),
    ]
    out_specs = [
        pl.BlockSpec((SPAN, SCAN_WIDE), lambda b, c, m: (c, b)),
        pl.BlockSpec((SCAN_WIDE, STATE), lambda b, c, m: (b, 0)),
        pl.BlockSpec((SPAN, LANES), lambda b, c, m: (once(b, c), 0)),
        pl.BlockSpec((SPAN, LANES), lambda b, c, m: (once(b, c), 0)),
        pl.BlockSpec((16, LANES), lambda b, c, m: (0, 0)),
        pl.BlockSpec((CONV - 1, inner + BCW), lambda b, c, m: (0, 0)),
        pl.BlockSpec((LANES, SCAN_WIDE), lambda b, c, m: (0, b)),
    ]
    return pl.pallas_call(
        functools.partial(scan_kernel, heads, slots, reqs),
        grid_spec=pltpu.PrefetchScalarGridSpec(
            num_scalar_prefetch=1,
            grid=(blocks, NCH),
            in_specs=in_specs,
            out_specs=out_specs,
            scratch_shapes=[
                pltpu.VMEM((8, inner + BCW), F32),
                pltpu.VMEM((STATE, SCAN_WIDE), F32),
                pltpu.VMEM((8, SCAN_WIDE), F32),
                pltpu.VMEM((2, 8, LANES), F32),
                pltpu.VMEM((NCH, SPAN, 2 * SPAN), BF16),
                pltpu.VMEM((NCH, STATE, SPAN), BF16),
                pltpu.VMEM((NCH, 2 * SPAN + 16, LANES), BF16),
                pltpu.VMEM((16, LANES), F32),
            ],
        ),
        out_shape=[
            jax.ShapeDtypeStruct((SUF, inner), F32),
            jax.ShapeDtypeStruct((inner, STATE), F32),
            jax.ShapeDtypeStruct((SUF, LANES), BF16),
            jax.ShapeDtypeStruct((SUF, LANES), BF16),
            jax.ShapeDtypeStruct((16, LANES), BF16),
            jax.ShapeDtypeStruct((CONV - 1, inner + BCW), BF16),
            jax.ShapeDtypeStruct((LANES, inner), BF16),
        ],
        compiler_params=pltpu.CompilerParams(
            dimension_semantics=("arbitrary", "arbitrary"), vmem_limit_bytes=VMEM_LIMIT
        ),
        cost_estimate=pl.CostEstimate(
            flops=8 * 10**9, bytes_accessed=12 * 2**20, transcendentals=SUF * inner
        ),
        name="local_scan",
    )(meta, *conv, mark, x, bc, bc, dt, rate, skip, wx, wbc, wbc)


def project_kernel(chunks, shares, picks, meta, *refs):
    if picks:
        reqs, slots = picks
        others = reqs // 2 - 1
        mine_ref, mate_ref = refs[:2]
        got_refs = refs[2 : 2 + others]
        refs = refs[2 + others :]
    else:
        start_ref, refs = refs[0], refs[1:]
    y_ref, gate_ref, cmap_ref, reach_ref, gain_ref, pick_ref, w_ref = refs[:7]
    out_refs = refs[7 : 7 + shares]
    sq_ref = refs[7 + shares]
    if picks:
        start_ref = refs[8 + shares]
    held, w_held, arrived = refs[-3:]
    step = pl.program_id(0)
    inner = y_ref.shape[1]
    share = out_refs[0].shape[1]

    def fetch(q):
        column = pl.multiple_of(wrap(q + meta[1], shares) * share, share)
        return pltpu.make_async_copy(
            w_ref.at[:, pl.ds(column, share)], w_held.at[q], arrived.at[q]
        )

    @pl.when(step == 0)
    def _():
        for q in range(shares):
            fetch(q).start()

    if picks:

        @pl.when(step == 0)
        def _():
            me = meta[0]
            owner = over(meta[2 + me], slots)
            away = wrap(over(me, 2) - over(owner, 2) + reqs // 2, reqs // 2)
            taken = jnp.where(owner == me, mine_ref[0], mate_ref[0])
            for k in range(others):
                taken = jnp.where(away == k + 1, got_refs[k][0].astype(F32), taken)
            start_ref[...] = jnp.where(meta[2 + reqs + me] > 0, taken, 0.0).astype(BF16)

    @pl.when(step < chunks)
    def _():
        squares = jnp.zeros((SPAN, LANES), F32)
        rows = pl.ds(pl.multiple_of(step * SPAN, SPAN), SPAN)
        for i in range(inner // WIDE):
            at = pl.ds(i * WIDE, WIDE)
            carried = dot_t(cmap_ref[...], start_ref[at, :])
            y = y_ref[:, at] + dot(reach_ref[...], pick_ref[:, at]) * carried
            gated = y * silu(gate_ref[:, at].astype(F32))
            held[rows, at] = (gated * gain_ref[:, at]).astype(BF16)
            gated = gated * gated
            for j in range(WIDE // LANES):
                squares += gated[:, j * LANES : (j + 1) * LANES]
        sq_ref[...] = lax.dot_general(
            jnp.ones((8, LANES), F32),
            squares,
            (((1,), (1,)), ((), ())),
            precision=HIGH,
            preferred_element_type=F32,
        )

    for q in range(shares):

        @pl.when(step == chunks + q)
        def _(q=q):
            fetch(q).wait()
            out_refs[q][...] = dot(held[...], w_held[q]).astype(BF16)


def run_project(first, chunks, meta, states, y, gate, cmap, reach, gain, pick, weight, shares, reqs):
    inner, width = weight.shape
    share = width // shares
    count = chunks * SPAN
    rows = lambda n, m: (first + jnp.minimum(n, chunks - 1), 0)
    whole = lambda n, m: (0, 0)
    state = (1, inner, STATE)
    choose = len(states) > 1
    slots = states[0].shape[0]

    def held(owner, m):
        return jnp.clip(m[2 + m[0]] - slots * owner, 0, slots - 1)

    if choose:
        state_specs = [
            pl.BlockSpec(state, lambda n, m: (held(m[0], m), 0, 0)),
            pl.BlockSpec(state, lambda n, m: (held(m[0] ^ 1, m), 0, 0)),
        ] + [pl.BlockSpec(state, lambda n, m: (0, 0, 0))] * (len(states) - 2)
    else:
        state_specs = [pl.BlockSpec((inner, STATE), whole)]
    out_specs = [
        pl.BlockSpec((count, share), whole)
        for q in range(shares)
    ] + [pl.BlockSpec((8, LANES), lambda n, m: (0, jnp.minimum(n, chunks - 1)))]
    out_shape = [jax.ShapeDtypeStruct((count, share), BF16)] * shares + [
        jax.ShapeDtypeStruct((8, count), F32)
    ]
    if choose:
        out_specs.append(pl.BlockSpec((inner, STATE), whole))
        out_shape.append(jax.ShapeDtypeStruct((inner, STATE), BF16))
    return pl.pallas_call(
        functools.partial(project_kernel, chunks, shares, (reqs, slots) if choose else None),
        grid_spec=pltpu.PrefetchScalarGridSpec(
            num_scalar_prefetch=1,
            grid=(chunks + shares,),
            in_specs=state_specs
            + [
                pl.BlockSpec((SPAN, inner), rows),
                pl.BlockSpec((SPAN, inner), rows),
                pl.BlockSpec((SPAN, LANES), rows),
                pl.BlockSpec((SPAN, LANES), rows),
                pl.BlockSpec((1, inner), whole),
                pl.BlockSpec((LANES, inner), whole),
                pl.BlockSpec(memory_space=pl.ANY),
            ],
            out_specs=out_specs,
            scratch_shapes=[
                pltpu.VMEM((count, inner), BF16),
                pltpu.VMEM((shares, inner, share), BF16),
                pltpu.SemaphoreType.DMA((shares,)),
            ],
        ),
        out_shape=out_shape,
        compiler_params=pltpu.CompilerParams(
            dimension_semantics=("arbitrary",), vmem_limit_bytes=VMEM_LIMIT
        ),
        cost_estimate=pl.CostEstimate(
            flops=2 * count * inner * width,
            bytes_accessed=2 * inner * width + 10 * 2**20,
            transcendentals=count * inner,
        ),
        name="project",
    )(meta, *states, y, gate, cmap, reach, gain, pick, weight)


def line_sums(parts, size):
    to_right = [(i, i + 1) for i in range(size - 1)]
    to_left = [(i + 1, i) for i in range(size - 1)]
    add = lambda a, b: (a.astype(F32) + b.astype(F32)).astype(BF16)
    right = [None] * len(parts)
    left = [None] * len(parts)
    for s in range(size - 1):
        for p, part in enumerate(parts):
            go_right, go_left = part[size - 1 - s], part[s + 1]
            if s:
                if p + 1 < len(parts) and s == 1:
                    right[p], left[p], _ = lax.optimization_barrier(
                        (right[p], left[p], parts[p + 1][0])
                    )
                go_right, go_left = add(go_right, right[p]), add(go_left, left[p])
            right[p] = lax.ppermute(go_right, "tp", to_right[: s + 1])
            left[p] = lax.ppermute(go_left, "tp", to_left[size - 2 - s :])
    return [
        part[0].astype(F32) + r.astype(F32) + l.astype(F32)
        for part, r, l in zip(parts, right, left)
    ]


def source_of(meta, device, reqs):
    found = jnp.int32(0)
    for r in range(reqs):
        found += jnp.where(meta[2 + 2 * reqs + r] == device, r, 0)
    return found


def ending_kernel(reqs, meta, mark_ref, local_ref, start_ref, total_ref, pick_ref, conv_ref, x_ref, bc_ref, out_ref):
    inner = local_ref.shape[0]
    length = meta[2 + 3 * reqs + meta[0]]
    for i in range(inner // WIDE):
        at = pl.ds(i * WIDE, WIDE)
        decay = dot(total_ref[...], pick_ref[:, at])[0:1]
        decay = jnp.transpose(jnp.broadcast_to(decay, (STATE, WIDE)))
        out_ref[at, :] = (local_ref[at, :] + decay * start_ref[at, :].astype(F32)).astype(BF16)
    row = lax.broadcasted_iota(jnp.int32, (16, SUF), 0) + length - (CONV - 1)
    found = (row == lax.broadcasted_iota(jnp.int32, (16, SUF), 1)).astype(BF16)
    conv = conv_ref[...].astype(F32)
    row = lax.broadcasted_iota(jnp.int32, (16, WIDE), 0) + length
    for i in range((inner + BCW) // WIDE):
        at = i * WIDE
        source = x_ref[:, at : at + WIDE] if at < inner else bc_ref[:, at - inner : at - inner + WIDE]
        tail = dot(found, source)
        for k in range(CONV - 1):
            tail += jnp.where(row == k, conv[k : k + 1, at : at + WIDE], 0.0)
        tail = tail.astype(BF16)
        for j in range(WIDE // LANES):
            to = inner + (at // LANES + j) * 16
            out_ref[to : to + 16, :] = tail[:, j * LANES : (j + 1) * LANES]


def run_ending(meta, mark, local, start, total, pick, conv, x, bc, reqs):
    inner = local.shape[0]
    rows = inner + (inner + BCW) // LANES * 16
    operands = (mark, local, start, total, pick, conv, x, bc)
    return pl.pallas_call(
        functools.partial(ending_kernel, reqs),
        grid_spec=pltpu.PrefetchScalarGridSpec(
            num_scalar_prefetch=1,
            grid=(1,),
            in_specs=[pl.BlockSpec(a.shape, lambda i, m: (0, 0)) for a in operands],
            out_specs=pl.BlockSpec((rows, LANES), lambda i, m: (0, 0)),
        ),
        out_shape=jax.ShapeDtypeStruct((rows, LANES), BF16),
        compiler_params=pltpu.CompilerParams(vmem_limit_bytes=VMEM_LIMIT),
        cost_estimate=pl.CostEstimate(flops=10**8, bytes_accessed=6 * 2**20, transcendentals=0),
        name="ending",
    )(meta, *operands)


def route_kernel(reqs, meta, *refs):
    origin = over(source_of(meta, meta[0] ^ 1, reqs), 2)
    away = wrap(over(meta[0], 2) - origin + reqs // 2, reqs // 2)
    taken = refs[0][...]
    for k in range(1, reqs // 2):
        taken = jnp.where(away == k, refs[k][...], taken)
    refs[-1][...] = taken


def run_route(meta, ends, reqs):
    shape = ends[0].shape
    return pl.pallas_call(
        functools.partial(route_kernel, reqs),
        grid_spec=pltpu.PrefetchScalarGridSpec(
            num_scalar_prefetch=1,
            grid=(1,),
            in_specs=[pl.BlockSpec(shape, lambda i, m: (0, 0))] * len(ends),
            out_specs=pl.BlockSpec(shape, lambda i, m: (0, 0)),
        ),
        out_shape=jax.ShapeDtypeStruct(shape, BF16),
        compiler_params=pltpu.CompilerParams(vmem_limit_bytes=VMEM_LIMIT),
        cost_estimate=pl.CostEstimate(flops=10**6, bytes_accessed=2 * 2**20, transcendentals=0),
        name="route",
    )(meta, *ends)


def land_kernel(reqs, meta, *refs):
    state_ref, x_ref, bc_ref = refs[-3:]
    crossed_ref = refs[-4]
    source = source_of(meta, meta[0], reqs)
    away = wrap(over(meta[0], 2) - over(source, 2) + reqs // 2, reqs // 2)
    inner = state_ref.shape[0]

    def taken(at):
        value = refs[0][at, :]
        for k in range(1, reqs // 2):
            value = jnp.where(away == k, refs[k][at, :], value)
        return jnp.where((source & 1) == (meta[0] & 1), value, crossed_ref[at, :])

    for i in range(inner // WIDE):
        at = pl.ds(i * WIDE, WIDE)
        state_ref[at, :] = taken(at).astype(F32)
    tiles = (inner + BCW) // LANES
    tails = [taken(pl.ds(inner + j * 16, 16))[: CONV - 1] for j in range(tiles)]
    x_ref[...] = jnp.concatenate(tails[: inner // LANES], axis=1)
    bc_ref[...] = jnp.concatenate(tails[inner // LANES :], axis=1)


def run_land(meta, ends, crossed, inner, reqs):
    shape = crossed.shape
    outs = [(inner, STATE), (CONV - 1, inner), (CONV - 1, BCW)]
    return pl.pallas_call(
        functools.partial(land_kernel, reqs),
        grid_spec=pltpu.PrefetchScalarGridSpec(
            num_scalar_prefetch=1,
            grid=(1,),
            in_specs=[pl.BlockSpec(shape, lambda i, m: (0, 0))] * (len(ends) + 1),
            out_specs=[pl.BlockSpec(o, lambda i, m: (0, 0)) for o in outs],
        ),
        out_shape=[jax.ShapeDtypeStruct(o, t) for o, t in zip(outs, (F32, BF16, BF16))],
        compiler_params=pltpu.CompilerParams(vmem_limit_bytes=VMEM_LIMIT),
        cost_estimate=pl.CostEstimate(flops=10**6, bytes_accessed=3 * 2**20, transcendentals=0),
        name="land",
    )(meta, *ends, crossed)


def shifted(x, axis, size, by):
    return lax.ppermute(x, axis, [(i, (i + by) % size) for i in range(size)])


def swap_core(x, size):
    return lax.ppermute(x, "req", [(i, i ^ 1) for i in range(size)])


def per_device(
    ssm_input,
    gate_input,
    bc_input,
    dt_input,
    decay_rate,
    skip_gain,
    norm_gain,
    conv_x_weight,
    conv_bc_weight,
    out_weight,
    pool_states,
    pool_conv_x,
    pool_conv_bc,
    prefix_slot,
    prefix_spans,
    dest_slot,
    suffix_len,
):
    num_req = lax.axis_size("req")
    num_tp = lax.axis_size("tp")
    me = lax.axis_index("req")
    z = lax.axis_index("tp")
    heads = dt_input.shape[1]
    inner = ssm_input.shape[1]
    slots = pool_states.shape[0]
    meta = jnp.concatenate(
        [jnp.stack([me, z]), prefix_slot, prefix_spans, dest_slot, suffix_len]
    ).astype(jnp.int32)

    mine = pool_states.reshape(slots, inner, STATE)
    other = swap_core(mine, num_req)
    conv = run_pack(
        meta,
        jnp.transpose(pool_conv_x, (1, 0, 2)),
        jnp.transpose(pool_conv_bc, (1, 0, 2)),
        num_req,
    )
    convs = [conv[0]] + [shifted(conv[by], "req", num_req, by) for by in range(1, num_req)]
    chosen, mark = run_choose(meta, mine, other, num_req)
    got = [
        shifted(chosen[k : k + 1], "req", num_req, 2 * k + 2) for k in range(num_req // 2 - 1)
    ]

    y_local, local_final, cmap, reach, total, start_conv, pick = run_scan(
        meta,
        convs,
        mark,
        ssm_input,
        bc_input,
        dt_input.T,
        decay_rate,
        skip_gain,
        conv_x_weight,
        conv_bc_weight,
        heads,
        slots,
    )
    states = [mine, other] + got
    parts, squares = [], []
    first = 0
    for chunks in PIECES:
        result = run_project(
            first,
            chunks,
            meta,
            states,
            y_local,
            gate_input,
            cmap,
            reach,
            norm_gain[None, :],
            pick,
            out_weight,
            num_tp,
            num_req,
        )
        first += chunks
        parts.append(result[:num_tp])
        squares.append(result[num_tp][0])
        if len(states) > 1:
            start = result[num_tp + 1]
            states = [start]
    summed = jnp.concatenate(line_sums(parts, num_tp), axis=0)

    my_len = suffix_len[me]
    square = jnp.concatenate(squares)
    square_total = square
    for by in range(1, num_tp):
        square_total = square_total + shifted(square, "tp", num_tp, by)
    scale = lax.rsqrt(square_total / INNER + 1e-05)
    scale = jnp.where(jnp.arange(SUF) < my_len, scale, 0.0)
    mixed = (summed * scale[:, None]).astype(BF16)

    end = run_ending(
        meta, result[num_tp], local_final, start, total, pick, start_conv, ssm_input, bc_input, num_req
    )
    ends = [end] + [shifted(end, "req", num_req, by) for by in range(2, num_req, 2)]
    crossed = swap_core(run_route(meta, ends, num_req), num_req)
    ckpt_states, ckpt_x, ckpt_bc = run_land(meta, ends, crossed, inner, num_req)
    return (
        mixed,
        ckpt_states.reshape((1, heads, HDIM, STATE)),
        ckpt_x[None],
        ckpt_bc[None],
    )


def solution(mesh):
    return jax.shard_map(
        per_device,
        mesh=mesh,
        in_specs=(
            P(("groups", "req"), "tp"),
            P(("groups", "req"), "tp"),
            P(("groups", "req"), None),
            P(("groups", "req"), "tp"),
            P("tp"),
            P("tp"),
            P("tp"),
            P(None, "tp"),
            P(),
            P("tp", None),
            P(("groups", "req"), "tp", None, None),
            P(("groups", "req"), None, "tp"),
            P(("groups", "req"), None, None),
            P("groups"),
            P("groups"),
            P("groups"),
            P("groups"),
        ),
        out_specs=(
            P(("groups", "req"), "tp"),
            P(("groups", "req"), "tp", None, None),
            P(("groups", "req"), None, "tp"),
            P(("groups", "req"), None, None),
        ),
        check_vma=False,
    )
```

time: 151 us -> 139 us (0.921)
  waiting for transfers between devices: 56.6 us -> 23.4 us
  starting transfers between devices: 12.3 us -> 43.5 us
  between operations: 20.9 us -> 1.01 us
  Pallas kernels: 35.9 us -> 55.4 us
  local copies, waits for them, and re-layouts: 17.5 us -> 7.02 us
    reduce_scatter x1 -> x0, waiting for transfers between devices: 38.7 us -> none  [per_device(): lax.psum_scatter(part, 'tp', scatter_dimension=0, tiled=True)[0].astype(F32)]
    ppermute x0 -> x12, starting transfers between devices: none -> 34 us  [the longest x6 28.7 us: line_sums(): right[p] = lax.ppermute(go_right, 'tp', to_right[:s + 1])]
    pallas_call x1 -> x5, Pallas kernels: 17.8 us -> 35.3 us  [the longest x2 24.4 us: run_project(): pl.pallas_call(functools.partial(project_kernel, chunks, shares, (reqs, s...]
    ppermute x0 -> x12, waiting for transfers between devices: none -> 16 us  [the longest x6 11.1 us: line_sums(): right[p] = lax.ppermute(go_right, 'tp', to_right[:s + 1])]
    ppermute x11 -> x8, waiting for transfers between devices: 17.9 us -> 7.37 us  [shifted(): return lax.ppermute(x, axis, [(i, (i + by) % size) for i in range(size)])]
    unnamed x40 -> x32, local copies, waits for them, and re-layouts: 8.76 us -> 3.76 us
    ppermute x11 -> x8, starting transfers between devices: 11.7 us -> 8.95 us  [shifted(): return lax.ppermute(x, axis, [(i, (i + by) % size) for i in range(size)])]
    another operation x5 -> x0, local copies, waits for them, and re-layouts: 2.69 us -> none  [the longest x2 1.81 us: per_device(): jnp.tile(dt_input, (1, copies))]
  transfers between devices with their start and end apart: 14 -> 22, of which waited for: 5 -> 7; matrix products, arithmetic and copies ran while one was open for 9% -> 6% of each run, Pallas kernels for 11% -> 23%
where the time goes in v3:
time: 139 us; the launch traced here: 138 us
  Pallas kernels  55.4 us (40%)
  starting transfers between devices  43.5 us (31%)
  waiting for transfers between devices  23.4 us (17%)
  other arithmetic  7.35 us (5%)
  local copies, waits for them, and re-layouts  7.02 us (5%)
    ppermute x6, starting transfers between devices, line_sums(): right[p] = lax.ppermute(go_right, 'tp', to_right[:s + 1])  28.7 us
    pallas_call x2, Pallas kernels, run_project(): pl.pallas_call(functools.partial(project_kernel, chunks, shares, (reqs, s...  24.4 us
    pallas_call x1, Pallas kernels, run_scan(): pl.pallas_call(functools.partial(scan_kernel, heads, slots, reqs), grid_s...  13.7 us
    ppermute x6, waiting for transfers between devices, line_sums(): right[p] = lax.ppermute(go_right, 'tp', to_right[:s + 1])  11.1 us
    ppermute x8, starting transfers between devices, shifted(): return lax.ppermute(x, axis, [(i, (i + by) % size) for i in range(size)])  8.95 us
    ppermute x8, waiting for transfers between devices, shifted(): return lax.ppermute(x, axis, [(i, (i + by) % size) for i in range(size)])  7.37 us
    ppermute x6, starting transfers between devices, line_sums(): left[p] = lax.ppermute(go_left, 'tp', to_left[size - 2 - s:])  5.33 us
    ppermute x6, waiting for transfers between devices, line_sums(): left[p] = lax.ppermute(go_left, 'tp', to_left[size - 2 - s:])  4.92 us
  transfers between devices with their start and end apart: 22, of which 7 were waited for; matrix products, arithmetic and copies ran while one was open for 6% of the time, Pallas kernels for 23%

profile of v3, /device:TPU:0, one launch (start us, length us, event | category | flops | bytes accessed | tf_op | source)
XLA Modules:
  0.0 137.7 jit_solution(17925980522477062609)
XLA Ops:
  1.1 1.3 concatenate.9.meta
  2.4 2.2 %pack.1 = (bf16[3,3072]{1,0:T(4,128)(2,1)}, bf16[3,3072]{1,0:T(4,128)(2,1)}, bf16[3,3072]{1,0:T(4,128)(2,1)}, bf16[3,3072]{1,0:T(4,128)(2,1)}) custom-call(s32[18]{0:T(128)} %concatenate.9.meta, bf16[3,2,2048]{2,1,0:T(2,128)(2,1)} %bitcast.18, bf16[3,2,1024]{2,1,0:T(2,128)(2,1)} %bitcast.19), custom_call_target="tpu_custom_call" | custom-call | flops 1000000 | bytes 262144 | tf_op jit(solution)/shard_map/pack/pallas_call | solution.py:85
  4.7 3.0 %collective-permute-start.3 = (bf16[3,3072]{1,0:T(4,128)(2,1)}, bf16[3,3072]{1,0:T(4,128)(2,1)S(1)}, u32[]{:S(2)}, u32[]{:S(2)}) collective-permute-start(bf16[3,3072]{1,0:T(4,128)(2,1)} %get-tuple-element.36), channel_id=1, source_target_pairs={{0,8},{4,12},{8,0},{12,4},{1,9},{5,13},{9,1},{13,5},{2,10},{6,14},... | collective-permute-start | bytes 55304 | tf_op jit(solution)/shard_map/ppermute | solution.py:612
  7.7 1.0 collective-permute-start.4
  8.7 1.4 copy-done
  10.1 4.2 %choose.1 = (bf16[1,2048,128]{2,1,0:T(8,128)(2,1)}, f32[8,128]{1,0:T(8,128)}) custom-call(s32[18]{0:T(128)} %concatenate.9.meta, f32[2,2048,128]{2,1,0:T(8,128)} %bitcast.14, f32[2,2048,128]{2,1,0:T(8,128)} %copy-done), custom_call_target="tpu_custom_call" | custom-call | flops 1000000 | bytes 2097152 | tf_op jit(solution)/shard_map/choose/pallas_call | solution.py:116
  15.2 13.7 %local_scan.1 = (f32[512,2048]{1,0:T(8,128)}, f32[2048,128]{1,0:T(8,128)}, bf16[512,128]{1,0:T(8,128)(2,1)}, bf16[512,128]{1,0:T(8,128)(2,1)}, bf16[16,128]{1,0:...) custom-call(s32[18]{0:T(128)} %concatenate.9.meta, bf16[3,3072]{1,0:T(4,128)(2,1)} %get-tuple-element.34.refs_0_, ...), custom_call_target="tpu_custom_call" | custom-call | flops 8000000000 | bytes 12582912 | tf_op jit(solution)/shard_map/local_scan/pallas_call | solution.py:299
  29.7 12.7 %project.2 = (bf16[256,1024]{1,0:T(8,128)(2,1)}, bf16[256,1024]{1,0:T(8,128)(2,1)}, bf16[256,1024]{1,0:T(8,128)(2,1)}, bf16[256,1024]{1,0:T(8,128)(2,1)}, f32[8,256]{1,0:T(8,128)}, /*index=5*/bf16[2048,128]{1,0:T(8,128)(2,1)}) custom-call(s32[18]{0:T(128)} %concatenate.9.meta, f32[2,2048,128]{2,1,0:T(8,128)} %bitcast.15, f32[2,2048,128]{2,1,0:T(8,128)} %copy-done, ...), custom_call_target="tpu_custom_call" | custom-call | flops 4294967296 | bytes 27262976 | tf_op jit(solution)/shard_map/project/pallas_call | solution.py:437
  42.5 11.7 %project.3 = (bf16[256,1024]{1,0:T(8,128)(2,1)}, bf16[256,1024]{1,0:T(8,128)(2,1)}, bf16[256,1024]{1,0:T(8,128)(2,1)}, bf16[256,1024]{1,0:T(8,128)(2,1)}, f32[8,256]{1,0:T(8,128)}) custom-call(s32[18]{0:T(128)} %concatenate.9.meta, bf16[2048,128]{1,0:T(8,128)(2,1)} %get-tuple-element.47.refs_0_.start_ref, f32[512,2048]{1,0:T(8,128)} %get-tuple-element.39.refs_3_.refs_1_, ...), custom_call_target="tpu_custom_call" | custom-call | flops 4294967296 | bytes 27262976 | tf_op jit(solution)/shard_map/project/pallas_call | solution.py:437
  54.8 3.6 %collective-permute-start.11 = (bf16[256,1024]{1,0:T(8,128)(2,1)}, bf16[256,1024]{1,0:T(8,128)(2,1)S(1)}, u32[]{:S(2)}, u32[]{:S(2)}) collective-permute-start(bf16[256,1024]{1,0:T(8,128)(2,1)} %get-tuple-element.53), channel_id=1, source_target_pairs={{0,1},{4,5},{8,9},{12,13},{16,17},{20,21},{24,25},{28,29}} | collective-permute-start | bytes 1572872 | tf_op jit(solution)/shard_map/ppermute | solution.py:487
  59.2 1.3 collective-permute-start.5
  60.5 4.8 %ending.1.refs_0_ = bf16[2432,128]{1,0:T(8,128)(2,1)} custom-call(s32[18]{0:T(128)} %concatenate.9.meta, f32[8,256]{1,0:T(8,128)} %get-tuple-element.55.mark_ref, f32[2048,128]{1,0:T(8,128)} %get-tuple-element.56.local_ref, bf16[2048,128]{1,0:T(8,128)(2,1)} %get-tuple-element.47.refs_0_.start_ref, bf16[16,128]{1,0:T(8,128)(2,1)} %get-tuple-element.57.total_ref, ...), custom_call_target="tpu_custom_call" | custom-call | flops 100000000 | bytes 6291456 | tf_op jit(solution)/shard_map/ending/pallas_call | solution.py:530
  65.3 1.5 %collective-permute-start.20 = (bf16[2432,128]{1,0:T(8,128)(2,1)}, bf16[2432,128]{1,0:T(8,128)(2,1)S(1)}, u32[]{:S(2)}, u32[]{:S(2)}) collective-permute-start(bf16[2432,128]{1,0:T(8,128)(2,1)} %ending.1.refs_0_), channel_id=1, source_target_pairs={{0,8},{4,12},{8,0},{12,4},{1,9},{5,13},{9,1},{13,5},{2,10},{6,14},... | collective-permute-start | bytes 1867784 | tf_op jit(solution)/shard_map/ppermute | solution.py:612
  66.8 4.3 %collective-permute-done.11 = bf16[256,1024]{1,0:T(8,128)(2,1)S(1)} collective-permute-done((bf16[256,1024]{1,0:T(8,128)(2,1)}, bf16[256,1024]{1,0:T(8,128)(2,1)S(1)}, u32[]{:S(2)}, u32[]{:S(2)}) %collective-permute-start.11) | collective-permute-done | bytes 524320 | tf_op jit(solution)/shard_map/ppermute | solution.py:487
  71.5 4.5 %collective-permute-start.12 = (bf16[256,1024]{1,0:T(8,128)(2,1)S(1)}, bf16[256,1024]{1,0:T(8,128)(2,1)S(1)}, u32[]{:S(2)}, u32[]{:S(2)}) collective-permute-start(bf16[256,1024]{1,0:T(8,128)(2,1)S(1)} %get-tuple-element.64), channel_id=1, source_target_pairs={{0,1},{1,2},{4,5},{5,6},{8,9},{9,10},{12,13},{13,14},{16,17},{17,1... | collective-permute-start | bytes 1572872 | tf_op jit(solution)/shard_map/ppermute | solution.py:487
  77.4 4.9 %collective-permute-done.5 = bf16[256,1024]{1,0:T(8,128)(2,1)S(1)} collective-permute-done((bf16[256,1024]{1,0:T(8,128)(2,1)S(1)}, bf16[256,1024]{1,0:T(8,128)(2,1)S(1)}, u32[]{:S(2)}, u32[]{:S(2)}) %collective-permute-start.5) | collective-permute-done | bytes 524320 | tf_op jit(solution)/shard_map/ppermute | solution.py:487
  83.0 1.1 fusion.1
  84.1 5.1 %collective-permute-start.7 = (bf16[256,1024]{1,0:T(8,128)(2,1)}, bf16[256,1024]{1,0:T(8,128)(2,1)S(1)}, u32[]{:S(2)}, u32[]{:S(2)}) collective-permute-start(bf16[256,1024]{1,0:T(8,128)(2,1)} %get-tuple-element.62), channel_id=1, source_target_pairs={{0,1},{1,2},{4,5},{5,6},{8,9},{9,10},{12,13},{13,14},{16,17},{17,1... | collective-permute-start | bytes 1572872 | tf_op jit(solution)/shard_map/ppermute | solution.py:487
  90.1 2.9 %route.1 = bf16[2432,128]{1,0:T(8,128)(2,1)} custom-call(s32[18]{0:T(128)} %concatenate.9.meta, bf16[2432,128]{1,0:T(8,128)(2,1)} %ending.1.refs_0_, bf16[2432,128]{1,0:T(8,128)(2,1)} %copy-done.1), custom_call_target="tpu_custom_call" | custom-call | flops 1000000 | bytes 2097152 | tf_op jit(solution)/shard_map/route/pallas_call | solution.py:556
  93.7 9.7 %collective-permute-start.13 = (bf16[256,1024]{1,0:T(8,128)(2,1)S(1)}, bf16[256,1024]{1,0:T(8,128)(2,1)S(1)}, u32[]{:S(2)}, u32[]{:S(2)}) collective-permute-start(bf16[256,1024]{1,0:T(8,128)(2,1)S(1)} %add_convert_fusion.1), channel_id=1, source_target_pairs={{0,1},{1,2},{2,3},{4,5},{5,6},{6,7},{8,9},{9,10},{10,11},{12,13},{... | collective-permute-start | bytes 1572872 | tf_op jit(solution)/shard_map/ppermute | solution.py:487
  103.6 1.3 collective-permute-done.7
  104.9 1.3 collective-permute-start.16
  106.2 1.0 add_convert_fusion.3
  107.2 3.1 %collective-permute-start.17 = (f32[512]{0:T(512)S(1)}, f32[512]{0:T(512)S(1)}, u32[]{:S(2)}, u32[]{:S(2)}) collective-permute-start(f32[512]{0:T(512)S(1)} %pad_maximum_fusion), channel_id=1, source_target_pairs={{0,1},{1,2},{2,3},{3,0},{4,5},{5,6},{6,7},{7,4},{8,9},{9,10},{10,1... | collective-permute-start | bytes 6152 | tf_op jit(solution)/shard_map/ppermute | solution.py:612
  110.2 1.0 add_convert_fusion.2
  111.2 7.4 %collective-permute-done.19 = f32[512]{0:T(512)S(1)} collective-permute-done((f32[512]{0:T(512)S(1)}, f32[512]{0:T(512)S(1)}, u32[]{:S(2)}, u32[]{:S(2)}) %collective-permute-start.19) | collective-permute-done | bytes 2080 | tf_op jit(solution)/shard_map/ppermute | solution.py:612
  118.6 4.4 %collective-permute-start.8 = (bf16[256,1024]{1,0:T(8,128)(2,1)}, bf16[256,1024]{1,0:T(8,128)(2,1)}, u32[]{:S(2)}, u32[]{:S(2)}) collective-permute-start(bf16[256,1024]{1,0:T(8,128)(2,1)} %add_convert_fusion.3), channel_id=1, source_target_pairs={{0,1},{1,2},{2,3},{4,5},{5,6},{6,7},{8,9},{9,10},{10,11},{12,13},{... | collective-permute-start | bytes 1572872 | tf_op jit(solution)/shard_map/ppermute | solution.py:487
  123.0 1.3 collective-permute-start.10
  126.4 3.3 %land.1 = (f32[2048,128]{1,0:T(8,128)}, bf16[3,2048]{1,0:T(4,128)(2,1)}, bf16[3,1024]{1,0:T(4,128)(2,1)}) custom-call(s32[18]{0:T(128)} %concatenate.9.meta, bf16[2432,128]{1,0:T(8,128)(2,1)} %ending.1.refs_0_, bf16[2432,128]{1,0:T(8,128)(2,1)} %copy-done.1, bf16[2432,128]{1,0:T(8,128)(2,1)} %copy-done.2), custom_call_target="tpu_custom_call" | custom-call | flops 1000000 | bytes 3145728 | tf_op jit(solution)/shard_map/land/pallas_call | solution.py:596
  130.2 4.9 %collective-permute-done.10 = bf16[256,1024]{1,0:T(8,128)(2,1)} collective-permute-done((bf16[256,1024]{1,0:T(8,128)(2,1)}, bf16[256,1024]{1,0:T(8,128)(2,1)}, u32[]{:S(2)}, u32[]{:S(2)}) %collective-permute-start.10) | collective-permute-done | bytes 524320 | tf_op jit(solution)/shard_map/ppermute | solution.py:488
  135.1 1.5 %convert_add_fusion.5 = f32[256,1024]{1,0:T(8,128)S(1)} fusion(bf16[256,1024]{1,0:T(8,128)(2,1)} %collective-permute-done.10, bf16[256,1024]{1,0:T(8,128)(2,1)} %collective-permute-done.8, bf16[256,1024]{1,0:T(8,128)(2,1)S(1)} %copy-done.4), kind=kLoop, calls=%fused_computation.13 | loop fusion | flops 1310720 | bytes 2621440 | tf_op jit(solution)/shard_map/add | solution.py:490
  136.6 1.1 fusion
  (67 shorter events, 10.5 us)
Async XLA Ops:
  0.6 8.0 %collective-permute-start = (f32[2,2048,128]{2,1,0:T(8,128)}, f32[2,2048,128]{2,1,0:T(8,128)S(1)}, u32[]{:S(2)}, u32[]{:S(2)}) collective-permute-start(f32[2,2048,128]{2,1,0:T(8,128)} %bitcast.13), channel_id=1, source_target_pairs={{0,4},{4,0},{8,12},{12,8},{1,5},{5,1},{9,13},{13,9},{2,6},{6,2},{1... | collective-permute-start | bytes 6291464 | tf_op jit(solution)/shard_map/ppermute | solution.py:616
  4.7 9.9 %collective-permute-start.2 = (bf16[3,3072]{1,0:T(4,128)(2,1)}, bf16[3,3072]{1,0:T(4,128)(2,1)S(1)}, u32[]{:S(2)}, u32[]{:S(2)}) collective-permute-start(bf16[3,3072]{1,0:T(4,128)(2,1)} %get-tuple-element.35), channel_id=1, source_target_pairs={{0,4},{4,8},{8,12},{12,0},{1,5},{5,9},{9,13},{13,1},{2,6},{6,10},{... | collective-permute-start | bytes 55304 | tf_op jit(solution)/shard_map/ppermute | solution.py:612
  4.7 9.9 %collective-permute-start.3 = (bf16[3,3072]{1,0:T(4,128)(2,1)}, bf16[3,3072]{1,0:T(4,128)(2,1)S(1)}, u32[]{:S(2)}, u32[]{:S(2)}) collective-permute-start(bf16[3,3072]{1,0:T(4,128)(2,1)} %get-tuple-element.36), channel_id=1, source_target_pairs={{0,8},{4,12},{8,0},{12,4},{1,9},{5,13},{9,1},{13,5},{2,10},{6,14},... | collective-permute-start | bytes 55304 | tf_op jit(solution)/shard_map/ppermute | solution.py:612
  7.7 6.9 %collective-permute-start.4 = (bf16[3,3072]{1,0:T(4,128)(2,1)}, bf16[3,3072]{1,0:T(4,128)(2,1)S(1)}, u32[]{:S(2)}, u32[]{:S(2)}) collective-permute-start(bf16[3,3072]{1,0:T(4,128)(2,1)} %get-tuple-element.37), channel_id=1, source_target_pairs={{0,12},{4,0},{8,4},{12,8},{1,13},{5,1},{9,5},{13,9},{2,14},{6,2},{... | collective-permute-start | bytes 55304 | tf_op jit(solution)/shard_map/ppermute | solution.py:612
  8.7 1.4 %copy-start = (f32[2,2048,128]{2,1,0:T(8,128)}, f32[2,2048,128]{2,1,0:T(8,128)S(1)}, u32[]{:S(2)}) copy-start(f32[2,2048,128]{2,1,0:T(8,128)S(1)} %collective-permute-done.mate_ref.refs_1_) | copy-start | bytes 6291460
  14.2 14.7 %collective-permute-start.1 = (bf16[1,2048,128]{2,1,0:T(8,128)(2,1)}, bf16[1,2048,128]{2,1,0:T(8,128)(2,1)S(1)}, u32[]{:S(2)}, u32[]{:S(2)}) collective-permute-start(bf16[1,2048,128]{2,1,0:T(8,128)(2,1)} %get-tuple-element.33), channel_id=1, source_target_pairs={{0,8},{4,12},{8,0},{12,4},{1,9},{5,13},{9,1},{13,5},{2,10},{6,14},... | collective-permute-start | bytes 1572872 | tf_op jit(solution)/shard_map/ppermute | solution.py:612
  42.4 16.0 %copy-start.7 = (bf16[256,1024]{1,0:T(8,128)(2,1)S(1)}, bf16[256,1024]{1,0:T(8,128)(2,1)}, u32[]{:S(2)}) copy-start(bf16[256,1024]{1,0:T(8,128)(2,1)} %get-tuple-element.44) | copy-start | bytes 1572868
  42.5 16.7 %copy-start.6 = (bf16[256,1024]{1,0:T(8,128)(2,1)S(1)}, bf16[256,1024]{1,0:T(8,128)(2,1)}, u32[]{:S(2)}) copy-start(bf16[256,1024]{1,0:T(8,128)(2,1)} %get-tuple-element.46) | copy-start | bytes 1572868
  54.1 12.7 %collective-permute-start.14 = (bf16[256,1024]{1,0:T(8,128)(2,1)}, bf16[256,1024]{1,0:T(8,128)(2,1)S(1)}, u32[]{:S(2)}, u32[]{:S(2)}) collective-permute-start(bf16[256,1024]{1,0:T(8,128)(2,1)} %get-tuple-element.51), channel_id=1, source_target_pairs={{3,2},{7,6},{11,10},{15,14},{19,18},{23,22},{27,26},{31,30}} | collective-permute-start | bytes 1572872 | tf_op jit(solution)/shard_map/ppermute | solution.py:488
  54.8 16.3 %collective-permute-start.11 = (bf16[256,1024]{1,0:T(8,128)(2,1)}, bf16[256,1024]{1,0:T(8,128)(2,1)S(1)}, u32[]{:S(2)}, u32[]{:S(2)}) collective-permute-start(bf16[256,1024]{1,0:T(8,128)(2,1)} %get-tuple-element.53), channel_id=1, source_target_pairs={{0,1},{4,5},{8,9},{12,13},{16,17},{20,21},{24,25},{28,29}} | collective-permute-start | bytes 1572872 | tf_op jit(solution)/shard_map/ppermute | solution.py:487
  58.5 18.9 %collective-permute-start.6 = (bf16[256,1024]{1,0:T(8,128)(2,1)S(1)}, bf16[256,1024]{1,0:T(8,128)(2,1)S(1)}, u32[]{:S(2)}, u32[]{:S(2)}) collective-permute-start(bf16[256,1024]{1,0:T(8,128)(2,1)S(1)} %copy-done.7), channel_id=1, source_target_pairs={{3,2},{7,6},{11,10},{15,14},{19,18},{23,22},{27,26},{31,30}} | collective-permute-start | bytes 1572872 | tf_op jit(solution)/shard_map/ppermute | solution.py:488
  59.2 23.0 %collective-permute-start.5 = (bf16[256,1024]{1,0:T(8,128)(2,1)S(1)}, bf16[256,1024]{1,0:T(8,128)(2,1)S(1)}, u32[]{:S(2)}, u32[]{:S(2)}) collective-permute-start(bf16[256,1024]{1,0:T(8,128)(2,1)S(1)} %copy-done.6), channel_id=1, source_target_pairs={{0,1},{4,5},{8,9},{12,13},{16,17},{20,21},{24,25},{28,29}} | collective-permute-start | bytes 1572872 | tf_op jit(solution)/shard_map/ppermute | solution.py:487
  60.5 10.6 %copy-start.11 = (bf16[256,1024]{1,0:T(8,128)(2,1)S(1)}, bf16[256,1024]{1,0:T(8,128)(2,1)}, u32[]{:S(2)}) copy-start(bf16[256,1024]{1,0:T(8,128)(2,1)} %get-tuple-element.52) | copy-start | bytes 1572868
  65.3 17.6 %copy-start.10 = (bf16[256,1024]{1,0:T(8,128)(2,1)S(1)}, bf16[256,1024]{1,0:T(8,128)(2,1)}, u32[]{:S(2)}) copy-start(bf16[256,1024]{1,0:T(8,128)(2,1)} %get-tuple-element.45) | copy-start | bytes 1572868
  65.3 23.9 %collective-permute-start.20 = (bf16[2432,128]{1,0:T(8,128)(2,1)}, bf16[2432,128]{1,0:T(8,128)(2,1)S(1)}, u32[]{:S(2)}, u32[]{:S(2)}) collective-permute-start(bf16[2432,128]{1,0:T(8,128)(2,1)} %ending.1.refs_0_), channel_id=1, source_target_pairs={{0,8},{4,12},{8,0},{12,4},{1,9},{5,13},{9,1},{13,5},{2,10},{6,14},... | collective-permute-start | bytes 1867784 | tf_op jit(solution)/shard_map/ppermute | solution.py:612
  71.5 22.0 %collective-permute-start.12 = (bf16[256,1024]{1,0:T(8,128)(2,1)S(1)}, bf16[256,1024]{1,0:T(8,128)(2,1)S(1)}, u32[]{:S(2)}, u32[]{:S(2)}) collective-permute-start(bf16[256,1024]{1,0:T(8,128)(2,1)S(1)} %get-tuple-element.64), channel_id=1, source_target_pairs={{0,1},{1,2},{4,5},{5,6},{8,9},{9,10},{12,13},{13,14},{16,17},{17,1... | collective-permute-start | bytes 1572872 | tf_op jit(solution)/shard_map/ppermute | solution.py:487
  77.4 29.8 %collective-permute-start.18 = (f32[512]{0:T(512)S(1)}, f32[512]{0:T(512)S(1)}, u32[]{:S(2)}, u32[]{:S(2)}) collective-permute-start(f32[512]{0:T(512)S(1)} %pad_maximum_fusion), channel_id=1, source_target_pairs={{0,2},{1,3},{2,0},{3,1},{4,6},{5,7},{6,4},{7,5},{8,10},{9,11},{10,... | collective-permute-start | bytes 6152 | tf_op jit(solution)/shard_map/ppermute | solution.py:612
  82.2 11.5 %collective-permute-start.15 = (bf16[256,1024]{1,0:T(8,128)(2,1)S(1)}, bf16[256,1024]{1,0:T(8,128)(2,1)S(1)}, u32[]{:S(2)}, u32[]{:S(2)}) collective-permute-start(bf16[256,1024]{1,0:T(8,128)(2,1)S(1)} %get-tuple-element.65), channel_id=1, source_target_pairs={{2,1},{3,2},{6,5},{7,6},{10,9},{11,10},{14,13},{15,14},{18,17},{19... | collective-permute-start | bytes 1572872 | tf_op jit(solution)/shard_map/ppermute | solution.py:488
  82.9 10.5 %copy-start.9 = (bf16[256,1024]{1,0:T(8,128)(2,1)S(1)}, bf16[256,1024]{1,0:T(8,128)(2,1)}, u32[]{:S(2)}) copy-start(bf16[256,1024]{1,0:T(8,128)(2,1)} %get-tuple-element.51) | copy-start | bytes 1572868
  84.1 19.3 %copy-start.8 = (bf16[256,1024]{1,0:T(8,128)(2,1)S(1)}, bf16[256,1024]{1,0:T(8,128)(2,1)}, u32[]{:S(2)}) copy-start(bf16[256,1024]{1,0:T(8,128)(2,1)} %get-tuple-element.53) | copy-start | bytes 1572868
  84.1 20.8 %collective-permute-start.7 = (bf16[256,1024]{1,0:T(8,128)(2,1)}, bf16[256,1024]{1,0:T(8,128)(2,1)S(1)}, u32[]{:S(2)}, u32[]{:S(2)}) collective-permute-start(bf16[256,1024]{1,0:T(8,128)(2,1)} %get-tuple-element.62), channel_id=1, source_target_pairs={{0,1},{1,2},{4,5},{5,6},{8,9},{9,10},{12,13},{13,14},{16,17},{17,1... | collective-permute-start | bytes 1572872 | tf_op jit(solution)/shard_map/ppermute | solution.py:487
  89.3 17.9 %collective-permute-start.9 = (bf16[256,1024]{1,0:T(8,128)(2,1)S(1)}, bf16[256,1024]{1,0:T(8,128)(2,1)S(1)}, u32[]{:S(2)}, u32[]{:S(2)}) collective-permute-start(bf16[256,1024]{1,0:T(8,128)(2,1)S(1)} %get-tuple-element.63), channel_id=1, source_target_pairs={{2,1},{3,2},{6,5},{7,6},{10,9},{11,10},{14,13},{15,14},{18,17},{19... | collective-permute-start | bytes 1572872 | tf_op jit(solution)/shard_map/ppermute | solution.py:488
  93.5 32.1 %collective-permute-start.21 = (bf16[2432,128]{1,0:T(8,128)(2,1)}, bf16[2432,128]{1,0:T(8,128)(2,1)S(1)}, u32[]{:S(2)}, u32[]{:S(2)}) collective-permute-start(bf16[2432,128]{1,0:T(8,128)(2,1)} %route.1), channel_id=1, source_target_pairs={{0,4},{4,0},{8,12},{12,8},{1,5},{5,1},{9,13},{13,9},{2,6},{6,2},{1... | collective-permute-start | bytes 1867784 | tf_op jit(solution)/shard_map/ppermute | solution.py:616
  93.7 30.6 %copy-start.12 = (s32[4]{0:T(128)S(1)}, s32[4]{0:T(128)}, u32[]{:S(2)}) copy-start(s32[4]{0:T(128)} %param.33) | copy-start | bytes 52
  93.7 36.0 %collective-permute-start.13 = (bf16[256,1024]{1,0:T(8,128)(2,1)S(1)}, bf16[256,1024]{1,0:T(8,128)(2,1)S(1)}, u32[]{:S(2)}, u32[]{:S(2)}) collective-permute-start(bf16[256,1024]{1,0:T(8,128)(2,1)S(1)} %add_convert_fusion.1), channel_id=1, source_target_pairs={{0,1},{1,2},{2,3},{4,5},{5,6},{6,7},{8,9},{9,10},{10,11},{12,13},{... | collective-permute-start | bytes 1572872 | tf_op jit(solution)/shard_map/ppermute | solution.py:487
  104.9 24.9 %collective-permute-start.16 = (bf16[256,1024]{1,0:T(8,128)(2,1)S(1)}, bf16[256,1024]{1,0:T(8,128)(2,1)S(1)}, u32[]{:S(2)}, u32[]{:S(2)}) collective-permute-start(bf16[256,1024]{1,0:T(8,128)(2,1)S(1)} %add_convert_fusion), channel_id=1, source_target_pairs={{1,0},{2,1},{3,2},{5,4},{6,5},{7,6},{9,8},{10,9},{11,10},{13,12},{... | collective-permute-start | bytes 1572872 | tf_op jit(solution)/shard_map/ppermute | solution.py:488
  107.2 22.6 %copy-start.5 = (bf16[256,1024]{1,0:T(8,128)(2,1)S(1)}, bf16[256,1024]{1,0:T(8,128)(2,1)}, u32[]{:S(2)}) copy-start(bf16[256,1024]{1,0:T(8,128)(2,1)} %get-tuple-element.48) | copy-start | bytes 1572868
  107.2 11.4 %collective-permute-start.19 = (f32[512]{0:T(512)S(1)}, f32[512]{0:T(512)S(1)}, u32[]{:S(2)}, u32[]{:S(2)}) collective-permute-start(f32[512]{0:T(512)S(1)} %pad_maximum_fusion), channel_id=1, source_target_pairs={{0,3},{1,0},{2,1},{3,2},{4,7},{5,4},{6,5},{7,6},{8,11},{9,8},{10,9... | collective-permute-start | bytes 6152 | tf_op jit(solution)/shard_map/ppermute | solution.py:612
  107.2 15.8 %collective-permute-start.17 = (f32[512]{0:T(512)S(1)}, f32[512]{0:T(512)S(1)}, u32[]{:S(2)}, u32[]{:S(2)}) collective-permute-start(f32[512]{0:T(512)S(1)} %pad_maximum_fusion), channel_id=1, source_target_pairs={{0,1},{1,2},{2,3},{3,0},{4,5},{5,6},{6,7},{7,4},{8,9},{9,10},{10,1... | collective-permute-start | bytes 6152 | tf_op jit(solution)/shard_map/ppermute | solution.py:612
  118.6 11.6 %collective-permute-start.8 = (bf16[256,1024]{1,0:T(8,128)(2,1)}, bf16[256,1024]{1,0:T(8,128)(2,1)}, u32[]{:S(2)}, u32[]{:S(2)}) collective-permute-start(bf16[256,1024]{1,0:T(8,128)(2,1)} %add_convert_fusion.3), channel_id=1, source_target_pairs={{0,1},{1,2},{2,3},{4,5},{5,6},{6,7},{8,9},{9,10},{10,11},{12,13},{... | collective-permute-start | bytes 1572872 | tf_op jit(solution)/shard_map/ppermute | solution.py:487
  123.0 12.1 %collective-permute-start.10 = (bf16[256,1024]{1,0:T(8,128)(2,1)}, bf16[256,1024]{1,0:T(8,128)(2,1)}, u32[]{:S(2)}, u32[]{:S(2)}) collective-permute-start(bf16[256,1024]{1,0:T(8,128)(2,1)} %add_convert_fusion.2), channel_id=1, source_target_pairs={{1,0},{2,1},{3,2},{5,4},{6,5},{7,6},{9,8},{10,9},{11,10},{13,12},{... | collective-permute-start | bytes 1572872 | tf_op jit(solution)/shard_map/ppermute | solution.py:488
  125.6 9.5 %copy-start.4 = (bf16[256,1024]{1,0:T(8,128)(2,1)S(1)}, bf16[256,1024]{1,0:T(8,128)(2,1)}, u32[]{:S(2)}) copy-start(bf16[256,1024]{1,0:T(8,128)(2,1)} %get-tuple-element.43) | copy-start | bytes 1572868
  (6 other events, 4.3 us)

commit v4 on v3

--- a/solution.py
+++ b/solution.py
@@ -21,7 +21,6 @@
 WIDE = 512
 SCAN_WIDE = 1024
 PIECES = (2, 2)
-VMEM_LIMIT = 56 * 2**20
 
 F32 = jnp.float32
 BF16 = jnp.bfloat16
@@ -94,7 +93,7 @@
             out_specs=[pl.BlockSpec((taps, inner + BCW), lambda i, m: (0, 0))] * reqs,
         ),
         out_shape=[jax.ShapeDtypeStruct((taps, inner + BCW), BF16)] * reqs,
-        compiler_params=pltpu.CompilerParams(vmem_limit_bytes=VMEM_LIMIT),
+        compiler_params=pltpu.CompilerParams(vmem_limit_bytes=8 * 2**20),
         cost_estimate=pl.CostEstimate(flops=10**6, bytes_accessed=2**18, transcendentals=0),
         name="pack",
     )(meta, px, pb)
@@ -131,7 +130,7 @@
             jax.ShapeDtypeStruct((reqs // 2 - 1, inner, STATE), BF16),
             jax.ShapeDtypeStruct((8, LANES), F32),
         ],
-        compiler_params=pltpu.CompilerParams(vmem_limit_bytes=VMEM_LIMIT),
+        compiler_params=pltpu.CompilerParams(vmem_limit_bytes=8 * 2**20),
         cost_estimate=pl.CostEstimate(flops=10**6, bytes_accessed=2 * 2**20, transcendentals=0),
         name="choose",
     )(meta, mine, mate)
@@ -324,7 +323,7 @@
             jax.ShapeDtypeStruct((LANES, inner), BF16),
         ],
         compiler_params=pltpu.CompilerParams(
-            dimension_semantics=("arbitrary", "arbitrary"), vmem_limit_bytes=VMEM_LIMIT
+            dimension_semantics=("arbitrary", "arbitrary"), vmem_limit_bytes=24 * 2**20
         ),
         cost_estimate=pl.CostEstimate(
             flops=8 * 10**9, bytes_accessed=12 * 2**20, transcendentals=SUF * inner
@@ -458,7 +457,7 @@
         ),
         out_shape=out_shape,
         compiler_params=pltpu.CompilerParams(
-            dimension_semantics=("arbitrary",), vmem_limit_bytes=VMEM_LIMIT
+            dimension_semantics=("arbitrary",), vmem_limit_bytes=36 * 2**20
         ),
         cost_estimate=pl.CostEstimate(
             flops=2 * count * inner * width,
@@ -469,24 +468,25 @@
     )(meta, *states, y, gate, cmap, reach, gain, pick, weight)
 
 
-def line_sums(parts, size):
+def line_sums(parts, mark, size):
     to_right = [(i, i + 1) for i in range(size - 1)]
     to_left = [(i + 1, i) for i in range(size - 1)]
     add = lambda a, b: (a.astype(F32) + b.astype(F32)).astype(BF16)
     right = [None] * len(parts)
     left = [None] * len(parts)
     for s in range(size - 1):
-        for p, part in enumerate(parts):
+        for p in range(len(parts)):
+            part = parts[p]
             go_right, go_left = part[size - 1 - s], part[s + 1]
             if s:
-                if p + 1 < len(parts) and s == 1:
-                    right[p], left[p], _ = lax.optimization_barrier(
-                        (right[p], left[p], parts[p + 1][0])
-                    )
                 go_right, go_left = add(go_right, right[p]), add(go_left, left[p])
             right[p] = lax.ppermute(go_right, "tp", to_right[: s + 1])
             left[p] = lax.ppermute(go_left, "tp", to_left[size - 2 - s :])
-    return [
+            if s == 0 and p + 1 < len(parts):
+                right[p], left[p], parts[p + 1], mark = lax.optimization_barrier(
+                    (right[p], left[p], parts[p + 1], mark)
+                )
+    return mark, [
         part[0].astype(F32) + r.astype(F32) + l.astype(F32)
         for part, r, l in zip(parts, right, left)
     ]
@@ -536,7 +536,7 @@
             out_specs=pl.BlockSpec((rows, LANES), lambda i, m: (0, 0)),
         ),
         out_shape=jax.ShapeDtypeStruct((rows, LANES), BF16),
-        compiler_params=pltpu.CompilerParams(vmem_limit_bytes=VMEM_LIMIT),
+        compiler_params=pltpu.CompilerParams(vmem_limit_bytes=24 * 2**20),
         cost_estimate=pl.CostEstimate(flops=10**8, bytes_accessed=6 * 2**20, transcendentals=0),
         name="ending",
     )(meta, *operands)
@@ -562,7 +562,7 @@
             out_specs=pl.BlockSpec(shape, lambda i, m: (0, 0)),
         ),
         out_shape=jax.ShapeDtypeStruct(shape, BF16),
-        compiler_params=pltpu.CompilerParams(vmem_limit_bytes=VMEM_LIMIT),
+        compiler_params=pltpu.CompilerParams(vmem_limit_bytes=12 * 2**20),
         cost_estimate=pl.CostEstimate(flops=10**6, bytes_accessed=2 * 2**20, transcendentals=0),
         name="route",
     )(meta, *ends)
@@ -602,7 +602,7 @@
             out_specs=[pl.BlockSpec(o, lambda i, m: (0, 0)) for o in outs],
         ),
         out_shape=[jax.ShapeDtypeStruct(o, t) for o, t in zip(outs, (F32, BF16, BF16))],
-        compiler_params=pltpu.CompilerParams(vmem_limit_bytes=VMEM_LIMIT),
+        compiler_params=pltpu.CompilerParams(vmem_limit_bytes=16 * 2**20),
         cost_estimate=pl.CostEstimate(flops=10**6, bytes_accessed=3 * 2**20, transcendentals=0),
         name="land",
     )(meta, *ends, crossed)
@@ -694,12 +694,13 @@
             num_req,
         )
         first += chunks
-        parts.append(result[:num_tp])
+        parts.append(tuple(result[:num_tp]))
         squares.append(result[num_tp][0])
         if len(states) > 1:
             start = result[num_tp + 1]
             states = [start]
-    summed = jnp.concatenate(line_sums(parts, num_tp), axis=0)
+    mark, summed = line_sums(parts, result[num_tp], num_tp)
+    summed = jnp.concatenate(summed, axis=0)
 
     my_len = suffix_len[me]
     square = jnp.concatenate(squares)
@@ -711,7 +712,7 @@
     mixed = (summed * scale[:, None]).astype(BF16)
 
     end = run_ending(
-        meta, result[num_tp], local_final, start, total, pick, start_conv, ssm_input, bc_input, num_req
+        meta, mark, local_final, start, total, pick, start_conv, ssm_input, bc_input, num_req
     )
     ends = [end] + [shifted(end, "req", num_req, by) for by in range(2, num_req, 2)]
     crossed = swap_core(run_route(meta, ends, num_req), num_req)

time: 139 us -> 119 us (0.86)
  Pallas kernels: 55.4 us -> 32.5 us
  waiting for transfers between devices: 23.4 us -> 29.8 us
  starting transfers between devices: 43.5 us -> 39.7 us
  other arithmetic: 7.35 us -> 9.98 us
    ppermute x6, waiting for transfers between devices: 11.1 us -> 22.4 us  [line_sums(): right[p] = lax.ppermute(go_right, 'tp', to_right[:s + 1])]
    pallas_call x2, Pallas kernels: 24.4 us -> 15.9 us  [run_project(): pl.pallas_call(functools.partial(project_kernel, chunks, shares, (reqs, s...]
    ppermute x6, starting transfers between devices: 28.7 us -> 21.7 us  [line_sums(): right[p] = lax.ppermute(go_right, 'tp', to_right[:s + 1])]
    ppermute x8, waiting for transfers between devices: 7.37 us -> 2.39 us  [shifted(): return lax.ppermute(x, axis, [(i, (i + by) % size) for i in range(size)])]
    pallas_call x1, Pallas kernels: 4.76 us -> 1.17 us  [run_ending(): pl.pallas_call(functools.partial(ending_kernel, reqs), grid_spec=pltpu.Pr...]
    pallas_call x1, Pallas kernels: 4.15 us -> 0.75 us  [run_choose(): pl.pallas_call(functools.partial(choose_kernel, reqs, slots), grid_spec=p...]
    ppermute x8, starting transfers between devices: 8.95 us -> 12.1 us  [shifted(): return lax.ppermute(x, axis, [(i, (i + by) % size) for i in range(size)])]
    pallas_call x1, Pallas kernels: 13.7 us -> 11.4 us  [run_scan(): pl.pallas_call(functools.partial(scan_kernel, heads, slots, reqs), grid_s...]
  transfers between devices with their start and end apart: 22 -> 22, of which waited for: 7 -> 8; matrix products, arithmetic and copies ran while one was open for 6% -> 8% of each run, Pallas kernels for 23% -> 21%
where the time goes in v4:
time: 119 us; the launch traced here: 118 us
  starting transfers between devices  39.7 us (33%)
  Pallas kernels  32.5 us (27%)
  waiting for transfers between devices  29.8 us (25%)
  other arithmetic  9.98 us (8%)
  local copies, waits for them, and re-layouts  5.63 us (5%)
    ppermute x6, waiting for transfers between devices, line_sums(): right[p] = lax.ppermute(go_right, 'tp', to_right[:s + 1])  22.4 us
    ppermute x6, starting transfers between devices, line_sums(): right[p] = lax.ppermute(go_right, 'tp', to_right[:s + 1])  21.7 us
    pallas_call x2, Pallas kernels, run_project(): pl.pallas_call(functools.partial(project_kernel, chunks, shares, (reqs, s...  15.9 us
    ppermute x8, starting transfers between devices, shifted(): return lax.ppermute(x, axis, [(i, (i + by) % size) for i in range(size)])  12.1 us
    pallas_call x1, Pallas kernels, run_scan(): pl.pallas_call(functools.partial(scan_kernel, heads, slots, reqs), grid_s...  11.4 us
    ppermute x6, starting transfers between devices, line_sums(): left[p] = lax.ppermute(go_left, 'tp', to_left[size - 2 - s:])  5.31 us
    ppermute x6, waiting for transfers between devices, line_sums(): left[p] = lax.ppermute(go_left, 'tp', to_left[size - 2 - s:])  4.93 us
    convert_element_type x6, other arithmetic, line_sums(): add = lambda a, b: (a.astype(F32) + b.astype(F32)).astype(BF16)  4.58 us
  transfers between devices with their start and end apart: 22, of which 8 were waited for; matrix products, arithmetic and copies ran while one was open for 8% of the time, Pallas kernels for 21%

profile of v4, /device:TPU:0, one launch (start us, length us, event | category | flops | bytes accessed | tf_op | source)
XLA Modules:
  0.0 118.4 jit_solution(17376904947399517385)
XLA Ops:
  4.3 3.0 %collective-permute-start.3 = (bf16[3,3072]{1,0:T(4,128)(2,1)S(1)}, bf16[3,3072]{1,0:T(4,128)(2,1)S(1)}, u32[]{:S(2)}, u32[]{:S(2)}) collective-permute-start(bf16[3,3072]{1,0:T(4,128)(2,1)S(1)} %get-tuple-element.41), channel_id=1, source_target_pairs={{0,8},{4,12},{8,0},{12,4},{1,9},{5,13},{9,1},{13,5},{2,10},{6,14},... | collective-permute-start | bytes 55304 | tf_op jit(solution)/shard_map/ppermute | solution.py:612
  8.2 1.6 %copy-done.1 = f32[2,32,64,128]{3,2,1,0:T(8,128)S(1)} copy-done((f32[2,32,64,128]{3,2,1,0:T(8,128)S(1)}, f32[2,32,64,128]{3,2,1,0:T(8,128)}, u32[]{:S(2)}) %copy-start.1) | copy-done | bytes 2097176
  11.7 11.4 %local_scan.1 = (f32[512,2048]{1,0:T(8,128)S(1)}, f32[2048,128]{1,0:T(8,128)S(1)}, bf16[512,128]{1,0:T(8,128)(2,1)S(1)}, bf16[512,128]{1,0:T(8,128)(2,1)S(1)}, b...) custom-call(s32[18]{0:T(128)S(1)} %concatenate.9.meta, ...), custom_call_target="tpu_custom_call" | custom-call | flops 8000000000 | bytes 12582912 | tf_op jit(solution)/shard_map/local_scan/pallas_call | solution.py:298
  24.1 8.0 %project.2 = (bf16[256,1024]{1,0:T(8,128)(2,1)S(1)}, bf16[256,1024]{1,0:T(8,128)(2,1)S(1)}, bf16[256,1024]{1,0:T(8,128)(2,1)S(1)}, bf16[256,1024]{1,0:T(8,128)(2...) custom-call(s32[18]{0:T(128)S(1)} %concatenate.9.meta, f32[2,2048,128]{2,1,0:T(8,128)S(1)} %bitcast.15, ...), custom_call_target="tpu_custom_call" | custom-call | flops 4294967296 | bytes 27262976 | tf_op jit(solution)/shard_map/project/pallas_call | solution.py:436
  32.7 3.5 %collective-permute-start.5 = (bf16[256,1024]{1,0:T(8,128)(2,1)S(1)}, bf16[256,1024]{1,0:T(8,128)(2,1)S(1)}, u32[]{:S(2)}, u32[]{:S(2)}) collective-permute-start(bf16[256,1024]{1,0:T(8,128)(2,1)S(1)} %get-tuple-element.51), channel_id=1, source_target_pairs={{0,1},{4,5},{8,9},{12,13},{16,17},{20,21},{24,25},{28,29}} | collective-permute-start | bytes 1572872 | tf_op jit(solution)/shard_map/ppermute | solution.py:483
  36.2 8.0 %project.3 = (bf16[256,1024]{1,0:T(8,128)(2,1)S(1)}, bf16[256,1024]{1,0:T(8,128)(2,1)S(1)}, bf16[256,1024]{1,0:T(8,128)(2,1)S(1)}, bf16[256,1024]{1,0:T(8,128)(2,1)S(1)}, f32[8,256]{1,0:T(8,128)S(1)}) custom-call(s32[18]{0:T(128)S(1)} %concatenate.9.meta, bf16[2048,128]{1,0:T(8,128)(2,1)S(1)} %get-tuple-element.52.refs_0_.start_ref, ...), custom_call_target="tpu_custom_call" | custom-call | flops 4294967296 | bytes 27262976 | tf_op jit(solution)/shard_map/project/pallas_call | solution.py:436
  44.2 2.0 %collective-permute-done.5 = bf16[256,1024]{1,0:T(8,128)(2,1)S(1)} collective-permute-done((bf16[256,1024]{1,0:T(8,128)(2,1)S(1)}, bf16[256,1024]{1,0:T(8,128)(2,1)S(1)}, u32[]{:S(2)}, u32[]{:S(2)}) %collective-permute-start.5) | collective-permute-done | bytes 524320 | tf_op jit(solution)/shard_map/ppermute | solution.py:483
  46.9 4.4 %collective-permute-start.11 = (bf16[256,1024]{1,0:T(8,128)(2,1)S(1)}, bf16[256,1024]{1,0:T(8,128)(2,1)S(1)}, u32[]{:S(2)}, u32[]{:S(2)}) collective-permute-start(bf16[256,1024]{1,0:T(8,128)(2,1)S(1)} %get-tuple-element.63), channel_id=1, source_target_pairs={{0,1},{4,5},{8,9},{12,13},{16,17},{20,21},{24,25},{28,29}} | collective-permute-start | bytes 1572872 | tf_op jit(solution)/shard_map/ppermute | solution.py:483
  51.7 1.3 %collective-permute-start.7 = (bf16[256,1024]{1,0:T(8,128)(2,1)S(1)}, bf16[256,1024]{1,0:T(8,128)(2,1)S(1)}, u32[]{:S(2)}, u32[]{:S(2)}) collective-permute-start(bf16[256,1024]{1,0:T(8,128)(2,1)S(1)} %get-tuple-element.72), channel_id=1, source_target_pairs={{0,1},{1,2},{4,5},{5,6},{8,9},{9,10},{12,13},{13,14},{16,17},{17,1... | collective-permute-start | bytes 1572872 | tf_op jit(solution)/shard_map/ppermute | solution.py:483
  53.1 3.2 %collective-permute-start.19 = (f32[512]{0:T(512)S(1)}, f32[512]{0:T(512)}, u32[]{:S(2)}, u32[]{:S(2)}) collective-permute-start(f32[512]{0:T(512)S(1)} %pad_maximum_fusion), channel_id=1, source_target_pairs={{0,3},{1,0},{2,1},{3,2},{4,7},{5,4},{6,5},{7,6},{8,11},{9,8},{10,9... | collective-permute-start | bytes 6152 | tf_op jit(solution)/shard_map/ppermute | solution.py:612
  56.3 1.2 ending.1.refs_0_
  58.1 5.5 %collective-permute-done.11 = bf16[256,1024]{1,0:T(8,128)(2,1)S(1)} collective-permute-done((bf16[256,1024]{1,0:T(8,128)(2,1)S(1)}, bf16[256,1024]{1,0:T(8,128)(2,1)S(1)}, u32[]{:S(2)}, u32[]{:S(2)}) %collective-permute-start.11) | collective-permute-done | bytes 524320 | tf_op jit(solution)/shard_map/ppermute | solution.py:483
  63.7 1.2 %collective-permute-start.20 = (bf16[2432,128]{1,0:T(8,128)(2,1)S(1)}, bf16[2432,128]{1,0:T(8,128)(2,1)S(1)}, u32[]{:S(2)}, u32[]{:S(2)}) collective-permute-start(bf16[2432,128]{1,0:T(8,128)(2,1)S(1)} %ending.1.refs_0_), channel_id=1, source_target_pairs={{0,8},{4,12},{8,0},{12,4},{1,9},{5,13},{9,1},{13,5},{2,10},{6,14},... | collective-permute-start | bytes 1867784 | tf_op jit(solution)/shard_map/ppermute | solution.py:612
  65.3 6.5 %collective-permute-done.7 = bf16[256,1024]{1,0:T(8,128)(2,1)S(1)} collective-permute-done((bf16[256,1024]{1,0:T(8,128)(2,1)S(1)}, bf16[256,1024]{1,0:T(8,128)(2,1)S(1)}, u32[]{:S(2)}, u32[]{:S(2)}) %collective-permute-start.7) | collective-permute-done | bytes 524320 | tf_op jit(solution)/shard_map/ppermute | solution.py:483
  71.7 4.4 %collective-permute-start.12 = (bf16[256,1024]{1,0:T(8,128)(2,1)S(1)}, bf16[256,1024]{1,0:T(8,128)(2,1)S(1)}, u32[]{:S(2)}, u32[]{:S(2)}) collective-permute-start(bf16[256,1024]{1,0:T(8,128)(2,1)S(1)} %get-tuple-element.74), channel_id=1, source_target_pairs={{0,1},{1,2},{4,5},{5,6},{8,9},{9,10},{12,13},{13,14},{16,17},{17,1... | collective-permute-start | bytes 1572872 | tf_op jit(solution)/shard_map/ppermute | solution.py:483
  76.1 1.0 add_convert_fusion.3
  78.8 3.3 %collective-permute-start.8 = (bf16[256,1024]{1,0:T(8,128)(2,1)}, bf16[256,1024]{1,0:T(8,128)(2,1)}, u32[]{:S(2)}, u32[]{:S(2)}) collective-permute-start(bf16[256,1024]{1,0:T(8,128)(2,1)} %add_convert_fusion.3), channel_id=1, source_target_pairs={{0,1},{1,2},{2,3},{4,5},{5,6},{6,7},{8,9},{9,10},{10,11},{12,13},{... | collective-permute-start | bytes 1572872 | tf_op jit(solution)/shard_map/ppermute | solution.py:483
  82.8 5.6 %collective-permute-done.12 = bf16[256,1024]{1,0:T(8,128)(2,1)S(1)} collective-permute-done((bf16[256,1024]{1,0:T(8,128)(2,1)S(1)}, bf16[256,1024]{1,0:T(8,128)(2,1)S(1)}, u32[]{:S(2)}, u32[]{:S(2)}) %collective-permute-start.12) | collective-permute-done | bytes 524320 | tf_op jit(solution)/shard_map/ppermute | solution.py:483
  88.5 1.3 %collective-permute-start.10 = (bf16[256,1024]{1,0:T(8,128)(2,1)}, bf16[256,1024]{1,0:T(8,128)(2,1)}, u32[]{:S(2)}, u32[]{:S(2)}) collective-permute-start(bf16[256,1024]{1,0:T(8,128)(2,1)} %add_convert_fusion.2), channel_id=1, source_target_pairs={{1,0},{2,1},{3,2},{5,4},{6,5},{7,6},{9,8},{10,9},{11,10},{13,12},{... | collective-permute-start | bytes 1572872 | tf_op jit(solution)/shard_map/ppermute | solution.py:484
  90.7 3.1 %collective-permute-start.17 = (f32[512]{0:T(512)S(1)}, f32[512]{0:T(512)}, u32[]{:S(2)}, u32[]{:S(2)}) collective-permute-start(f32[512]{0:T(512)S(1)} %pad_maximum_fusion), channel_id=1, source_target_pairs={{0,1},{1,2},{2,3},{3,0},{4,5},{5,6},{6,7},{7,4},{8,9},{9,10},{10,1... | collective-permute-start | bytes 6152 | tf_op jit(solution)/shard_map/ppermute | solution.py:612
  93.9 1.0 add_convert_fusion
  94.8 4.7 %collective-permute-start.13 = (bf16[256,1024]{1,0:T(8,128)(2,1)}, bf16[256,1024]{1,0:T(8,128)(2,1)}, u32[]{:S(2)}, u32[]{:S(2)}) collective-permute-start(bf16[256,1024]{1,0:T(8,128)(2,1)} %add_convert_fusion.1), channel_id=1, source_target_pairs={{0,1},{1,2},{2,3},{4,5},{5,6},{6,7},{8,9},{9,10},{10,11},{12,13},{... | collective-permute-start | bytes 1572872 | tf_op jit(solution)/shard_map/ppermute | solution.py:483
  99.6 1.5 %collective-permute-done.17 = f32[512]{0:T(512)} collective-permute-done((f32[512]{0:T(512)S(1)}, f32[512]{0:T(512)}, u32[]{:S(2)}, u32[]{:S(2)}) %collective-permute-start.17) | collective-permute-done | bytes 2080 | tf_op jit(solution)/shard_map/ppermute | solution.py:612
  101.1 1.3 %collective-permute-start.16 = (bf16[256,1024]{1,0:T(8,128)(2,1)}, bf16[256,1024]{1,0:T(8,128)(2,1)}, u32[]{:S(2)}, u32[]{:S(2)}) collective-permute-start(bf16[256,1024]{1,0:T(8,128)(2,1)} %add_convert_fusion), channel_id=1, source_target_pairs={{1,0},{2,1},{3,2},{5,4},{6,5},{7,6},{9,8},{10,9},{11,10},{13,12},{... | collective-permute-start | bytes 1572872 | tf_op jit(solution)/shard_map/ppermute | solution.py:484
  102.4 1.2 %dynamic_slice.3 = s32[1]{0:T(128)} dynamic-slice(s32[4]{0:T(128)} %param.33, s32[]{:T(128)S(6)} %select_n.7), dynamic_slice_sizes={1} | dynamic-slice | bytes 12 | tf_op jit(solution)/shard_map/dynamic_slice | solution.py:705
  103.6 1.3 %rsqrt_select_fusion = f32[512]{0:T(512)S(1)} fusion(f32[512]{0:T(512)} %collective-permute-done.19, f32[512]{0:T(512)S(1)} %collective-permute-done.18, f32[512]{0:T(512)} %collective-permute-done.17, s32[]{:T(128)} %bitcast.7, f32[256]{0:T(256)S(1)} %bitcast.22, f32[256]{0:T(256)S(1)} %bitcast.24), kind=kLoop, calls=%fused_computation.17 | loop fusion | flops 4096 | bytes 10244 | tf_op jit(solution)/shard_map/jit(_where)/select_n | solution.py:711
  105.0 1.5 %convert_add_fusion.5 = f32[256,1024]{1,0:T(8,128)S(1)} fusion(bf16[256,1024]{1,0:T(8,128)(2,1)} %collective-permute-done.10, bf16[256,1024]{1,0:T(8,128)(2,1)} %collective-permute-done.8, bf16[256,1024]{1,0:T(8,128)(2,1)S(1)} %get-tuple-element.48), kind=kLoop, calls=%fused_computation.13 | loop fusion | flops 1310720 | bytes 2621440 | tf_op jit(solution)/shard_map/add | solution.py:490
  106.4 1.7 %land.1 = (f32[2048,128]{1,0:T(8,128)}, bf16[3,2048]{1,0:T(4,128)(2,1)}, bf16[3,1024]{1,0:T(4,128)(2,1)}) custom-call(s32[18]{0:T(128)S(1)} %concatenate.9.meta, bf16[2432,128]{1,0:T(8,128)(2,1)S(1)} %ending.1.refs_0_, bf16[2432,128]{1,0:T(8,128)(2,1)S(1)} %collective-permute-done.20.refs_1_, bf16[2432,128]{1,0:T(8,128)(2,1)S(1)} %collective-permute-done.21.refs_2_), custom_call_target="tpu_custom_call" | custom-call | flops 1000000 | bytes 3145728 | tf_op jit(solution)/shard_map/land/pallas_call | solution.py:596
  108.2 2.8 %collective-permute-done.13 = bf16[256,1024]{1,0:T(8,128)(2,1)} collective-permute-done((bf16[256,1024]{1,0:T(8,128)(2,1)}, bf16[256,1024]{1,0:T(8,128)(2,1)}, u32[]{:S(2)}, u32[]{:S(2)}) %collective-permute-start.13) | collective-permute-done | bytes 524320 | tf_op jit(solution)/shard_map/ppermute | solution.py:483
  110.9 4.9 %collective-permute-done.16 = bf16[256,1024]{1,0:T(8,128)(2,1)} collective-permute-done((bf16[256,1024]{1,0:T(8,128)(2,1)}, bf16[256,1024]{1,0:T(8,128)(2,1)}, u32[]{:S(2)}, u32[]{:S(2)}) %collective-permute-start.16) | collective-permute-done | bytes 524320 | tf_op jit(solution)/shard_map/ppermute | solution.py:484
  115.8 1.5 %convert_add_fusion.4 = f32[256,1024]{1,0:T(8,128)S(1)} fusion(bf16[256,1024]{1,0:T(8,128)(2,1)} %collective-permute-done.16, bf16[256,1024]{1,0:T(8,128)(2,1)} %collective-permute-done.13, bf16[256,1024]{1,0:T(8,128)(2,1)S(1)} %get-tuple-element.60), kind=kLoop, calls=%fused_computation.10 | loop fusion | flops 1310720 | bytes 2621440 | tf_op jit(solution)/shard_map/add | solution.py:490
  117.3 1.1 fusion
  (61 shorter events, 13.5 us)
Async XLA Ops:
  0.6 7.6 %collective-permute-start = (f32[2,2048,128]{2,1,0:T(8,128)}, f32[2,2048,128]{2,1,0:T(8,128)S(1)}, u32[]{:S(2)}, u32[]{:S(2)}) collective-permute-start(f32[2,2048,128]{2,1,0:T(8,128)} %bitcast.13), channel_id=1, source_target_pairs={{0,4},{4,0},{8,12},{12,8},{1,5},{5,1},{9,13},{13,9},{2,6},{6,2},{1... | collective-permute-start | bytes 6291464 | tf_op jit(solution)/shard_map/ppermute | solution.py:616
  4.2 7.0 %collective-permute-start.2 = (bf16[3,3072]{1,0:T(4,128)(2,1)S(1)}, bf16[3,3072]{1,0:T(4,128)(2,1)S(1)}, u32[]{:S(2)}, u32[]{:S(2)}) collective-permute-start(bf16[3,3072]{1,0:T(4,128)(2,1)S(1)} %get-tuple-element.40), channel_id=1, source_target_pairs={{0,4},{4,8},{8,12},{12,0},{1,5},{5,9},{9,13},{13,1},{2,6},{6,10},{... | collective-permute-start | bytes 55304 | tf_op jit(solution)/shard_map/ppermute | solution.py:612
  4.3 6.9 %collective-permute-start.3 = (bf16[3,3072]{1,0:T(4,128)(2,1)S(1)}, bf16[3,3072]{1,0:T(4,128)(2,1)S(1)}, u32[]{:S(2)}, u32[]{:S(2)}) collective-permute-start(bf16[3,3072]{1,0:T(4,128)(2,1)S(1)} %get-tuple-element.41), channel_id=1, source_target_pairs={{0,8},{4,12},{8,0},{12,4},{1,9},{5,13},{9,1},{13,5},{2,10},{6,14},... | collective-permute-start | bytes 55304 | tf_op jit(solution)/shard_map/ppermute | solution.py:612
  7.2 3.9 %copy-start.11 = (f32[32]{0:T(128)S(1)}, f32[32]{0:T(128)}, u32[]{:S(2)}) copy-start(f32[32]{0:T(128)} %refs_9_.2) | copy-start | bytes 388
  7.3 3.9 %copy-start.12 = (f32[32]{0:T(128)S(1)}, f32[32]{0:T(128)}, u32[]{:S(2)}) copy-start(f32[32]{0:T(128)} %refs_10_.1) | copy-start | bytes 388
  7.3 3.9 %collective-permute-start.4 = (bf16[3,3072]{1,0:T(4,128)(2,1)S(1)}, bf16[3,3072]{1,0:T(4,128)(2,1)S(1)}, u32[]{:S(2)}, u32[]{:S(2)}) collective-permute-start(bf16[3,3072]{1,0:T(4,128)(2,1)S(1)} %get-tuple-element.42), channel_id=1, source_target_pairs={{0,12},{4,0},{8,4},{12,8},{1,13},{5,1},{9,5},{13,9},{2,14},{6,2},{... | collective-permute-start | bytes 55304 | tf_op jit(solution)/shard_map/ppermute | solution.py:612
  8.2 1.6 %copy-start.1 = (f32[2,32,64,128]{3,2,1,0:T(8,128)S(1)}, f32[2,32,64,128]{3,2,1,0:T(8,128)}, u32[]{:S(2)}) copy-start(f32[2,32,64,128]{3,2,1,0:T(8,128)} %param.27) | copy-start | bytes 6291460
  9.8 1.9 %copy-start.4 = (bf16[512,1024]{1,0:T(8,128)(2,1)S(1)}, bf16[512,1024]{1,0:T(8,128)(2,1)}, u32[]{:S(2)}) copy-start(bf16[512,1024]{1,0:T(8,128)(2,1)} %bc_ref.1) | copy-start | bytes 3145732
  9.8 1.9 %copy-start.8 = (f32[512,32]{0,1:T(8,128)S(1)}, f32[512,32]{0,1:T(8,128)}, u32[]{:S(2)}) copy-start(f32[512,32]{0,1:T(8,128)} %param.20) | copy-start | bytes 196612
  9.8 1.9 %copy-start.9 = (bf16[4,2048]{1,0:T(4,128)(2,1)S(1)}, bf16[4,2048]{1,0:T(4,128)(2,1)}, u32[]{:S(2)}) copy-start(bf16[4,2048]{1,0:T(4,128)(2,1)} %refs_11_.1) | copy-start | bytes 49156
  9.8 1.9 %copy-start.10 = (bf16[4,1024]{1,0:T(4,128)(2,1)S(1)}, bf16[4,1024]{1,0:T(4,128)(2,1)}, u32[]{:S(2)}) copy-start(bf16[4,1024]{1,0:T(4,128)(2,1)} %refs_13_.1) | copy-start | bytes 24580
  10.6 13.4 %collective-permute-start.1 = (bf16[1,2048,128]{2,1,0:T(8,128)(2,1)S(1)}, bf16[1,2048,128]{2,1,0:T(8,128)(2,1)S(1)}, u32[]{:S(2)}, u32[]{:S(2)}) collective-permute-start(bf16[1,2048,128]{2,1,0:T(8,128)(2,1)S(1)} %get-tuple-element.38), channel_id=1, source_target_pairs={{0,8},{4,12},{8,0},{12,4},{1,9},{5,13},{9,1},{13,5},{2,10},{6,14},... | collective-permute-start | bytes 1572872 | tf_op jit(solution)/shard_map/ppermute | solution.py:612
  11.7 12.4 %copy-start = (bf16[512,2048]{1,0:T(8,128)(2,1)S(1)}, bf16[512,2048]{1,0:T(8,128)(2,1)}, u32[]{:S(2)}) copy-start(bf16[512,2048]{1,0:T(8,128)(2,1)} %refs_2_.1) | copy-start | bytes 6291460
  11.7 12.3 %copy-start.2 = (f32[2,32,64,128]{3,2,1,0:T(8,128)S(1)}, f32[2,32,64,128]{3,2,1,0:T(8,128)}, u32[]{:S(2)}) copy-start(f32[2,32,64,128]{3,2,1,0:T(8,128)} %param.27) | copy-start | bytes 6291460
  11.7 12.3 %copy-start.5 = (f32[2048]{0:T(1024)S(1)}, f32[2048]{0:T(1024)}, u32[]{:S(2)}) copy-start(f32[2048]{0:T(1024)} %param.23) | copy-start | bytes 24580
  32.0 12.2 %collective-permute-start.6 = (bf16[256,1024]{1,0:T(8,128)(2,1)S(1)}, bf16[256,1024]{1,0:T(8,128)(2,1)S(1)}, u32[]{:S(2)}, u32[]{:S(2)}) collective-permute-start(bf16[256,1024]{1,0:T(8,128)(2,1)S(1)} %get-tuple-element.49), channel_id=1, source_target_pairs={{3,2},{7,6},{11,10},{15,14},{19,18},{23,22},{27,26},{31,30}} | collective-permute-start | bytes 1572872 | tf_op jit(solution)/shard_map/ppermute | solution.py:484
  32.7 13.5 %collective-permute-start.5 = (bf16[256,1024]{1,0:T(8,128)(2,1)S(1)}, bf16[256,1024]{1,0:T(8,128)(2,1)S(1)}, u32[]{:S(2)}, u32[]{:S(2)}) collective-permute-start(bf16[256,1024]{1,0:T(8,128)(2,1)S(1)} %get-tuple-element.51), channel_id=1, source_target_pairs={{0,1},{4,5},{8,9},{12,13},{16,17},{20,21},{24,25},{28,29}} | collective-permute-start | bytes 1572872 | tf_op jit(solution)/shard_map/ppermute | solution.py:483
  46.2 11.2 %collective-permute-start.14 = (bf16[256,1024]{1,0:T(8,128)(2,1)S(1)}, bf16[256,1024]{1,0:T(8,128)(2,1)S(1)}, u32[]{:S(2)}, u32[]{:S(2)}) collective-permute-start(bf16[256,1024]{1,0:T(8,128)(2,1)S(1)} %get-tuple-element.61), channel_id=1, source_target_pairs={{3,2},{7,6},{11,10},{15,14},{19,18},{23,22},{27,26},{31,30}} | collective-permute-start | bytes 1572872 | tf_op jit(solution)/shard_map/ppermute | solution.py:484
  46.9 16.8 %collective-permute-start.11 = (bf16[256,1024]{1,0:T(8,128)(2,1)S(1)}, bf16[256,1024]{1,0:T(8,128)(2,1)S(1)}, u32[]{:S(2)}, u32[]{:S(2)}) collective-permute-start(bf16[256,1024]{1,0:T(8,128)(2,1)S(1)} %get-tuple-element.63), channel_id=1, source_target_pairs={{0,1},{4,5},{8,9},{12,13},{16,17},{20,21},{24,25},{28,29}} | collective-permute-start | bytes 1572872 | tf_op jit(solution)/shard_map/ppermute | solution.py:483
  51.7 20.1 %collective-permute-start.7 = (bf16[256,1024]{1,0:T(8,128)(2,1)S(1)}, bf16[256,1024]{1,0:T(8,128)(2,1)S(1)}, u32[]{:S(2)}, u32[]{:S(2)}) collective-permute-start(bf16[256,1024]{1,0:T(8,128)(2,1)S(1)} %get-tuple-element.72), channel_id=1, source_target_pairs={{0,1},{1,2},{4,5},{5,6},{8,9},{9,10},{12,13},{13,14},{16,17},{17,1... | collective-permute-start | bytes 1572872 | tf_op jit(solution)/shard_map/ppermute | solution.py:483
  53.0 37.7 %collective-permute-start.18 = (f32[512]{0:T(512)S(1)}, f32[512]{0:T(512)S(1)}, u32[]{:S(2)}, u32[]{:S(2)}) collective-permute-start(f32[512]{0:T(512)S(1)} %pad_maximum_fusion), channel_id=1, source_target_pairs={{0,2},{1,3},{2,0},{3,1},{4,6},{5,7},{6,4},{7,5},{8,10},{9,11},{10,... | collective-permute-start | bytes 6152 | tf_op jit(solution)/shard_map/ppermute | solution.py:612
  53.1 41.7 %collective-permute-start.19 = (f32[512]{0:T(512)S(1)}, f32[512]{0:T(512)}, u32[]{:S(2)}, u32[]{:S(2)}) collective-permute-start(f32[512]{0:T(512)S(1)} %pad_maximum_fusion), channel_id=1, source_target_pairs={{0,3},{1,0},{2,1},{3,2},{4,7},{5,4},{6,5},{7,6},{8,11},{9,8},{10,9... | collective-permute-start | bytes 6152 | tf_op jit(solution)/shard_map/ppermute | solution.py:612
  57.4 19.7 %collective-permute-start.9 = (bf16[256,1024]{1,0:T(8,128)(2,1)S(1)}, bf16[256,1024]{1,0:T(8,128)(2,1)S(1)}, u32[]{:S(2)}, u32[]{:S(2)}) collective-permute-start(bf16[256,1024]{1,0:T(8,128)(2,1)S(1)} %get-tuple-element.73), channel_id=1, source_target_pairs={{2,1},{3,2},{6,5},{7,6},{10,9},{11,10},{14,13},{15,14},{18,17},{19... | collective-permute-start | bytes 1572872 | tf_op jit(solution)/shard_map/ppermute | solution.py:484
  63.7 15.1 %collective-permute-start.20 = (bf16[2432,128]{1,0:T(8,128)(2,1)S(1)}, bf16[2432,128]{1,0:T(8,128)(2,1)S(1)}, u32[]{:S(2)}, u32[]{:S(2)}) collective-permute-start(bf16[2432,128]{1,0:T(8,128)(2,1)S(1)} %ending.1.refs_0_), channel_id=1, source_target_pairs={{0,8},{4,12},{8,0},{12,4},{1,9},{5,13},{9,1},{13,5},{2,10},{6,14},... | collective-permute-start | bytes 1867784 | tf_op jit(solution)/shard_map/ppermute | solution.py:612
  71.7 16.7 %collective-permute-start.12 = (bf16[256,1024]{1,0:T(8,128)(2,1)S(1)}, bf16[256,1024]{1,0:T(8,128)(2,1)S(1)}, u32[]{:S(2)}, u32[]{:S(2)}) collective-permute-start(bf16[256,1024]{1,0:T(8,128)(2,1)S(1)} %get-tuple-element.74), channel_id=1, source_target_pairs={{0,1},{1,2},{4,5},{5,6},{8,9},{9,10},{12,13},{13,14},{16,17},{17,1... | collective-permute-start | bytes 1572872 | tf_op jit(solution)/shard_map/ppermute | solution.py:483
  77.1 16.7 %collective-permute-start.15 = (bf16[256,1024]{1,0:T(8,128)(2,1)S(1)}, bf16[256,1024]{1,0:T(8,128)(2,1)S(1)}, u32[]{:S(2)}, u32[]{:S(2)}) collective-permute-start(bf16[256,1024]{1,0:T(8,128)(2,1)S(1)} %get-tuple-element.75), channel_id=1, source_target_pairs={{2,1},{3,2},{6,5},{7,6},{10,9},{11,10},{14,13},{15,14},{18,17},{19... | collective-permute-start | bytes 1572872 | tf_op jit(solution)/shard_map/ppermute | solution.py:484
  78.8 26.1 %collective-permute-start.8 = (bf16[256,1024]{1,0:T(8,128)(2,1)}, bf16[256,1024]{1,0:T(8,128)(2,1)}, u32[]{:S(2)}, u32[]{:S(2)}) collective-permute-start(bf16[256,1024]{1,0:T(8,128)(2,1)} %add_convert_fusion.3), channel_id=1, source_target_pairs={{0,1},{1,2},{2,3},{4,5},{5,6},{6,7},{8,9},{9,10},{10,11},{12,13},{... | collective-permute-start | bytes 1572872 | tf_op jit(solution)/shard_map/ppermute | solution.py:483
  88.5 16.5 %collective-permute-start.10 = (bf16[256,1024]{1,0:T(8,128)(2,1)}, bf16[256,1024]{1,0:T(8,128)(2,1)}, u32[]{:S(2)}, u32[]{:S(2)}) collective-permute-start(bf16[256,1024]{1,0:T(8,128)(2,1)} %add_convert_fusion.2), channel_id=1, source_target_pairs={{1,0},{2,1},{3,2},{5,4},{6,5},{7,6},{9,8},{10,9},{11,10},{13,12},{... | collective-permute-start | bytes 1572872 | tf_op jit(solution)/shard_map/ppermute | solution.py:484
  90.7 10.3 %collective-permute-start.17 = (f32[512]{0:T(512)S(1)}, f32[512]{0:T(512)}, u32[]{:S(2)}, u32[]{:S(2)}) collective-permute-start(f32[512]{0:T(512)S(1)} %pad_maximum_fusion), channel_id=1, source_target_pairs={{0,1},{1,2},{2,3},{3,0},{4,5},{5,6},{6,7},{7,4},{8,9},{9,10},{10,1... | collective-permute-start | bytes 6152 | tf_op jit(solution)/shard_map/ppermute | solution.py:612
  93.8 12.6 %collective-permute-start.21 = (bf16[2432,128]{1,0:T(8,128)(2,1)S(1)}, bf16[2432,128]{1,0:T(8,128)(2,1)S(1)}, u32[]{:S(2)}, u32[]{:S(2)}) collective-permute-start(bf16[2432,128]{1,0:T(8,128)(2,1)S(1)} %route.1), channel_id=1, source_target_pairs={{0,4},{4,0},{8,12},{12,8},{1,5},{5,1},{9,13},{13,9},{2,6},{6,2},{1... | collective-permute-start | bytes 1867784 | tf_op jit(solution)/shard_map/ppermute | solution.py:616
  94.8 16.1 %collective-permute-start.13 = (bf16[256,1024]{1,0:T(8,128)(2,1)}, bf16[256,1024]{1,0:T(8,128)(2,1)}, u32[]{:S(2)}, u32[]{:S(2)}) collective-permute-start(bf16[256,1024]{1,0:T(8,128)(2,1)} %add_convert_fusion.1), channel_id=1, source_target_pairs={{0,1},{1,2},{2,3},{4,5},{5,6},{6,7},{8,9},{9,10},{10,11},{12,13},{... | collective-permute-start | bytes 1572872 | tf_op jit(solution)/shard_map/ppermute | solution.py:483
  101.1 14.8 %collective-permute-start.16 = (bf16[256,1024]{1,0:T(8,128)(2,1)}, bf16[256,1024]{1,0:T(8,128)(2,1)}, u32[]{:S(2)}, u32[]{:S(2)}) collective-permute-start(bf16[256,1024]{1,0:T(8,128)(2,1)} %add_convert_fusion), channel_id=1, source_target_pairs={{1,0},{2,1},{3,2},{5,4},{6,5},{7,6},{9,8},{10,9},{11,10},{13,12},{... | collective-permute-start | bytes 1572872 | tf_op jit(solution)/shard_map/ppermute | solution.py:484
  (3 other events, 3.0 us)

commit v5 on v4

--- a/solution.py
+++ b/solution.py
@@ -19,8 +19,9 @@
 NCH = 4
 LANES = 128
 WIDE = 512
-SCAN_WIDE = 1024
-PIECES = (2, 2)
+PIECE = 2
+PROJ = 36
+AHEAD = 3
 
 F32 = jnp.float32
 BF16 = jnp.bfloat16
@@ -182,6 +183,7 @@
     me = meta[0]
     slot = meta[2 + me]
     inner = conv_ref.shape[1] - BCW
+    wide = x_ref.shape[1]
     group = over(meta[1] * heads, GHEADS)
 
     @pl.when((block == 0) & (c == 0))
@@ -245,10 +247,10 @@
     @pl.when(c == 0)
     def _():
         state[...] = jnp.zeros_like(state)
-        lane = lax.broadcasted_iota(jnp.int32, (LANES, SCAN_WIDE), 0)
-        channel = lax.broadcasted_iota(jnp.int32, (LANES, SCAN_WIDE), 1) + block * SCAN_WIDE
+        lane = lax.broadcasted_iota(jnp.int32, (LANES, wide), 0)
+        channel = lax.broadcasted_iota(jnp.int32, (LANES, wide), 1) + block * wide
         pick_ref[...] = ((wrap(lane, heads) == over(channel, HDIM)) & (lane < 2 * heads)).astype(BF16)
-        tail_x[...] = start[:, pl.ds(pl.multiple_of(block * SCAN_WIDE, SCAN_WIDE), SCAN_WIDE)]
+        tail_x[...] = start[:, pl.ds(pl.multiple_of(block * wide, wide), wide)]
 
     x = x_ref[...].astype(F32)
     conv = conv_taps(tail_x[...], x, wx_ref[...].astype(F32))
@@ -259,41 +261,42 @@
     scaled = (values * spread[SPAN : 2 * SPAN]).astype(BF16)
     held = state[...] * rows[0:1]
     right = jnp.concatenate([scaled, held.astype(BF16)], axis=0)
-    y_ref[...] = dot(left[c], right) * spread[:SPAN] + rows[2:3] * values
+    y_ref[...] = (dot(left[c], right) * spread[:SPAN] + rows[2:3] * values).astype(BF16)
     state[...] = (held + dot(bmap_t[c], scaled)) * rows[1:2]
 
     @pl.when(c == NCH - 1)
     def _():
-        final_ref[...] = jnp.transpose(state[...])
+        final_ref[...] = jnp.transpose(state[...]).astype(BF16)
 
 
 def run_scan(meta, conv, mark, x, bc, dt, rate, skip, wx, wbc, heads, slots):
     inner = x.shape[1]
-    blocks = inner // SCAN_WIDE
+    wide = min(2048, inner)
+    blocks = inner // wide
     reqs = len(conv)
     once = lambda b, c: jnp.where(b == 0, c, NCH - 1)
     group = lambda m: over(m[1] * heads, GHEADS)
     in_specs = [pl.BlockSpec((CONV - 1, inner + BCW), lambda b, c, m: (0, 0))] * reqs
     in_specs += [
         pl.BlockSpec((8, LANES), lambda b, c, m: (0, 0)),
-        pl.BlockSpec((SPAN, SCAN_WIDE), lambda b, c, m: (c, b)),
+        pl.BlockSpec((SPAN, wide), lambda b, c, m: (c, b)),
         pl.BlockSpec((SPAN, LANES), lambda b, c, m: (once(b, c), group(m))),
         pl.BlockSpec((SPAN, LANES), lambda b, c, m: (once(b, c), group(m) + BCG)),
         pl.BlockSpec((heads, SPAN), lambda b, c, m: (0, once(b, c))),
         pl.BlockSpec((heads,), lambda b, c, m: (0,)),
         pl.BlockSpec((heads,), lambda b, c, m: (0,)),
-        pl.BlockSpec((CONV, SCAN_WIDE), lambda b, c, m: (0, b)),
+        pl.BlockSpec((CONV, wide), lambda b, c, m: (0, b)),
         pl.BlockSpec((CONV, LANES), lambda b, c, m: (0, group(m))),
         pl.BlockSpec((CONV, LANES), lambda b, c, m: (0, group(m) + BCG)),
     ]
     out_specs = [
-        pl.BlockSpec((SPAN, SCAN_WIDE), lambda b, c, m: (c, b)),
-        pl.BlockSpec((SCAN_WIDE, STATE), lambda b, c, m: (b, 0)),
+        pl.BlockSpec((SPAN, wide), lambda b, c, m: (c, b)),
+        pl.BlockSpec((wide, STATE), lambda b, c, m: (b, 0)),
         pl.BlockSpec((SPAN, LANES), lambda b, c, m: (once(b, c), 0)),
         pl.BlockSpec((SPAN, LANES), lambda b, c, m: (once(b, c), 0)),
         pl.BlockSpec((16, LANES), lambda b, c, m: (0, 0)),
         pl.BlockSpec((CONV - 1, inner + BCW), lambda b, c, m: (0, 0)),
-        pl.BlockSpec((LANES, SCAN_WIDE), lambda b, c, m: (0, b)),
+        pl.BlockSpec((LANES, wide), lambda b, c, m: (0, b)),
     ]
     return pl.pallas_call(
         functools.partial(scan_kernel, heads, slots, reqs),
@@ -304,8 +307,8 @@
             out_specs=out_specs,
             scratch_shapes=[
                 pltpu.VMEM((8, inner + BCW), F32),
-                pltpu.VMEM((STATE, SCAN_WIDE), F32),
-                pltpu.VMEM((8, SCAN_WIDE), F32),
+                pltpu.VMEM((STATE, wide), F32),
+                pltpu.VMEM((8, wide), F32),
                 pltpu.VMEM((2, 8, LANES), F32),
                 pltpu.VMEM((NCH, SPAN, 2 * SPAN), BF16),
                 pltpu.VMEM((NCH, STATE, SPAN), BF16),
@@ -314,8 +317,8 @@
             ],
         ),
         out_shape=[
-            jax.ShapeDtypeStruct((SUF, inner), F32),
-            jax.ShapeDtypeStruct((inner, STATE), F32),
+            jax.ShapeDtypeStruct((SUF, inner), BF16),
+            jax.ShapeDtypeStruct((inner, STATE), BF16),
             jax.ShapeDtypeStruct((SUF, LANES), BF16),
             jax.ShapeDtypeStruct((SUF, LANES), BF16),
             jax.ShapeDtypeStruct((16, LANES), BF16),
@@ -323,7 +326,7 @@
             jax.ShapeDtypeStruct((LANES, inner), BF16),
         ],
         compiler_params=pltpu.CompilerParams(
-            dimension_semantics=("arbitrary", "arbitrary"), vmem_limit_bytes=24 * 2**20
+            dimension_semantics=("arbitrary", "arbitrary"), vmem_limit_bytes=16 * 2**20
         ),
         cost_estimate=pl.CostEstimate(
             flops=8 * 10**9, bytes_accessed=12 * 2**20, transcendentals=SUF * inner
@@ -332,7 +335,7 @@
     )(meta, *conv, mark, x, bc, bc, dt, rate, skip, wx, wbc, wbc)
 
 
-def project_kernel(chunks, shares, picks, meta, *refs):
+def project_kernel(chunks, shares, picks, emit, late, meta, *refs):
     if picks:
         reqs, slots = picks
         others = reqs // 2 - 1
@@ -341,26 +344,32 @@
         refs = refs[2 + others :]
     else:
         start_ref, refs = refs[0], refs[1:]
+    if late:
+        before_ref, refs = refs[0], refs[1:]
     y_ref, gate_ref, cmap_ref, reach_ref, gain_ref, pick_ref, w_ref = refs[:7]
-    out_refs = refs[7 : 7 + shares]
-    sq_ref = refs[7 + shares]
+    out_refs = refs[7 : 7 + len(emit)]
+    late_refs = refs[7 + len(emit) : 7 + len(emit) + len(late)]
+    refs = refs[7 + len(emit) + len(late) :]
+    sq_ref = refs[0]
     if picks:
-        start_ref = refs[8 + shares]
+        start_ref = refs[1]
     held, w_held, arrived = refs[-3:]
     step = pl.program_id(0)
     inner = y_ref.shape[1]
     share = out_refs[0].shape[1]
 
-    def fetch(q):
-        column = pl.multiple_of(wrap(q + meta[1], shares) * share, share)
+    def fetch(i):
+        q = emit[i]
+        to = jnp.where(2 * meta[1] < shares, meta[1] + q, meta[1] - q + shares)
+        column = pl.multiple_of(wrap(to, shares) * share, share)
         return pltpu.make_async_copy(
-            w_ref.at[:, pl.ds(column, share)], w_held.at[q], arrived.at[q]
+            w_ref.at[:, pl.ds(column, share)], w_held.at[i % AHEAD], arrived.at[i % AHEAD]
         )
 
     @pl.when(step == 0)
     def _():
-        for q in range(shares):
-            fetch(q).start()
+        for i in range(min(AHEAD, len(emit))):
+            fetch(i).start()
 
     if picks:
 
@@ -381,7 +390,7 @@
         for i in range(inner // WIDE):
             at = pl.ds(i * WIDE, WIDE)
             carried = dot_t(cmap_ref[...], start_ref[at, :])
-            y = y_ref[:, at] + dot(reach_ref[...], pick_ref[:, at]) * carried
+            y = y_ref[:, at].astype(F32) + dot(reach_ref[...], pick_ref[:, at]) * carried
             gated = y * silu(gate_ref[:, at].astype(F32))
             held[rows, at] = (gated * gain_ref[:, at]).astype(BF16)
             gated = gated * gated
@@ -395,15 +404,23 @@
             preferred_element_type=F32,
         )
 
-    for q in range(shares):
-
-        @pl.when(step == chunks + q)
-        def _(q=q):
-            fetch(q).wait()
-            out_refs[q][...] = dot(held[...], w_held[q]).astype(BF16)
-
-
-def run_project(first, chunks, meta, states, y, gate, cmap, reach, gain, pick, weight, shares, reqs):
+    for i in range(len(emit)):
+
+        @pl.when(step == chunks + i)
+        def _(i=i):
+            fetch(i).wait()
+            out_refs[i][...] = dot(held[...], w_held[i % AHEAD]).astype(BF16)
+            if emit[i] in late:
+                late_refs[late.index(emit[i])][...] = dot(
+                    before_ref[...], w_held[i % AHEAD]
+                ).astype(BF16)
+            if i + AHEAD < len(emit):
+                fetch(i + AHEAD).start()
+
+
+def run_project(
+    first, chunks, emit, late, meta, states, before, y, gate, cmap, reach, gain, pick, weight, shares, reqs
+):
     inner, width = weight.shape
     share = width // shares
     count = chunks * SPAN
@@ -411,6 +428,7 @@
     whole = lambda n, m: (0, 0)
     state = (1, inner, STATE)
     choose = len(states) > 1
+    single = pl.Buffered(1)
     slots = states[0].shape[0]
 
     def held(owner, m):
@@ -418,26 +436,36 @@
 
     if choose:
         state_specs = [
-            pl.BlockSpec(state, lambda n, m: (held(m[0], m), 0, 0)),
-            pl.BlockSpec(state, lambda n, m: (held(m[0] ^ 1, m), 0, 0)),
-        ] + [pl.BlockSpec(state, lambda n, m: (0, 0, 0))] * (len(states) - 2)
+            pl.BlockSpec(state, lambda n, m: (held(m[0], m), 0, 0), pipeline_mode=single),
+            pl.BlockSpec(state, lambda n, m: (held(m[0] ^ 1, m), 0, 0), pipeline_mode=single),
+        ] + [pl.BlockSpec(state, lambda n, m: (0, 0, 0), pipeline_mode=single)] * (len(states) - 2)
     else:
-        state_specs = [pl.BlockSpec((inner, STATE), whole)]
+        state_specs = [pl.BlockSpec((inner, STATE), whole, pipeline_mode=single)]
     out_specs = [
         pl.BlockSpec((count, share), whole)
-        for q in range(shares)
-    ] + [pl.BlockSpec((8, LANES), lambda n, m: (0, jnp.minimum(n, chunks - 1)))]
-    out_shape = [jax.ShapeDtypeStruct((count, share), BF16)] * shares + [
-        jax.ShapeDtypeStruct((8, count), F32)
+        for q in emit
     ]
+    out_specs += [pl.BlockSpec((first * SPAN, share), whole) for q in late]
+    out_specs += [pl.BlockSpec((8, LANES), lambda n, m: (0, jnp.minimum(n, chunks - 1)))]
+    out_shape = [jax.ShapeDtypeStruct((count, share), BF16)] * len(emit)
+    out_shape += [jax.ShapeDtypeStruct((first * SPAN, share), BF16)] * len(late)
+    out_shape.append(jax.ShapeDtypeStruct((8, count), F32))
     if choose:
         out_specs.append(pl.BlockSpec((inner, STATE), whole))
         out_shape.append(jax.ShapeDtypeStruct((inner, STATE), BF16))
+    gated = jax.ShapeDtypeStruct((count, inner), BF16)
+    scratch = []
+    if late:
+        state_specs.append(pl.BlockSpec(before[0].shape, whole, pipeline_mode=single))
+        scratch.append(pltpu.VMEM(gated.shape, BF16))
+    else:
+        out_specs.append(pl.BlockSpec(gated.shape, whole))
+        out_shape.append(gated)
     return pl.pallas_call(
-        functools.partial(project_kernel, chunks, shares, (reqs, slots) if choose else None),
+        functools.partial(project_kernel, chunks, shares, (reqs, slots) if choose else None, emit, late),
         grid_spec=pltpu.PrefetchScalarGridSpec(
             num_scalar_prefetch=1,
-            grid=(chunks + shares,),
+            grid=(chunks + len(emit),),
             in_specs=state_specs
             + [
                 pl.BlockSpec((SPAN, inner), rows),
@@ -445,51 +473,50 @@
                 pl.BlockSpec((SPAN, LANES), rows),
                 pl.BlockSpec((SPAN, LANES), rows),
                 pl.BlockSpec((1, inner), whole),
-                pl.BlockSpec((LANES, inner), whole),
+                pl.BlockSpec((LANES, inner), whole, pipeline_mode=single),
                 pl.BlockSpec(memory_space=pl.ANY),
             ],
             out_specs=out_specs,
-            scratch_shapes=[
-                pltpu.VMEM((count, inner), BF16),
-                pltpu.VMEM((shares, inner, share), BF16),
-                pltpu.SemaphoreType.DMA((shares,)),
+            scratch_shapes=scratch
+            + [
+                pltpu.VMEM((AHEAD, inner, share), BF16),
+                pltpu.SemaphoreType.DMA((AHEAD,)),
             ],
         ),
         out_shape=out_shape,
         compiler_params=pltpu.CompilerParams(
-            dimension_semantics=("arbitrary",), vmem_limit_bytes=36 * 2**20
-        ),
-        cost_estimate=pl.CostEstimate(
-            flops=2 * count * inner * width,
-            bytes_accessed=2 * inner * width + 10 * 2**20,
-            transcendentals=count * inner,
-        ),
+            dimension_semantics=("arbitrary",), vmem_limit_bytes=PROJ * 2**20
+        ),
+        cost_estimate=pl.CostEstimate(flops=1, bytes_accessed=1, transcendentals=0),
         name="project",
-    )(meta, *states, y, gate, cmap, reach, gain, pick, weight)
+    )(meta, *states, *before, y, gate, cmap, reach, gain, pick, weight)
 
 
 def line_sums(parts, mark, size):
-    to_right = [(i, i + 1) for i in range(size - 1)]
-    to_left = [(i + 1, i) for i in range(size - 1)]
-    add = lambda a, b: (a.astype(F32) + b.astype(F32)).astype(BF16)
-    right = [None] * len(parts)
-    left = [None] * len(parts)
-    for s in range(size - 1):
-        for p in range(len(parts)):
-            part = parts[p]
-            go_right, go_left = part[size - 1 - s], part[s + 1]
-            if s:
-                go_right, go_left = add(go_right, right[p]), add(go_left, left[p])
-            right[p] = lax.ppermute(go_right, "tp", to_right[: s + 1])
-            left[p] = lax.ppermute(go_left, "tp", to_left[size - 2 - s :])
-            if s == 0 and p + 1 < len(parts):
-                right[p], left[p], parts[p + 1], mark = lax.optimization_barrier(
-                    (right[p], left[p], parts[p + 1], mark)
+    parts = list(parts)
+    sums = []
+    for p in range(len(parts)):
+        landed = []
+        came = {}
+        for k in range(size - 1):
+            for d in range(size - 1, k, -1):
+                slot = d - k if 2 * k < size else size - d + k
+                go = parts[p][slot]
+                if k:
+                    go = (go.astype(F32) + came[k - 1, d].astype(F32)).astype(BF16)
+                came[k, d] = lax.ppermute(
+                    go, "tp", [(k, k + 1), (size - 1 - k, size - 2 - k)]
                 )
-    return mark, [
-        part[0].astype(F32) + r.astype(F32) + l.astype(F32)
-        for part, r, l in zip(parts, right, left)
-    ]
+                if k == 0 and d == size - 1 and p + 1 < len(parts):
+                    came[k, d], parts[p + 1], mark = lax.optimization_barrier(
+                        (came[k, d], parts[p + 1], mark)
+                    )
+            landed.append(came[k, k + 1])
+        total = parts[p][0].astype(F32)
+        for value in landed:
+            total += value.astype(F32)
+        sums.append(total)
+    return mark, sums
 
 
 def source_of(meta, device, reqs):
@@ -506,7 +533,7 @@
         at = pl.ds(i * WIDE, WIDE)
         decay = dot(total_ref[...], pick_ref[:, at])[0:1]
         decay = jnp.transpose(jnp.broadcast_to(decay, (STATE, WIDE)))
-        out_ref[at, :] = (local_ref[at, :] + decay * start_ref[at, :].astype(F32)).astype(BF16)
+        out_ref[at, :] = (local_ref[at, :].astype(F32) + decay * start_ref[at, :].astype(F32)).astype(BF16)
     row = lax.broadcasted_iota(jnp.int32, (16, SUF), 0) + length - (CONV - 1)
     found = (row == lax.broadcasted_iota(jnp.int32, (16, SUF), 1)).astype(BF16)
     conv = conv_ref[...].astype(F32)
@@ -536,8 +563,8 @@
             out_specs=pl.BlockSpec((rows, LANES), lambda i, m: (0, 0)),
         ),
         out_shape=jax.ShapeDtypeStruct((rows, LANES), BF16),
-        compiler_params=pltpu.CompilerParams(vmem_limit_bytes=24 * 2**20),
-        cost_estimate=pl.CostEstimate(flops=10**8, bytes_accessed=6 * 2**20, transcendentals=0),
+        compiler_params=pltpu.CompilerParams(vmem_limit_bytes=16 * 2**20),
+        cost_estimate=pl.CostEstimate(flops=1, bytes_accessed=1, transcendentals=0),
         name="ending",
     )(meta, *operands)
 
@@ -563,7 +590,7 @@
         ),
         out_shape=jax.ShapeDtypeStruct(shape, BF16),
         compiler_params=pltpu.CompilerParams(vmem_limit_bytes=12 * 2**20),
-        cost_estimate=pl.CostEstimate(flops=10**6, bytes_accessed=2 * 2**20, transcendentals=0),
+        cost_estimate=pl.CostEstimate(flops=1, bytes_accessed=1, transcendentals=0),
         name="route",
     )(meta, *ends)
 
@@ -603,7 +630,7 @@
         ),
         out_shape=[jax.ShapeDtypeStruct(o, t) for o, t in zip(outs, (F32, BF16, BF16))],
         compiler_params=pltpu.CompilerParams(vmem_limit_bytes=16 * 2**20),
-        cost_estimate=pl.CostEstimate(flops=10**6, bytes_accessed=3 * 2**20, transcendentals=0),
+        cost_estimate=pl.CostEstimate(flops=1, bytes_accessed=1, transcendentals=0),
         name="land",
     )(meta, *ends, crossed)
 
@@ -654,8 +681,9 @@
         jnp.transpose(pool_conv_bc, (1, 0, 2)),
         num_req,
     )
+    chosen, mark = run_choose(meta, mine, other, num_req)
+    conv, mark = lax.optimization_barrier((conv, mark))
     convs = [conv[0]] + [shifted(conv[by], "req", num_req, by) for by in range(1, num_req)]
-    chosen, mark = run_choose(meta, mine, other, num_req)
     got = [
         shifted(chosen[k : k + 1], "req", num_req, 2 * k + 2) for k in range(num_req // 2 - 1)
     ]
@@ -675,30 +703,18 @@
         slots,
     )
     states = [mine, other] + got
-    parts, squares = [], []
-    first = 0
-    for chunks in PIECES:
-        result = run_project(
-            first,
-            chunks,
-            meta,
-            states,
-            y_local,
-            gate_input,
-            cmap,
-            reach,
-            norm_gain[None, :],
-            pick,
-            out_weight,
-            num_tp,
-            num_req,
-        )
-        first += chunks
-        parts.append(tuple(result[:num_tp]))
-        squares.append(result[num_tp][0])
-        if len(states) > 1:
-            start = result[num_tp + 1]
-            states = [start]
+    operands = (y_local, gate_input, cmap, reach, norm_gain[None, :], pick, out_weight, num_tp, num_req)
+    soon, rest = (num_tp - 1, num_tp - 2), tuple(range(num_tp - 2))
+    first = run_project(0, PIECE, soon, (), meta, [mine, other] + got, [], *operands)
+    start, gated = first[3], first[4]
+    second = list(
+        run_project(PIECE, NCH - PIECE, rest + soon, rest, meta, [start], [gated], *operands)
+    )
+    parts = [second[num_tp : num_tp + len(rest)] + [first[1], first[0]], list(second[: len(rest)])]
+    parts[1] += [second[num_tp - 1], second[num_tp - 2]]
+    parts = [tuple(part) for part in parts]
+    result = {num_tp: second[-1]}
+    squares = [first[2][0], second[-1][0]]
     mark, summed = line_sums(parts, result[num_tp], num_tp)
     summed = jnp.concatenate(summed, axis=0)
 

time: 119 us -> 117 us (0.983)
  local copies, waits for them, and re-layouts: 5.63 us -> 9.58 us
  other arithmetic: 9.98 us -> 6.92 us
  waiting for transfers between devices: 29.8 us -> 27.2 us
  Pallas kernels: 32.5 us -> 31.2 us
    ppermute x12, waiting for transfers between devices: 27.4 us -> 20 us  [line_sums(): lax.ppermute(go, 'tp', [(k, k + 1), (size - 1 - k, size - 2 - k)])]
    unnamed x26 -> x48, local copies, waits for them, and re-layouts: 3.6 us -> 8.21 us
    ppermute x8, waiting for transfers between devices: 2.39 us -> 6.19 us  [shifted(): return lax.ppermute(x, axis, [(i, (i + by) % size) for i in range(size)])]
    add x2, other arithmetic: 2.91 us -> 0.66 us  [line_sums(): total += value.astype(F32)]
    pallas_call x1, Pallas kernels: 11.4 us -> 9.38 us  [run_scan(): pl.pallas_call(functools.partial(scan_kernel, heads, slots, reqs), grid_s...]
    ppermute x8, starting transfers between devices: 12.1 us -> 13.9 us  [shifted(): return lax.ppermute(x, axis, [(i, (i + by) % size) for i in range(size)])]
    ppermute x12, starting transfers between devices: 27 us -> 25.5 us  [line_sums(): lax.ppermute(go, 'tp', [(k, k + 1), (size - 1 - k, size - 2 - k)])]
  transfers between devices with their start and end apart: 22 -> 22, of which waited for: 8 -> 9; matrix products, arithmetic and copies ran while one was open for 8% -> 6% of each run, Pallas kernels for 21% -> 21%
where the time goes in v5:
time: 117 us; the launch traced here: 116 us
  starting transfers between devices  40 us (34%)
  Pallas kernels  31.2 us (27%)
  waiting for transfers between devices  27.2 us (23%)
  local copies, waits for them, and re-layouts  9.58 us (8%)
  other arithmetic  6.92 us (6%)
    ppermute x12, starting transfers between devices, line_sums(): lax.ppermute(go, 'tp', [(k, k + 1), (size - 1 - k, size - 2 - k)])  25.5 us
    ppermute x12, waiting for transfers between devices, line_sums(): lax.ppermute(go, 'tp', [(k, k + 1), (size - 1 - k, size - 2 - k)])  20 us
    pallas_call x2, Pallas kernels, run_project(): pl.pallas_call(functools.partial(project_kernel, chunks, shares, (reqs, s...  16.7 us
    ppermute x8, starting transfers between devices, shifted(): return lax.ppermute(x, axis, [(i, (i + by) % size) for i in range(size)])  13.9 us
    pallas_call x1, Pallas kernels, run_scan(): pl.pallas_call(functools.partial(scan_kernel, heads, slots, reqs), grid_s...  9.38 us
    unnamed x48, local copies, waits for them, and re-layouts  8.21 us
    ppermute x8, waiting for transfers between devices, shifted(): return lax.ppermute(x, axis, [(i, (i + by) % size) for i in range(size)])  6.19 us
    convert_element_type x6, other arithmetic, line_sums(): go = (go.astype(F32) + came[k - 1, d].astype(F32)).astype(BF16)  4.44 us
  transfers between devices with their start and end apart: 22, of which 9 were waited for; matrix products, arithmetic and copies ran while one was open for 6% of the time, Pallas kernels for 21%

profile of v5, /device:TPU:0, one launch (start us, length us, event | category | flops | bytes accessed | tf_op | source)
XLA Modules:
  0.0 116.0 jit_solution(4820347047364510030)
XLA Ops:
  5.1 1.6 %copy-done.3 = f32[2,32,64,128]{3,2,1,0:T(8,128)S(1)} copy-done((f32[2,32,64,128]{3,2,1,0:T(8,128)S(1)}, f32[2,32,64,128]{3,2,1,0:T(8,128)}, u32[]{:S(2)}) %copy-start.3) | copy-done | bytes 2097176
  8.5 2.7 %collective-permute-start.3 = (bf16[3,3072]{1,0:T(4,128)(2,1)S(1)}, bf16[3,3072]{1,0:T(4,128)(2,1)S(1)}, u32[]{:S(2)}, u32[]{:S(2)}) collective-permute-start(bf16[3,3072]{1,0:T(4,128)(2,1)S(1)} %get-tuple-element.51), channel_id=1, source_target_pairs={{0,8},{4,12},{8,0},{12,4},{1,9},{5,13},{9,1},{13,5},{2,10},{6,14},... | collective-permute-start | bytes 55304 | tf_op jit(solution)/shard_map/ppermute | solution.py:639
  11.1 1.3 %collective-permute-start.4 = (bf16[3,3072]{1,0:T(4,128)(2,1)S(1)}, bf16[3,3072]{1,0:T(4,128)(2,1)S(1)}, u32[]{:S(2)}, u32[]{:S(2)}) collective-permute-start(bf16[3,3072]{1,0:T(4,128)(2,1)S(1)} %get-tuple-element.52), channel_id=1, source_target_pairs={{0,12},{4,0},{8,4},{12,8},{1,13},{5,1},{9,5},{13,9},{2,14},{6,2},{... | collective-permute-start | bytes 55304 | tf_op jit(solution)/shard_map/ppermute | solution.py:639
  12.9 1.1 collective-permute-done.4.refs_3_
  14.1 9.4 %local_scan.1 = (bf16[512,2048]{1,0:T(8,128)(2,1)S(1)}, bf16[2048,128]{1,0:T(8,128)(2,1)S(1)}, bf16[512,128]{1,0:T(8,128)(2,1)S(1)}, bf16[512,128]{1,0:T(8,128)(...) custom-call(s32[18]{0:T(128)S(1)} %concatenate.9.meta, ...), custom_call_target="tpu_custom_call" | custom-call | flops 8000000000 | bytes 12582912 | tf_op jit(solution)/shard_map/local_scan/pallas_call | solution.py:301
  24.3 1.4 %collective-permute-done.1.refs_2_ = bf16[1,2048,128]{2,1,0:T(8,128)(2,1)S(1)} collective-permute-done((bf16[1,2048,128]{2,1,0:T(8,128)(2,1)S(1)}, bf16[1,2048,128]{2,1,0:T(8,128)(2,1)S(1)}, u32[]{:S(2)}, u32[]{:S(2)}) %collective-permute-start.1) | collective-permute-done | bytes 524320 | tf_op jit(solution)/shard_map/ppermute | solution.py:639
  25.7 6.3 %project.2 = (bf16[256,1024]{1,0:T(8,128)(2,1)}, bf16[256,1024]{1,0:T(8,128)(2,1)}, f32[8,256]{1,0:T(8,128)S(1)}, bf16[2048,128]{1,0:T(8,128)(2,1)S(1)}, bf16[256,2048]{1,0:T(8,128)(2,1)S(1)}) custom-call(s32[18]{0:T(128)S(1)} %concatenate.9.meta, f32[2,2048,128]{2,1,0:T(8,128)S(1)} %bitcast.15, f32[2,2048,128]{2,1,0:T(8,128)S(1)} %copy-done.6, ...), custom_call_target="tpu_custom_call" | custom-call | flops 1 | bytes 1 | tf_op jit(solution)/shard_map/project/pallas_call | solution.py:464
  33.1 4.3 %collective-permute-start.8 = (bf16[256,1024]{1,0:T(8,128)(2,1)}, bf16[256,1024]{1,0:T(8,128)(2,1)}, u32[]{:S(2)}, u32[]{:S(2)}) collective-permute-start(bf16[256,1024]{1,0:T(8,128)(2,1)} %get-tuple-element.63), channel_id=1, source_target_pairs={{0,1},{3,2},{4,5},{7,6},{8,9},{11,10},{12,13},{15,14},{16,17},{19,... | collective-permute-start | bytes 1572872 | tf_op jit(solution)/shard_map/ppermute | solution.py:507
  37.3 2.1 %collective-permute-start.6 = (bf16[256,1024]{1,0:T(8,128)(2,1)}, bf16[256,1024]{1,0:T(8,128)(2,1)}, u32[]{:S(2)}, u32[]{:S(2)}) collective-permute-start(bf16[256,1024]{1,0:T(8,128)(2,1)} %get-tuple-element.62), channel_id=1, source_target_pairs={{0,1},{3,2},{4,5},{7,6},{8,9},{11,10},{12,13},{15,14},{16,17},{19,... | collective-permute-start | bytes 1572872 | tf_op jit(solution)/shard_map/ppermute | solution.py:507
  40.0 1.6 %copy-done.2 = bf16[512,2048]{1,0:T(8,128)(2,1)S(1)} copy-done((bf16[512,2048]{1,0:T(8,128)(2,1)S(1)}, bf16[512,2048]{1,0:T(8,128)(2,1)}, u32[]{:S(2)}) %copy-start.2) | copy-done | bytes 2097176
  41.6 1.2 %copy-done.12 = bf16[256,2048]{1,0:T(8,128)(2,1)S(1)} copy-done((bf16[256,2048]{1,0:T(8,128)(2,1)S(1)}, bf16[256,2048]{1,0:T(8,128)(2,1)}, u32[]{:S(2)}) %copy-start.12) | copy-done | bytes 1048600
  42.8 10.3 %project.3 = (bf16[256,1024]{1,0:T(8,128)(2,1)S(1)}, bf16[256,1024]{1,0:T(8,128)(2,1)S(1)}, bf16[256,1024]{1,0:T(8,128)(2,1)S(1)}, bf16[256,1024]{1,0:T(8,128)(2...) custom-call(s32[18]{0:T(128)S(1)} %concatenate.9.meta, ...), custom_call_target="tpu_custom_call" | custom-call | flops 1 | bytes 1 | tf_op jit(solution)/shard_map/project/pallas_call | solution.py:464
  53.3 2.5 %collective-permute-start.19 = (f32[512]{0:T(512)S(1)}, f32[512]{0:T(512)S(1)}, u32[]{:S(2)}, u32[]{:S(2)}) collective-permute-start(f32[512]{0:T(512)S(1)} %pad_maximum_fusion), channel_id=1, source_target_pairs={{0,3},{1,0},{2,1},{3,2},{4,7},{5,4},{6,5},{7,6},{8,11},{9,8},{10,9... | collective-permute-start | bytes 6152 | tf_op jit(solution)/shard_map/ppermute | solution.py:639
  55.8 2.4 %collective-permute-start.14 = (bf16[256,1024]{1,0:T(8,128)(2,1)S(1)}, bf16[256,1024]{1,0:T(8,128)(2,1)S(1)}, u32[]{:S(2)}, u32[]{:S(2)}) collective-permute-start(bf16[256,1024]{1,0:T(8,128)(2,1)S(1)} %get-tuple-element.73), channel_id=1, source_target_pairs={{0,1},{3,2},{4,5},{7,6},{8,9},{11,10},{12,13},{15,14},{16,17},{19,... | collective-permute-start | bytes 1572872 | tf_op jit(solution)/shard_map/ppermute | solution.py:507
  58.3 1.4 %add_convert_fusion.4 = bf16[256,1024]{1,0:T(8,128)(2,1)S(1)} fusion(bf16[256,1024]{1,0:T(8,128)(2,1)} %collective-permute-done.8, bf16[256,1024]{1,0:T(8,128)(2,1)} %get-tuple-element.62), kind=kLoop, calls=%fused_computation.8 | loop fusion | flops 1048576 | bytes 1572864 | tf_op jit(solution)/shard_map/convert_element_type | solution.py:506
  60.6 1.2 %ending.1.refs_0_ = bf16[2432,128]{1,0:T(8,128)(2,1)S(1)} custom-call(s32[18]{0:T(128)S(1)} %concatenate.9.meta, f32[8,256]{1,0:T(8,128)S(1)} %get-tuple-element.75.mark_ref, bf16[2048,128]{1,0:T(8,128)(2,1)S(1)} %copy-done.14, bf16[2048,128]{1,0:T(8,128)(2,1)S(1)} %get-tuple-element.58.refs_0_.start_ref, bf16[16,128]{1,0:T(8,128)(2,1)S(1)} %get-tuple-element.77.total_ref, ...), custom_call_target="tpu_custom_call" | custom-call | flops 1 | bytes 1 | tf_op jit(solution)/shard_map/ending/pallas_call | solution.py:557
  61.8 1.3 %collective-permute-start.20 = (bf16[2432,128]{1,0:T(8,128)(2,1)S(1)}, bf16[2432,128]{1,0:T(8,128)(2,1)S(1)}, u32[]{:S(2)}, u32[]{:S(2)}) collective-permute-start(bf16[2432,128]{1,0:T(8,128)(2,1)S(1)} %ending.1.refs_0_), channel_id=1, source_target_pairs={{0,8},{4,12},{8,0},{12,4},{1,9},{5,13},{9,1},{13,5},{2,10},{6,14},... | collective-permute-start | bytes 1867784 | tf_op jit(solution)/shard_map/ppermute | solution.py:639
  63.1 1.2 %add_convert_fusion.5 = bf16[256,1024]{1,0:T(8,128)(2,1)S(1)} fusion(bf16[256,1024]{1,0:T(8,128)(2,1)} %collective-permute-done.6, bf16[256,1024]{1,0:T(8,128)(2,1)S(1)} %get-tuple-element.61), kind=kLoop, calls=%fused_computation.9 | loop fusion | flops 1048576 | bytes 1572864 | tf_op jit(solution)/shard_map/convert_element_type | solution.py:506
  64.3 5.8 %collective-permute-done.14 = bf16[256,1024]{1,0:T(8,128)(2,1)S(1)} collective-permute-done((bf16[256,1024]{1,0:T(8,128)(2,1)S(1)}, bf16[256,1024]{1,0:T(8,128)(2,1)S(1)}, u32[]{:S(2)}, u32[]{:S(2)}) %collective-permute-start.14) | collective-permute-done | bytes 524320 | tf_op jit(solution)/shard_map/ppermute | solution.py:507
  70.2 4.4 %collective-permute-start.12 = (bf16[256,1024]{1,0:T(8,128)(2,1)S(1)}, bf16[256,1024]{1,0:T(8,128)(2,1)S(1)}, u32[]{:S(2)}, u32[]{:S(2)}) collective-permute-start(bf16[256,1024]{1,0:T(8,128)(2,1)S(1)} %get-tuple-element.72), channel_id=1, source_target_pairs={{0,1},{3,2},{4,5},{7,6},{8,9},{11,10},{12,13},{15,14},{16,17},{19,... | collective-permute-start | bytes 1572872 | tf_op jit(solution)/shard_map/ppermute | solution.py:507
  75.5 1.2 %add_convert_fusion.3 = bf16[256,1024]{1,0:T(8,128)(2,1)S(1)} fusion(bf16[256,1024]{1,0:T(8,128)(2,1)S(1)} %collective-permute-done.9, bf16[256,1024]{1,0:T(8,128)(2,1)} %get-tuple-element.63), kind=kLoop, calls=%fused_computation.7 | loop fusion | flops 1048576 | bytes 1572864 | tf_op jit(solution)/shard_map/convert_element_type | solution.py:506
  76.8 4.1 %collective-permute-start.5 = (bf16[256,1024]{1,0:T(8,128)(2,1)S(1)}, bf16[256,1024]{1,0:T(8,128)(2,1)S(1)}, u32[]{:S(2)}, u32[]{:S(2)}) collective-permute-start(bf16[256,1024]{1,0:T(8,128)(2,1)S(1)} %get-tuple-element.61), channel_id=1, source_target_pairs={{0,1},{3,2},{4,5},{7,6},{8,9},{11,10},{12,13},{15,14},{16,17},{19,... | collective-permute-start | bytes 1572872 | tf_op jit(solution)/shard_map/ppermute | solution.py:507
  80.8 6.1 %collective-permute-done.12 = bf16[256,1024]{1,0:T(8,128)(2,1)S(1)} collective-permute-done((bf16[256,1024]{1,0:T(8,128)(2,1)S(1)}, bf16[256,1024]{1,0:T(8,128)(2,1)S(1)}, u32[]{:S(2)}, u32[]{:S(2)}) %collective-permute-start.12) | collective-permute-done | bytes 524320 | tf_op jit(solution)/shard_map/ppermute | solution.py:507
  87.6 1.3 %collective-permute-start.10 = (bf16[256,1024]{1,0:T(8,128)(2,1)S(1)}, bf16[256,1024]{1,0:T(8,128)(2,1)S(1)}, u32[]{:S(2)}, u32[]{:S(2)}) collective-permute-start(bf16[256,1024]{1,0:T(8,128)(2,1)S(1)} %add_convert_fusion.3), channel_id=1, source_target_pairs={{2,3},{1,0},{6,7},{5,4},{10,11},{9,8},{14,15},{13,12},{18,19},{17,... | collective-permute-start | bytes 1572872 | tf_op jit(solution)/shard_map/ppermute | solution.py:507
  89.8 5.3 %collective-permute-start.17 = (f32[512]{0:T(512)S(1)}, f32[512]{0:T(512)S(1)}, u32[]{:S(2)}, u32[]{:S(2)}) collective-permute-start(f32[512]{0:T(512)S(1)} %pad_maximum_fusion), channel_id=1, source_target_pairs={{0,1},{1,2},{2,3},{3,0},{4,5},{5,6},{6,7},{7,4},{8,9},{9,10},{10,1... | collective-permute-start | bytes 6152 | tf_op jit(solution)/shard_map/ppermute | solution.py:639
  95.4 3.5 %collective-permute-done.17 = f32[512]{0:T(512)S(1)} collective-permute-done((f32[512]{0:T(512)S(1)}, f32[512]{0:T(512)S(1)}, u32[]{:S(2)}, u32[]{:S(2)}) %collective-permute-start.17) | collective-permute-done | bytes 2080 | tf_op jit(solution)/shard_map/ppermute | solution.py:639
  98.9 2.7 %collective-permute-start.11 = (bf16[256,1024]{1,0:T(8,128)(2,1)S(1)}, bf16[256,1024]{1,0:T(8,128)(2,1)S(1)}, u32[]{:S(2)}, u32[]{:S(2)}) collective-permute-start(bf16[256,1024]{1,0:T(8,128)(2,1)S(1)} %get-tuple-element.71), channel_id=1, source_target_pairs={{0,1},{3,2},{4,5},{7,6},{8,9},{11,10},{12,13},{15,14},{16,17},{19,... | collective-permute-start | bytes 1572872 | tf_op jit(solution)/shard_map/ppermute | solution.py:507
  102.4 1.3 %collective-permute-start.16 = (bf16[256,1024]{1,0:T(8,128)(2,1)S(1)}, bf16[256,1024]{1,0:T(8,128)(2,1)S(1)}, u32[]{:S(2)}, u32[]{:S(2)}) collective-permute-start(bf16[256,1024]{1,0:T(8,128)(2,1)S(1)} %add_convert_fusion), channel_id=1, source_target_pairs={{2,3},{1,0},{6,7},{5,4},{10,11},{9,8},{14,15},{13,12},{18,19},{17,... | collective-permute-start | bytes 1572872 | tf_op jit(solution)/shard_map/ppermute | solution.py:507
  104.7 1.7 %land.1 = (f32[2048,128]{1,0:T(8,128)}, bf16[3,2048]{1,0:T(4,128)(2,1)}, bf16[3,1024]{1,0:T(4,128)(2,1)}) custom-call(s32[18]{0:T(128)S(1)} %concatenate.9.meta, bf16[2432,128]{1,0:T(8,128)(2,1)S(1)} %ending.1.refs_0_, bf16[2432,128]{1,0:T(8,128)(2,1)S(1)} %collective-permute-done.20.refs_1_, bf16[2432,128]{1,0:T(8,128)(2,1)S(1)} %collective-permute-done.21.refs_2_), custom_call_target="tpu_custom_call" | custom-call | flops 1 | bytes 1 | tf_op jit(solution)/shard_map/land/pallas_call | solution.py:623
  106.4 3.2 %collective-permute-done.11 = bf16[256,1024]{1,0:T(8,128)(2,1)S(1)} collective-permute-done((bf16[256,1024]{1,0:T(8,128)(2,1)S(1)}, bf16[256,1024]{1,0:T(8,128)(2,1)S(1)}, u32[]{:S(2)}, u32[]{:S(2)}) %collective-permute-start.11) | collective-permute-done | bytes 524320 | tf_op jit(solution)/shard_map/ppermute | solution.py:507
  109.6 4.9 %collective-permute-done.16 = bf16[256,1024]{1,0:T(8,128)(2,1)S(1)} collective-permute-done((bf16[256,1024]{1,0:T(8,128)(2,1)S(1)}, bf16[256,1024]{1,0:T(8,128)(2,1)S(1)}, u32[]{:S(2)}, u32[]{:S(2)}) %collective-permute-start.16) | collective-permute-done | bytes 524320 | tf_op jit(solution)/shard_map/ppermute | solution.py:507
  114.8 1.1 fusion
  (83 shorter events, 14.7 us)
Async XLA Ops:
  0.6 4.5 %collective-permute-start = (f32[2,2048,128]{2,1,0:T(8,128)}, f32[2,2048,128]{2,1,0:T(8,128)S(1)}, u32[]{:S(2)}, u32[]{:S(2)}) collective-permute-start(f32[2,2048,128]{2,1,0:T(8,128)} %bitcast.13), channel_id=1, source_target_pairs={{0,4},{4,0},{8,12},{12,8},{1,5},{5,1},{9,13},{13,9},{2,6},{6,2},{1... | collective-permute-start | bytes 6291464 | tf_op jit(solution)/shard_map/ppermute | solution.py:643
  6.7 7.2 %copy-start.18 = (f32[512,32]{0,1:T(8,128)S(1)}, f32[512,32]{0,1:T(8,128)}, u32[]{:S(2)}) copy-start(f32[512,32]{0,1:T(8,128)} %param.20) | copy-start | bytes 196612
  8.1 4.7 %collective-permute-start.2 = (bf16[3,3072]{1,0:T(4,128)(2,1)S(1)}, bf16[3,3072]{1,0:T(4,128)(2,1)S(1)}, u32[]{:S(2)}, u32[]{:S(2)}) collective-permute-start(bf16[3,3072]{1,0:T(4,128)(2,1)S(1)} %get-tuple-element.50), channel_id=1, source_target_pairs={{0,4},{4,8},{8,12},{12,0},{1,5},{5,9},{9,13},{13,1},{2,6},{6,10},{... | collective-permute-start | bytes 55304 | tf_op jit(solution)/shard_map/ppermute | solution.py:639
  8.5 4.5 %collective-permute-start.3 = (bf16[3,3072]{1,0:T(4,128)(2,1)S(1)}, bf16[3,3072]{1,0:T(4,128)(2,1)S(1)}, u32[]{:S(2)}, u32[]{:S(2)}) collective-permute-start(bf16[3,3072]{1,0:T(4,128)(2,1)S(1)} %get-tuple-element.51), channel_id=1, source_target_pairs={{0,8},{4,12},{8,0},{12,4},{1,9},{5,13},{9,1},{13,5},{2,10},{6,14},... | collective-permute-start | bytes 55304 | tf_op jit(solution)/shard_map/ppermute | solution.py:639
  11.1 2.9 %collective-permute-start.4 = (bf16[3,3072]{1,0:T(4,128)(2,1)S(1)}, bf16[3,3072]{1,0:T(4,128)(2,1)S(1)}, u32[]{:S(2)}, u32[]{:S(2)}) collective-permute-start(bf16[3,3072]{1,0:T(4,128)(2,1)S(1)} %get-tuple-element.52), channel_id=1, source_target_pairs={{0,12},{4,0},{8,4},{12,8},{1,13},{5,1},{9,5},{13,9},{2,14},{6,2},{... | collective-permute-start | bytes 55304 | tf_op jit(solution)/shard_map/ppermute | solution.py:639
  12.4 13.3 %collective-permute-start.1 = (bf16[1,2048,128]{2,1,0:T(8,128)(2,1)S(1)}, bf16[1,2048,128]{2,1,0:T(8,128)(2,1)S(1)}, u32[]{:S(2)}, u32[]{:S(2)}) collective-permute-start(bf16[1,2048,128]{2,1,0:T(8,128)(2,1)S(1)} %get-tuple-element.43), channel_id=1, source_target_pairs={{0,8},{4,12},{8,0},{12,4},{1,9},{5,13},{9,1},{13,5},{2,10},{6,14},... | collective-permute-start | bytes 1572872 | tf_op jit(solution)/shard_map/ppermute | solution.py:639
  14.0 11.7 %copy-start = (bf16[512,2048]{1,0:T(8,128)(2,1)S(1)}, bf16[512,2048]{1,0:T(8,128)(2,1)}, u32[]{:S(2)}) copy-start(bf16[512,2048]{1,0:T(8,128)(2,1)} %refs_3_.1) | copy-start | bytes 6291460
  14.0 11.7 %copy-start.4 = (f32[2,32,64,128]{3,2,1,0:T(8,128)S(1)}, f32[2,32,64,128]{3,2,1,0:T(8,128)}, u32[]{:S(2)}) copy-start(f32[2,32,64,128]{3,2,1,0:T(8,128)} %param.27) | copy-start | bytes 6291460
  14.0 11.7 %copy-start.6 = (f32[2,2048,128]{2,1,0:T(8,128)S(1)}, f32[2,2048,128]{2,1,0:T(8,128)}, u32[]{:S(2)}) copy-start(f32[2,2048,128]{2,1,0:T(8,128)} %copy-done.5) | copy-start | bytes 6291460
  14.1 11.7 %copy-start.15 = (f32[2048]{0:T(1024)S(1)}, f32[2048]{0:T(1024)}, u32[]{:S(2)}) copy-start(f32[2048]{0:T(1024)} %param.23) | copy-start | bytes 24580
  24.3 7.8 %copy-start.1 = (bf16[512,2048]{1,0:T(8,128)(2,1)}, bf16[512,2048]{1,0:T(8,128)(2,1)S(1)}, u32[]{:S(2)}) copy-start(bf16[512,2048]{1,0:T(8,128)(2,1)S(1)} %get-tuple-element.54.refs_3_.refs_2_) | copy-start | bytes 6291460
  25.7 13.7 %copy-start.23 = (s32[4]{0:T(128)S(1)}, s32[4]{0:T(128)}, u32[]{:S(2)}) copy-start(s32[4]{0:T(128)} %param.33) | copy-start | bytes 52
  33.1 22.8 %collective-permute-start.8 = (bf16[256,1024]{1,0:T(8,128)(2,1)}, bf16[256,1024]{1,0:T(8,128)(2,1)}, u32[]{:S(2)}, u32[]{:S(2)}) collective-permute-start(bf16[256,1024]{1,0:T(8,128)(2,1)} %get-tuple-element.63), channel_id=1, source_target_pairs={{0,1},{3,2},{4,5},{7,6},{8,9},{11,10},{12,13},{15,14},{16,17},{19,... | collective-permute-start | bytes 1572872 | tf_op jit(solution)/shard_map/ppermute | solution.py:507
  37.3 24.4 %collective-permute-start.6 = (bf16[256,1024]{1,0:T(8,128)(2,1)}, bf16[256,1024]{1,0:T(8,128)(2,1)}, u32[]{:S(2)}, u32[]{:S(2)}) collective-permute-start(bf16[256,1024]{1,0:T(8,128)(2,1)} %get-tuple-element.62), channel_id=1, source_target_pairs={{0,1},{3,2},{4,5},{7,6},{8,9},{11,10},{12,13},{15,14},{16,17},{19,... | collective-permute-start | bytes 1572872 | tf_op jit(solution)/shard_map/ppermute | solution.py:507
  42.8 17.7 %copy-start.8 = (bf16[512,2048]{1,0:T(8,128)(2,1)S(1)}, bf16[512,2048]{1,0:T(8,128)(2,1)}, u32[]{:S(2)}) copy-start(bf16[512,2048]{1,0:T(8,128)(2,1)} %x_ref.1) | copy-start | bytes 6291460
  42.8 17.7 %copy-start.14 = (bf16[2048,128]{1,0:T(8,128)(2,1)S(1)}, bf16[2048,128]{1,0:T(8,128)(2,1)}, u32[]{:S(2)}) copy-start(bf16[2048,128]{1,0:T(8,128)(2,1)} %copy-done.13) | copy-start | bytes 1572868
  53.2 7.4 %copy-start.10 = (bf16[512,1024]{1,0:T(8,128)(2,1)S(1)}, bf16[512,1024]{1,0:T(8,128)(2,1)}, u32[]{:S(2)}) copy-start(bf16[512,1024]{1,0:T(8,128)(2,1)} %bc_ref.1) | copy-start | bytes 3145732
  53.2 23.5 %collective-permute-start.18 = (f32[512]{0:T(512)S(1)}, f32[512]{0:T(512)S(1)}, u32[]{:S(2)}, u32[]{:S(2)}) collective-permute-start(f32[512]{0:T(512)S(1)} %pad_maximum_fusion), channel_id=1, source_target_pairs={{0,2},{1,3},{2,0},{3,1},{4,6},{5,7},{6,4},{7,5},{8,10},{9,11},{10,... | collective-permute-start | bytes 6152 | tf_op jit(solution)/shard_map/ppermute | solution.py:639
  53.3 36.5 %collective-permute-start.19 = (f32[512]{0:T(512)S(1)}, f32[512]{0:T(512)S(1)}, u32[]{:S(2)}, u32[]{:S(2)}) collective-permute-start(f32[512]{0:T(512)S(1)} %pad_maximum_fusion), channel_id=1, source_target_pairs={{0,3},{1,0},{2,1},{3,2},{4,7},{5,4},{6,5},{7,6},{8,11},{9,8},{10,9... | collective-permute-start | bytes 6152 | tf_op jit(solution)/shard_map/ppermute | solution.py:639
  55.8 14.3 %collective-permute-start.14 = (bf16[256,1024]{1,0:T(8,128)(2,1)S(1)}, bf16[256,1024]{1,0:T(8,128)(2,1)S(1)}, u32[]{:S(2)}, u32[]{:S(2)}) collective-permute-start(bf16[256,1024]{1,0:T(8,128)(2,1)S(1)} %get-tuple-element.73), channel_id=1, source_target_pairs={{0,1},{3,2},{4,5},{7,6},{8,9},{11,10},{12,13},{15,14},{16,17},{19,... | collective-permute-start | bytes 1572872 | tf_op jit(solution)/shard_map/ppermute | solution.py:507
  59.7 15.1 %collective-permute-start.9 = (bf16[256,1024]{1,0:T(8,128)(2,1)S(1)}, bf16[256,1024]{1,0:T(8,128)(2,1)S(1)}, u32[]{:S(2)}, u32[]{:S(2)}) collective-permute-start(bf16[256,1024]{1,0:T(8,128)(2,1)S(1)} %add_convert_fusion.4), channel_id=1, source_target_pairs={{1,2},{2,1},{5,6},{6,5},{9,10},{10,9},{13,14},{14,13},{17,18},{18,... | collective-permute-start | bytes 1572872 | tf_op jit(solution)/shard_map/ppermute | solution.py:507
  61.8 25.8 %collective-permute-start.20 = (bf16[2432,128]{1,0:T(8,128)(2,1)S(1)}, bf16[2432,128]{1,0:T(8,128)(2,1)S(1)}, u32[]{:S(2)}, u32[]{:S(2)}) collective-permute-start(bf16[2432,128]{1,0:T(8,128)(2,1)S(1)} %ending.1.refs_0_), channel_id=1, source_target_pairs={{0,8},{4,12},{8,0},{12,4},{1,9},{5,13},{9,1},{13,5},{2,10},{6,14},... | collective-permute-start | bytes 1867784 | tf_op jit(solution)/shard_map/ppermute | solution.py:639
  70.2 16.7 %collective-permute-start.12 = (bf16[256,1024]{1,0:T(8,128)(2,1)S(1)}, bf16[256,1024]{1,0:T(8,128)(2,1)S(1)}, u32[]{:S(2)}, u32[]{:S(2)}) collective-permute-start(bf16[256,1024]{1,0:T(8,128)(2,1)S(1)} %get-tuple-element.72), channel_id=1, source_target_pairs={{0,1},{3,2},{4,5},{7,6},{8,9},{11,10},{12,13},{15,14},{16,17},{19,... | collective-permute-start | bytes 1572872 | tf_op jit(solution)/shard_map/ppermute | solution.py:507
  74.8 20.4 %collective-permute-start.15 = (bf16[256,1024]{1,0:T(8,128)(2,1)S(1)}, bf16[256,1024]{1,0:T(8,128)(2,1)S(1)}, u32[]{:S(2)}, u32[]{:S(2)}) collective-permute-start(bf16[256,1024]{1,0:T(8,128)(2,1)S(1)} %add_convert_fusion.1), channel_id=1, source_target_pairs={{1,2},{2,1},{5,6},{6,5},{9,10},{10,9},{13,14},{14,13},{17,18},{18,... | collective-permute-start | bytes 1572872 | tf_op jit(solution)/shard_map/ppermute | solution.py:507
  76.8 24.9 %collective-permute-start.5 = (bf16[256,1024]{1,0:T(8,128)(2,1)S(1)}, bf16[256,1024]{1,0:T(8,128)(2,1)S(1)}, u32[]{:S(2)}, u32[]{:S(2)}) collective-permute-start(bf16[256,1024]{1,0:T(8,128)(2,1)S(1)} %get-tuple-element.61), channel_id=1, source_target_pairs={{0,1},{3,2},{4,5},{7,6},{8,9},{11,10},{12,13},{15,14},{16,17},{19,... | collective-permute-start | bytes 1572872 | tf_op jit(solution)/shard_map/ppermute | solution.py:507
  86.9 15.5 %collective-permute-start.7 = (bf16[256,1024]{1,0:T(8,128)(2,1)S(1)}, bf16[256,1024]{1,0:T(8,128)(2,1)S(1)}, u32[]{:S(2)}, u32[]{:S(2)}) collective-permute-start(bf16[256,1024]{1,0:T(8,128)(2,1)S(1)} %add_convert_fusion.5), channel_id=1, source_target_pairs={{1,2},{2,1},{5,6},{6,5},{9,10},{10,9},{13,14},{14,13},{17,18},{18,... | collective-permute-start | bytes 1572872 | tf_op jit(solution)/shard_map/ppermute | solution.py:507
  87.6 16.7 %collective-permute-start.10 = (bf16[256,1024]{1,0:T(8,128)(2,1)S(1)}, bf16[256,1024]{1,0:T(8,128)(2,1)S(1)}, u32[]{:S(2)}, u32[]{:S(2)}) collective-permute-start(bf16[256,1024]{1,0:T(8,128)(2,1)S(1)} %add_convert_fusion.3), channel_id=1, source_target_pairs={{2,3},{1,0},{6,7},{5,4},{10,11},{9,8},{14,15},{13,12},{18,19},{17,... | collective-permute-start | bytes 1572872 | tf_op jit(solution)/shard_map/ppermute | solution.py:507
  89.8 9.1 %collective-permute-start.17 = (f32[512]{0:T(512)S(1)}, f32[512]{0:T(512)S(1)}, u32[]{:S(2)}, u32[]{:S(2)}) collective-permute-start(f32[512]{0:T(512)S(1)} %pad_maximum_fusion), channel_id=1, source_target_pairs={{0,1},{1,2},{2,3},{3,0},{4,5},{5,6},{6,7},{7,4},{8,9},{9,10},{10,1... | collective-permute-start | bytes 6152 | tf_op jit(solution)/shard_map/ppermute | solution.py:639
  95.2 9.5 %collective-permute-start.21 = (bf16[2432,128]{1,0:T(8,128)(2,1)S(1)}, bf16[2432,128]{1,0:T(8,128)(2,1)S(1)}, u32[]{:S(2)}, u32[]{:S(2)}) collective-permute-start(bf16[2432,128]{1,0:T(8,128)(2,1)S(1)} %route.1), channel_id=1, source_target_pairs={{0,4},{4,0},{8,12},{12,8},{1,5},{5,1},{9,13},{13,9},{2,6},{6,2},{1... | collective-permute-start | bytes 1867784 | tf_op jit(solution)/shard_map/ppermute | solution.py:643
  98.9 10.7 %collective-permute-start.11 = (bf16[256,1024]{1,0:T(8,128)(2,1)S(1)}, bf16[256,1024]{1,0:T(8,128)(2,1)S(1)}, u32[]{:S(2)}, u32[]{:S(2)}) collective-permute-start(bf16[256,1024]{1,0:T(8,128)(2,1)S(1)} %get-tuple-element.71), channel_id=1, source_target_pairs={{0,1},{3,2},{4,5},{7,6},{8,9},{11,10},{12,13},{15,14},{16,17},{19,... | collective-permute-start | bytes 1572872 | tf_op jit(solution)/shard_map/ppermute | solution.py:507
  101.7 7.9 %collective-permute-start.13 = (bf16[256,1024]{1,0:T(8,128)(2,1)S(1)}, bf16[256,1024]{1,0:T(8,128)(2,1)S(1)}, u32[]{:S(2)}, u32[]{:S(2)}) collective-permute-start(bf16[256,1024]{1,0:T(8,128)(2,1)S(1)} %add_convert_fusion.2), channel_id=1, source_target_pairs={{1,2},{2,1},{5,6},{6,5},{9,10},{10,9},{13,14},{14,13},{17,18},{18,... | collective-permute-start | bytes 1572872 | tf_op jit(solution)/shard_map/ppermute | solution.py:507
  102.4 12.1 %collective-permute-start.16 = (bf16[256,1024]{1,0:T(8,128)(2,1)S(1)}, bf16[256,1024]{1,0:T(8,128)(2,1)S(1)}, u32[]{:S(2)}, u32[]{:S(2)}) collective-permute-start(bf16[256,1024]{1,0:T(8,128)(2,1)S(1)} %add_convert_fusion), channel_id=1, source_target_pairs={{2,3},{1,0},{6,7},{5,4},{10,11},{9,8},{14,15},{13,12},{18,19},{17,... | collective-permute-start | bytes 1572872 | tf_op jit(solution)/shard_map/ppermute | solution.py:507
  (14 other events, 52.4 us)

commit v6 on v5

--- a/solution.py
+++ b/solution.py
@@ -344,8 +344,6 @@
         refs = refs[2 + others :]
     else:
         start_ref, refs = refs[0], refs[1:]
-    if late:
-        before_ref, refs = refs[0], refs[1:]
     y_ref, gate_ref, cmap_ref, reach_ref, gain_ref, pick_ref, w_ref = refs[:7]
     out_refs = refs[7 : 7 + len(emit)]
     late_refs = refs[7 + len(emit) : 7 + len(emit) + len(late)]
@@ -409,22 +407,23 @@
         @pl.when(step == chunks + i)
         def _(i=i):
             fetch(i).wait()
-            out_refs[i][...] = dot(held[...], w_held[i % AHEAD]).astype(BF16)
+            done = held.shape[0] - out_refs[i].shape[0]
+            out_refs[i][...] = dot(held[done:], w_held[i % AHEAD]).astype(BF16)
             if emit[i] in late:
                 late_refs[late.index(emit[i])][...] = dot(
-                    before_ref[...], w_held[i % AHEAD]
+                    held[:done], w_held[i % AHEAD]
                 ).astype(BF16)
             if i + AHEAD < len(emit):
                 fetch(i + AHEAD).start()
 
 
 def run_project(
-    first, chunks, emit, late, meta, states, before, y, gate, cmap, reach, gain, pick, weight, shares, reqs
+    done, chunks, emit, late, meta, states, y, gate, cmap, reach, gain, pick, weight, shares, reqs
 ):
     inner, width = weight.shape
     share = width // shares
-    count = chunks * SPAN
-    rows = lambda n, m: (first + jnp.minimum(n, chunks - 1), 0)
+    count = (chunks - done) * SPAN
+    rows = lambda n, m: (jnp.minimum(n, chunks - 1), 0)
     whole = lambda n, m: (0, 0)
     state = (1, inner, STATE)
     choose = len(states) > 1
@@ -445,22 +444,14 @@
         pl.BlockSpec((count, share), whole)
         for q in emit
     ]
-    out_specs += [pl.BlockSpec((first * SPAN, share), whole) for q in late]
+    out_specs += [pl.BlockSpec((done * SPAN, share), whole) for q in late]
     out_specs += [pl.BlockSpec((8, LANES), lambda n, m: (0, jnp.minimum(n, chunks - 1)))]
     out_shape = [jax.ShapeDtypeStruct((count, share), BF16)] * len(emit)
-    out_shape += [jax.ShapeDtypeStruct((first * SPAN, share), BF16)] * len(late)
-    out_shape.append(jax.ShapeDtypeStruct((8, count), F32))
+    out_shape += [jax.ShapeDtypeStruct((done * SPAN, share), BF16)] * len(late)
+    out_shape.append(jax.ShapeDtypeStruct((8, chunks * SPAN), F32))
     if choose:
         out_specs.append(pl.BlockSpec((inner, STATE), whole))
         out_shape.append(jax.ShapeDtypeStruct((inner, STATE), BF16))
-    gated = jax.ShapeDtypeStruct((count, inner), BF16)
-    scratch = []
-    if late:
-        state_specs.append(pl.BlockSpec(before[0].shape, whole, pipeline_mode=single))
-        scratch.append(pltpu.VMEM(gated.shape, BF16))
-    else:
-        out_specs.append(pl.BlockSpec(gated.shape, whole))
-        out_shape.append(gated)
     return pl.pallas_call(
         functools.partial(project_kernel, chunks, shares, (reqs, slots) if choose else None, emit, late),
         grid_spec=pltpu.PrefetchScalarGridSpec(
@@ -477,8 +468,8 @@
                 pl.BlockSpec(memory_space=pl.ANY),
             ],
             out_specs=out_specs,
-            scratch_shapes=scratch
-            + [
+            scratch_shapes=[
+                pltpu.VMEM((chunks * SPAN, inner), BF16),
                 pltpu.VMEM((AHEAD, inner, share), BF16),
                 pltpu.SemaphoreType.DMA((AHEAD,)),
             ],
@@ -489,7 +480,7 @@
         ),
         cost_estimate=pl.CostEstimate(flops=1, bytes_accessed=1, transcendentals=0),
         name="project",
-    )(meta, *states, *before, y, gate, cmap, reach, gain, pick, weight)
+    )(meta, *states, y, gate, cmap, reach, gain, pick, weight)
 
 
 def line_sums(parts, mark, size):
@@ -682,7 +673,6 @@
         num_req,
     )
     chosen, mark = run_choose(meta, mine, other, num_req)
-    conv, mark = lax.optimization_barrier((conv, mark))
     convs = [conv[0]] + [shifted(conv[by], "req", num_req, by) for by in range(1, num_req)]
     got = [
         shifted(chosen[k : k + 1], "req", num_req, 2 * k + 2) for k in range(num_req // 2 - 1)
@@ -705,21 +695,18 @@
     states = [mine, other] + got
     operands = (y_local, gate_input, cmap, reach, norm_gain[None, :], pick, out_weight, num_tp, num_req)
     soon, rest = (num_tp - 1, num_tp - 2), tuple(range(num_tp - 2))
-    first = run_project(0, PIECE, soon, (), meta, [mine, other] + got, [], *operands)
-    start, gated = first[3], first[4]
-    second = list(
-        run_project(PIECE, NCH - PIECE, rest + soon, rest, meta, [start], [gated], *operands)
-    )
+    first = run_project(0, PIECE, soon, (), meta, [mine, other] + got, *operands)
+    start = first[3]
+    second = list(run_project(PIECE, NCH, rest + soon, rest, meta, [start], *operands))
     parts = [second[num_tp : num_tp + len(rest)] + [first[1], first[0]], list(second[: len(rest)])]
     parts[1] += [second[num_tp - 1], second[num_tp - 2]]
     parts = [tuple(part) for part in parts]
     result = {num_tp: second[-1]}
-    squares = [first[2][0], second[-1][0]]
     mark, summed = line_sums(parts, result[num_tp], num_tp)
     summed = jnp.concatenate(summed, axis=0)
 
     my_len = suffix_len[me]
-    square = jnp.concatenate(squares)
+    square = second[-1][0]
     square_total = square
     for by in range(1, num_tp):
         square_total = square_total + shifted(square, "tp", num_tp, by)

time: 117 us -> 115 us (0.983)
  starting transfers between devices: 40 us -> 36.1 us
  waiting for transfers between devices: 27.2 us -> 29.7 us
  local copies, waits for them, and re-layouts: 9.58 us -> 8.2 us
    ppermute x8, waiting for transfers between devices: 6.19 us -> 10.7 us  [shifted(): return lax.ppermute(x, axis, [(i, (i + by) % size) for i in range(size)])]
    ppermute x8, starting transfers between devices: 13.9 us -> 9.57 us  [shifted(): return lax.ppermute(x, axis, [(i, (i + by) % size) for i in range(size)])]
    unnamed x48 -> x44, local copies, waits for them, and re-layouts: 8.21 us -> 6.83 us
  transfers between devices with their start and end apart: 22 -> 22, of which waited for: 9 -> 6; matrix products, arithmetic and copies ran while one was open for 6% -> 6% of each run, Pallas kernels for 21% -> 23%
where the time goes in v6:
time: 115 us; the launch traced here: 114 us
  starting transfers between devices  36.1 us (31%)
  Pallas kernels  32.3 us (28%)
  waiting for transfers between devices  29.7 us (26%)
  local copies, waits for them, and re-layouts  8.2 us (7%)
  other arithmetic  6.91 us (6%)
    ppermute x12, starting transfers between devices, line_sums(): lax.ppermute(go, 'tp', [(k, k + 1), (size - 1 - k, size - 2 - k)])  26 us
    ppermute x12, waiting for transfers between devices, line_sums(): lax.ppermute(go, 'tp', [(k, k + 1), (size - 1 - k, size - 2 - k)])  19 us
    pallas_call x2, Pallas kernels, run_project(): pl.pallas_call(functools.partial(project_kernel, chunks, shares, (reqs, s...  17.7 us
    ppermute x8, waiting for transfers between devices, shifted(): return lax.ppermute(x, axis, [(i, (i + by) % size) for i in range(size)])  10.7 us
    ppermute x8, starting transfers between devices, shifted(): return lax.ppermute(x, axis, [(i, (i + by) % size) for i in range(size)])  9.57 us
    pallas_call x1, Pallas kernels, run_scan(): pl.pallas_call(functools.partial(scan_kernel, heads, slots, reqs), grid_s...  9.38 us
    unnamed x44, local copies, waits for them, and re-layouts  6.83 us
    convert_element_type x6, other arithmetic, line_sums(): go = (go.astype(F32) + came[k - 1, d].astype(F32)).astype(BF16)  4.44 us
  transfers between devices with their start and end apart: 22, of which 6 were waited for; matrix products, arithmetic and copies ran while one was open for 6% of the time, Pallas kernels for 23%

profile of v6, /device:TPU:0, one launch (start us, length us, event | category | flops | bytes accessed | tf_op | source)
XLA Modules:
  0.0 114.3 jit_solution(15736407387105486463)
XLA Ops:
  3.4 0.8 pack.1
  4.3 3.0 %collective-permute-start.3 = (bf16[3,3072]{1,0:T(4,128)(2,1)S(1)}, bf16[3,3072]{1,0:T(4,128)(2,1)S(1)}, u32[]{:S(2)}, u32[]{:S(2)}) collective-permute-start(bf16[3,3072]{1,0:T(4,128)(2,1)S(1)} %get-tuple-element.39), channel_id=1, source_target_pairs={{0,8},{4,12},{8,0},{12,4},{1,9},{5,13},{9,1},{13,5},{2,10},{6,14},... | collective-permute-start | bytes 55304 | tf_op jit(solution)/shard_map/ppermute | solution.py:630
  7.3 1.0 collective-permute-start.4
  8.2 1.6 %copy-done.3 = f32[2,32,64,128]{3,2,1,0:T(8,128)S(1)} copy-done((f32[2,32,64,128]{3,2,1,0:T(8,128)S(1)}, f32[2,32,64,128]{3,2,1,0:T(8,128)}, u32[]{:S(2)}) %copy-start.3) | copy-done | bytes 2097176
  12.5 9.4 %local_scan.1 = (bf16[512,2048]{1,0:T(8,128)(2,1)S(1)}, bf16[2048,128]{1,0:T(8,128)(2,1)S(1)}, bf16[512,128]{1,0:T(8,128)(2,1)S(1)}, bf16[512,128]{1,0:T(8,128)(...) custom-call(s32[18]{0:T(128)S(1)} %concatenate.6.meta, ...), custom_call_target="tpu_custom_call" | custom-call | flops 8000000000 | bytes 12582912 | tf_op jit(solution)/shard_map/local_scan/pallas_call | solution.py:301
  21.9 0.8 copy-done.11
  22.7 1.8 %collective-permute-done.1.refs_2_ = bf16[1,2048,128]{2,1,0:T(8,128)(2,1)S(1)} collective-permute-done((bf16[1,2048,128]{2,1,0:T(8,128)(2,1)S(1)}, bf16[1,2048,128]{2,1,0:T(8,128)(2,1)S(1)}, u32[]{:S(2)}, u32[]{:S(2)}) %collective-permute-start.1) | collective-permute-done | bytes 524320 | tf_op jit(solution)/shard_map/ppermute | solution.py:630
  24.6 6.4 %project.2 = (bf16[256,1024]{1,0:T(8,128)(2,1)}, bf16[256,1024]{1,0:T(8,128)(2,1)}, f32[8,256]{1,0:T(8,128)}, bf16[2048,128]{1,0:T(8,128)(2,1)S(1)}) custom-call(s32[18]{0:T(128)S(1)} %concatenate.6.meta, f32[2,2048,128]{2,1,0:T(8,128)S(1)} %bitcast.14, f32[2,2048,128]{2,1,0:T(8,128)S(1)} %copy-done.6, ...), custom_call_target="tpu_custom_call" | custom-call | flops 1 | bytes 1 | tf_op jit(solution)/shard_map/project/pallas_call | solution.py:455
  30.9 4.3 %collective-permute-start.8 = (bf16[256,1024]{1,0:T(8,128)(2,1)}, bf16[256,1024]{1,0:T(8,128)(2,1)}, u32[]{:S(2)}, u32[]{:S(2)}) collective-permute-start(bf16[256,1024]{1,0:T(8,128)(2,1)} %get-tuple-element.50), channel_id=1, source_target_pairs={{0,1},{3,2},{4,5},{7,6},{8,9},{11,10},{12,13},{15,14},{16,17},{19,... | collective-permute-start | bytes 1572872 | tf_op jit(solution)/shard_map/ppermute | solution.py:498
  35.2 2.1 %collective-permute-start.6 = (bf16[256,1024]{1,0:T(8,128)(2,1)}, bf16[256,1024]{1,0:T(8,128)(2,1)}, u32[]{:S(2)}, u32[]{:S(2)}) collective-permute-start(bf16[256,1024]{1,0:T(8,128)(2,1)} %get-tuple-element.49), channel_id=1, source_target_pairs={{0,1},{3,2},{4,5},{7,6},{8,9},{11,10},{12,13},{15,14},{16,17},{19,... | collective-permute-start | bytes 1572872 | tf_op jit(solution)/shard_map/ppermute | solution.py:498
  37.9 1.6 %copy-done.2 = bf16[512,2048]{1,0:T(8,128)(2,1)S(1)} copy-done((bf16[512,2048]{1,0:T(8,128)(2,1)S(1)}, bf16[512,2048]{1,0:T(8,128)(2,1)}, u32[]{:S(2)}) %copy-start.2) | copy-done | bytes 2097176
  39.5 11.4 %project.3 = (bf16[256,1024]{1,0:T(8,128)(2,1)S(1)}, bf16[256,1024]{1,0:T(8,128)(2,1)S(1)}, bf16[256,1024]{1,0:T(8,128)(2,1)S(1)}, bf16[256,1024]{1,0:T(8,128)(2...) custom-call(s32[18]{0:T(128)S(1)} %concatenate.6.meta, ...), custom_call_target="tpu_custom_call" | custom-call | flops 1 | bytes 1 | tf_op jit(solution)/shard_map/project/pallas_call | solution.py:455
  51.1 3.0 %collective-permute-start.18 = (f32[512]{0:T(512)S(1)}, f32[512]{0:T(512)S(1)}, u32[]{:S(2)}, u32[]{:S(2)}) collective-permute-start(f32[512]{0:T(512)S(1)} %bitcast.21), channel_id=1, source_target_pairs={{0,2},{1,3},{2,0},{3,1},{4,6},{5,7},{6,4},{7,5},{8,10},{9,11},{10,... | collective-permute-start | bytes 6152 | tf_op jit(solution)/shard_map/ppermute | solution.py:630
  54.2 1.2 %ending.1.refs_0_ = bf16[2432,128]{1,0:T(8,128)(2,1)S(1)} custom-call(s32[18]{0:T(128)S(1)} %concatenate.6.meta, f32[8,512]{1,0:T(8,128)S(1)} %get-tuple-element.61.mark_ref, bf16[2048,128]{1,0:T(8,128)(2,1)S(1)} %copy-done.12, bf16[2048,128]{1,0:T(8,128)(2,1)S(1)} %get-tuple-element.46.refs_0_.start_ref, bf16[16,128]{1,0:T(8,128)(2,1)S(1)} %get-tuple-element.63.total_ref, ...), custom_call_target="tpu_custom_call" | custom-call | flops 1 | bytes 1 | tf_op jit(solution)/shard_map/ending/pallas_call | solution.py:548
  55.3 0.9 collective-permute-start.20
  56.2 3.3 %collective-permute-start.14 = (bf16[256,1024]{1,0:T(8,128)(2,1)S(1)}, bf16[256,1024]{1,0:T(8,128)(2,1)S(1)}, u32[]{:S(2)}, u32[]{:S(2)}) collective-permute-start(bf16[256,1024]{1,0:T(8,128)(2,1)S(1)} %get-tuple-element.60), channel_id=1, source_target_pairs={{0,1},{3,2},{4,5},{7,6},{8,9},{11,10},{12,13},{15,14},{16,17},{19,... | collective-permute-start | bytes 1572872 | tf_op jit(solution)/shard_map/ppermute | solution.py:498
  59.5 1.4 %add_convert_fusion.4 = bf16[256,1024]{1,0:T(8,128)(2,1)S(1)} fusion(bf16[256,1024]{1,0:T(8,128)(2,1)} %collective-permute-done.8, bf16[256,1024]{1,0:T(8,128)(2,1)} %get-tuple-element.49), kind=kLoop, calls=%fused_computation.8 | loop fusion | flops 1048576 | bytes 1572864 | tf_op jit(solution)/shard_map/convert_element_type | solution.py:497
  61.6 1.2 %add_convert_fusion.5 = bf16[256,1024]{1,0:T(8,128)(2,1)S(1)} fusion(bf16[256,1024]{1,0:T(8,128)(2,1)} %collective-permute-done.6, bf16[256,1024]{1,0:T(8,128)(2,1)S(1)} %get-tuple-element.48), kind=kLoop, calls=%fused_computation.9 | loop fusion | flops 1048576 | bytes 1572864 | tf_op jit(solution)/shard_map/convert_element_type | solution.py:497
  62.9 5.9 %collective-permute-done.14 = bf16[256,1024]{1,0:T(8,128)(2,1)S(1)} collective-permute-done((bf16[256,1024]{1,0:T(8,128)(2,1)S(1)}, bf16[256,1024]{1,0:T(8,128)(2,1)S(1)}, u32[]{:S(2)}, u32[]{:S(2)}) %collective-permute-start.14) | collective-permute-done | bytes 524320 | tf_op jit(solution)/shard_map/ppermute | solution.py:498
  68.8 4.4 %collective-permute-start.12 = (bf16[256,1024]{1,0:T(8,128)(2,1)S(1)}, bf16[256,1024]{1,0:T(8,128)(2,1)S(1)}, u32[]{:S(2)}, u32[]{:S(2)}) collective-permute-start(bf16[256,1024]{1,0:T(8,128)(2,1)S(1)} %get-tuple-element.59), channel_id=1, source_target_pairs={{0,1},{3,2},{4,5},{7,6},{8,9},{11,10},{12,13},{15,14},{16,17},{19,... | collective-permute-start | bytes 1572872 | tf_op jit(solution)/shard_map/ppermute | solution.py:498
  74.1 1.2 %add_convert_fusion.3 = bf16[256,1024]{1,0:T(8,128)(2,1)S(1)} fusion(bf16[256,1024]{1,0:T(8,128)(2,1)S(1)} %collective-permute-done.9, bf16[256,1024]{1,0:T(8,128)(2,1)} %get-tuple-element.50), kind=kLoop, calls=%fused_computation.7 | loop fusion | flops 1048576 | bytes 1572864 | tf_op jit(solution)/shard_map/convert_element_type | solution.py:497
  75.3 4.0 %collective-permute-start.5 = (bf16[256,1024]{1,0:T(8,128)(2,1)S(1)}, bf16[256,1024]{1,0:T(8,128)(2,1)S(1)}, u32[]{:S(2)}, u32[]{:S(2)}) collective-permute-start(bf16[256,1024]{1,0:T(8,128)(2,1)S(1)} %get-tuple-element.48), channel_id=1, source_target_pairs={{0,1},{3,2},{4,5},{7,6},{8,9},{11,10},{12,13},{15,14},{16,17},{19,... | collective-permute-start | bytes 1572872 | tf_op jit(solution)/shard_map/ppermute | solution.py:498
  79.3 6.2 %collective-permute-done.12 = bf16[256,1024]{1,0:T(8,128)(2,1)S(1)} collective-permute-done((bf16[256,1024]{1,0:T(8,128)(2,1)S(1)}, bf16[256,1024]{1,0:T(8,128)(2,1)S(1)}, u32[]{:S(2)}, u32[]{:S(2)}) %collective-permute-start.12) | collective-permute-done | bytes 524320 | tf_op jit(solution)/shard_map/ppermute | solution.py:498
  86.2 1.3 %collective-permute-start.10 = (bf16[256,1024]{1,0:T(8,128)(2,1)S(1)}, bf16[256,1024]{1,0:T(8,128)(2,1)S(1)}, u32[]{:S(2)}, u32[]{:S(2)}) collective-permute-start(bf16[256,1024]{1,0:T(8,128)(2,1)S(1)} %add_convert_fusion.3), channel_id=1, source_target_pairs={{2,3},{1,0},{6,7},{5,4},{10,11},{9,8},{14,15},{13,12},{18,19},{17,... | collective-permute-start | bytes 1572872 | tf_op jit(solution)/shard_map/ppermute | solution.py:498
  88.4 0.9 collective-permute-start.19
  89.5 8.8 %collective-permute-done.19 = f32[512]{0:T(512)S(1)} collective-permute-done((f32[512]{0:T(512)S(1)}, f32[512]{0:T(512)S(1)}, u32[]{:S(2)}, u32[]{:S(2)}) %collective-permute-start.19) | collective-permute-done | bytes 2080 | tf_op jit(solution)/shard_map/ppermute | solution.py:630
  98.4 2.6 %collective-permute-start.11 = (bf16[256,1024]{1,0:T(8,128)(2,1)S(1)}, bf16[256,1024]{1,0:T(8,128)(2,1)S(1)}, u32[]{:S(2)}, u32[]{:S(2)}) collective-permute-start(bf16[256,1024]{1,0:T(8,128)(2,1)S(1)} %get-tuple-element.58), channel_id=1, source_target_pairs={{0,1},{3,2},{4,5},{7,6},{8,9},{11,10},{12,13},{15,14},{16,17},{19,... | collective-permute-start | bytes 1572872 | tf_op jit(solution)/shard_map/ppermute | solution.py:498
  101.7 1.3 %collective-permute-start.16 = (bf16[256,1024]{1,0:T(8,128)(2,1)S(1)}, bf16[256,1024]{1,0:T(8,128)(2,1)S(1)}, u32[]{:S(2)}, u32[]{:S(2)}) collective-permute-start(bf16[256,1024]{1,0:T(8,128)(2,1)S(1)} %add_convert_fusion), channel_id=1, source_target_pairs={{2,3},{1,0},{6,7},{5,4},{10,11},{9,8},{14,15},{13,12},{18,19},{17,... | collective-permute-start | bytes 1572872 | tf_op jit(solution)/shard_map/ppermute | solution.py:498
  104.0 1.8 %land.1 = (f32[2048,128]{1,0:T(8,128)}, bf16[3,2048]{1,0:T(4,128)(2,1)}, bf16[3,1024]{1,0:T(4,128)(2,1)}) custom-call(s32[18]{0:T(128)S(1)} %concatenate.6.meta, bf16[2432,128]{1,0:T(8,128)(2,1)S(1)} %ending.1.refs_0_, bf16[2432,128]{1,0:T(8,128)(2,1)S(1)} %collective-permute-done.20.refs_1_, bf16[2432,128]{1,0:T(8,128)(2,1)S(1)} %collective-permute-done.21.refs_2_), custom_call_target="tpu_custom_call" | custom-call | flops 1 | bytes 1 | tf_op jit(solution)/shard_map/land/pallas_call | solution.py:614
  105.8 1.8 %collective-permute-done.11 = bf16[256,1024]{1,0:T(8,128)(2,1)S(1)} collective-permute-done((bf16[256,1024]{1,0:T(8,128)(2,1)S(1)}, bf16[256,1024]{1,0:T(8,128)(2,1)S(1)}, u32[]{:S(2)}, u32[]{:S(2)}) %collective-permute-start.11) | collective-permute-done | bytes 524320 | tf_op jit(solution)/shard_map/ppermute | solution.py:498
  107.7 5.1 %collective-permute-done.16 = bf16[256,1024]{1,0:T(8,128)(2,1)S(1)} collective-permute-done((bf16[256,1024]{1,0:T(8,128)(2,1)S(1)}, bf16[256,1024]{1,0:T(8,128)(2,1)S(1)}, u32[]{:S(2)}, u32[]{:S(2)}) %collective-permute-start.16) | collective-permute-done | bytes 524320 | tf_op jit(solution)/shard_map/ppermute | solution.py:498
  113.1 1.1 %fusion = bf16[512,1024]{1,0:T(8,128)(2,1)} fusion(f32[256,1024]{1,0:T(8,128)S(1)} %convert_add_fusion, f32[256,1024]{1,0:T(8,128)S(1)} %convert_add_fusion.1, f32[512]{0:T(512)S(1)} %rsqrt_select_fusion), kind=kLoop, calls=%fused_computation.1 | loop fusion | flops 1572864 | bytes 3147776 | tf_op jit(solution)/shard_map/convert_element_type | solution.py:715
  (77 shorter events, 11.7 us)
Async XLA Ops:
  0.6 7.6 %collective-permute-start = (f32[2,2048,128]{2,1,0:T(8,128)}, f32[2,2048,128]{2,1,0:T(8,128)S(1)}, u32[]{:S(2)}, u32[]{:S(2)}) collective-permute-start(f32[2,2048,128]{2,1,0:T(8,128)} %bitcast.12), channel_id=1, source_target_pairs={{0,4},{4,0},{8,12},{12,8},{1,5},{5,1},{9,13},{13,9},{2,6},{6,2},{1... | collective-permute-start | bytes 6291464 | tf_op jit(solution)/shard_map/ppermute | solution.py:634
  4.2 7.4 %collective-permute-start.2 = (bf16[3,3072]{1,0:T(4,128)(2,1)S(1)}, bf16[3,3072]{1,0:T(4,128)(2,1)S(1)}, u32[]{:S(2)}, u32[]{:S(2)}) collective-permute-start(bf16[3,3072]{1,0:T(4,128)(2,1)S(1)} %get-tuple-element.38), channel_id=1, source_target_pairs={{0,4},{4,8},{8,12},{12,0},{1,5},{5,9},{9,13},{13,1},{2,6},{6,10},{... | collective-permute-start | bytes 55304 | tf_op jit(solution)/shard_map/ppermute | solution.py:630
  4.3 7.3 %collective-permute-start.3 = (bf16[3,3072]{1,0:T(4,128)(2,1)S(1)}, bf16[3,3072]{1,0:T(4,128)(2,1)S(1)}, u32[]{:S(2)}, u32[]{:S(2)}) collective-permute-start(bf16[3,3072]{1,0:T(4,128)(2,1)S(1)} %get-tuple-element.39), channel_id=1, source_target_pairs={{0,8},{4,12},{8,0},{12,4},{1,9},{5,13},{9,1},{13,5},{2,10},{6,14},... | collective-permute-start | bytes 55304 | tf_op jit(solution)/shard_map/ppermute | solution.py:630
  7.3 4.4 %copy-start.20 = (f32[32]{0:T(128)S(1)}, f32[32]{0:T(128)}, u32[]{:S(2)}) copy-start(f32[32]{0:T(128)} %refs_10_.1) | copy-start | bytes 388
  7.3 4.4 %collective-permute-start.4 = (bf16[3,3072]{1,0:T(4,128)(2,1)S(1)}, bf16[3,3072]{1,0:T(4,128)(2,1)S(1)}, u32[]{:S(2)}, u32[]{:S(2)}) collective-permute-start(bf16[3,3072]{1,0:T(4,128)(2,1)S(1)} %get-tuple-element.40), channel_id=1, source_target_pairs={{0,12},{4,0},{8,4},{12,8},{1,13},{5,1},{9,5},{13,9},{2,14},{6,2},{... | collective-permute-start | bytes 55304 | tf_op jit(solution)/shard_map/ppermute | solution.py:630
  11.2 13.4 %collective-permute-start.1 = (bf16[1,2048,128]{2,1,0:T(8,128)(2,1)S(1)}, bf16[1,2048,128]{2,1,0:T(8,128)(2,1)S(1)}, u32[]{:S(2)}, u32[]{:S(2)}) collective-permute-start(bf16[1,2048,128]{2,1,0:T(8,128)(2,1)S(1)} %get-tuple-element.36), channel_id=1, source_target_pairs={{0,8},{4,12},{8,0},{12,4},{1,9},{5,13},{9,1},{13,5},{2,10},{6,14},... | collective-permute-start | bytes 1572872 | tf_op jit(solution)/shard_map/ppermute | solution.py:630
  12.4 12.1 %copy-start = (bf16[512,2048]{1,0:T(8,128)(2,1)S(1)}, bf16[512,2048]{1,0:T(8,128)(2,1)}, u32[]{:S(2)}) copy-start(bf16[512,2048]{1,0:T(8,128)(2,1)} %refs_2_.1) | copy-start | bytes 6291460
  12.5 12.1 %copy-start.4 = (f32[2,32,64,128]{3,2,1,0:T(8,128)S(1)}, f32[2,32,64,128]{3,2,1,0:T(8,128)}, u32[]{:S(2)}) copy-start(f32[2,32,64,128]{3,2,1,0:T(8,128)} %param.27) | copy-start | bytes 6291460
  12.5 12.1 %copy-start.6 = (f32[2,2048,128]{2,1,0:T(8,128)S(1)}, f32[2,2048,128]{2,1,0:T(8,128)}, u32[]{:S(2)}) copy-start(f32[2,2048,128]{2,1,0:T(8,128)} %copy-done.5) | copy-start | bytes 6291460
  12.5 12.1 %copy-start.13 = (f32[2048]{0:T(1024)S(1)}, f32[2048]{0:T(1024)}, u32[]{:S(2)}) copy-start(f32[2048]{0:T(1024)} %param.23) | copy-start | bytes 24580
  22.7 8.2 %copy-start.1 = (bf16[512,2048]{1,0:T(8,128)(2,1)}, bf16[512,2048]{1,0:T(8,128)(2,1)S(1)}, u32[]{:S(2)}) copy-start(bf16[512,2048]{1,0:T(8,128)(2,1)S(1)} %get-tuple-element.42.refs_3_.refs_1_) | copy-start | bytes 6291460
  24.5 12.8 %copy-start.21 = (s32[4]{0:T(128)S(1)}, s32[4]{0:T(128)}, u32[]{:S(2)}) copy-start(s32[4]{0:T(128)} %param.33) | copy-start | bytes 52
  30.9 23.2 %collective-permute-start.8 = (bf16[256,1024]{1,0:T(8,128)(2,1)}, bf16[256,1024]{1,0:T(8,128)(2,1)}, u32[]{:S(2)}, u32[]{:S(2)}) collective-permute-start(bf16[256,1024]{1,0:T(8,128)(2,1)} %get-tuple-element.50), channel_id=1, source_target_pairs={{0,1},{3,2},{4,5},{7,6},{8,9},{11,10},{12,13},{15,14},{16,17},{19,... | collective-permute-start | bytes 1572872 | tf_op jit(solution)/shard_map/ppermute | solution.py:498
  35.2 25.7 %collective-permute-start.6 = (bf16[256,1024]{1,0:T(8,128)(2,1)}, bf16[256,1024]{1,0:T(8,128)(2,1)}, u32[]{:S(2)}, u32[]{:S(2)}) collective-permute-start(bf16[256,1024]{1,0:T(8,128)(2,1)} %get-tuple-element.49), channel_id=1, source_target_pairs={{0,1},{3,2},{4,5},{7,6},{8,9},{11,10},{12,13},{15,14},{16,17},{19,... | collective-permute-start | bytes 1572872 | tf_op jit(solution)/shard_map/ppermute | solution.py:498
  39.5 14.7 %copy-start.8 = (bf16[512,2048]{1,0:T(8,128)(2,1)S(1)}, bf16[512,2048]{1,0:T(8,128)(2,1)}, u32[]{:S(2)}) copy-start(bf16[512,2048]{1,0:T(8,128)(2,1)} %x_ref.1) | copy-start | bytes 6291460
  39.5 14.7 %copy-start.10 = (bf16[512,1024]{1,0:T(8,128)(2,1)S(1)}, bf16[512,1024]{1,0:T(8,128)(2,1)}, u32[]{:S(2)}) copy-start(bf16[512,1024]{1,0:T(8,128)(2,1)} %bc_ref.1) | copy-start | bytes 3145732
  39.5 14.7 %copy-start.12 = (bf16[2048,128]{1,0:T(8,128)(2,1)S(1)}, bf16[2048,128]{1,0:T(8,128)(2,1)}, u32[]{:S(2)}) copy-start(bf16[2048,128]{1,0:T(8,128)(2,1)} %copy-done.11) | copy-start | bytes 1572868
  50.9 24.5 %collective-permute-start.17 = (f32[512]{0:T(512)S(1)}, f32[512]{0:T(512)S(1)}, u32[]{:S(2)}, u32[]{:S(2)}) collective-permute-start(f32[512]{0:T(512)S(1)} %bitcast.20), channel_id=1, source_target_pairs={{0,1},{1,2},{2,3},{3,0},{4,5},{5,6},{6,7},{7,4},{8,9},{9,10},{10,1... | collective-permute-start | bytes 6152 | tf_op jit(solution)/shard_map/ppermute | solution.py:630
  51.1 37.3 %collective-permute-start.18 = (f32[512]{0:T(512)S(1)}, f32[512]{0:T(512)S(1)}, u32[]{:S(2)}, u32[]{:S(2)}) collective-permute-start(f32[512]{0:T(512)S(1)} %bitcast.21), channel_id=1, source_target_pairs={{0,2},{1,3},{2,0},{3,1},{4,6},{5,7},{6,4},{7,5},{8,10},{9,11},{10,... | collective-permute-start | bytes 6152 | tf_op jit(solution)/shard_map/ppermute | solution.py:630
  55.3 30.9 %collective-permute-start.20 = (bf16[2432,128]{1,0:T(8,128)(2,1)S(1)}, bf16[2432,128]{1,0:T(8,128)(2,1)S(1)}, u32[]{:S(2)}, u32[]{:S(2)}) collective-permute-start(bf16[2432,128]{1,0:T(8,128)(2,1)S(1)} %ending.1.refs_0_), channel_id=1, source_target_pairs={{0,8},{4,12},{8,0},{12,4},{1,9},{5,13},{9,1},{13,5},{2,10},{6,14},... | collective-permute-start | bytes 1867784 | tf_op jit(solution)/shard_map/ppermute | solution.py:630
  56.2 12.5 %collective-permute-start.14 = (bf16[256,1024]{1,0:T(8,128)(2,1)S(1)}, bf16[256,1024]{1,0:T(8,128)(2,1)S(1)}, u32[]{:S(2)}, u32[]{:S(2)}) collective-permute-start(bf16[256,1024]{1,0:T(8,128)(2,1)S(1)} %get-tuple-element.60), channel_id=1, source_target_pairs={{0,1},{3,2},{4,5},{7,6},{8,9},{11,10},{12,13},{15,14},{16,17},{19,... | collective-permute-start | bytes 1572872 | tf_op jit(solution)/shard_map/ppermute | solution.py:498
  60.9 12.4 %collective-permute-start.9 = (bf16[256,1024]{1,0:T(8,128)(2,1)S(1)}, bf16[256,1024]{1,0:T(8,128)(2,1)S(1)}, u32[]{:S(2)}, u32[]{:S(2)}) collective-permute-start(bf16[256,1024]{1,0:T(8,128)(2,1)S(1)} %add_convert_fusion.4), channel_id=1, source_target_pairs={{1,2},{2,1},{5,6},{6,5},{9,10},{10,9},{13,14},{14,13},{17,18},{18,... | collective-permute-start | bytes 1572872 | tf_op jit(solution)/shard_map/ppermute | solution.py:498
  68.8 16.7 %collective-permute-start.12 = (bf16[256,1024]{1,0:T(8,128)(2,1)S(1)}, bf16[256,1024]{1,0:T(8,128)(2,1)S(1)}, u32[]{:S(2)}, u32[]{:S(2)}) collective-permute-start(bf16[256,1024]{1,0:T(8,128)(2,1)S(1)} %get-tuple-element.59), channel_id=1, source_target_pairs={{0,1},{3,2},{4,5},{7,6},{8,9},{11,10},{12,13},{15,14},{16,17},{19,... | collective-permute-start | bytes 1572872 | tf_op jit(solution)/shard_map/ppermute | solution.py:498
  73.4 15.9 %collective-permute-start.15 = (bf16[256,1024]{1,0:T(8,128)(2,1)S(1)}, bf16[256,1024]{1,0:T(8,128)(2,1)S(1)}, u32[]{:S(2)}, u32[]{:S(2)}) collective-permute-start(bf16[256,1024]{1,0:T(8,128)(2,1)S(1)} %add_convert_fusion.1), channel_id=1, source_target_pairs={{1,2},{2,1},{5,6},{6,5},{9,10},{10,9},{13,14},{14,13},{17,18},{18,... | collective-permute-start | bytes 1572872 | tf_op jit(solution)/shard_map/ppermute | solution.py:498
  75.3 25.7 %collective-permute-start.5 = (bf16[256,1024]{1,0:T(8,128)(2,1)S(1)}, bf16[256,1024]{1,0:T(8,128)(2,1)S(1)}, u32[]{:S(2)}, u32[]{:S(2)}) collective-permute-start(bf16[256,1024]{1,0:T(8,128)(2,1)S(1)} %get-tuple-element.48), channel_id=1, source_target_pairs={{0,1},{3,2},{4,5},{7,6},{8,9},{11,10},{12,13},{15,14},{16,17},{19,... | collective-permute-start | bytes 1572872 | tf_op jit(solution)/shard_map/ppermute | solution.py:498
  85.5 16.2 %collective-permute-start.7 = (bf16[256,1024]{1,0:T(8,128)(2,1)S(1)}, bf16[256,1024]{1,0:T(8,128)(2,1)S(1)}, u32[]{:S(2)}, u32[]{:S(2)}) collective-permute-start(bf16[256,1024]{1,0:T(8,128)(2,1)S(1)} %add_convert_fusion.5), channel_id=1, source_target_pairs={{1,2},{2,1},{5,6},{6,5},{9,10},{10,9},{13,14},{14,13},{17,18},{18,... | collective-permute-start | bytes 1572872 | tf_op jit(solution)/shard_map/ppermute | solution.py:498
  86.2 17.5 %collective-permute-start.10 = (bf16[256,1024]{1,0:T(8,128)(2,1)S(1)}, bf16[256,1024]{1,0:T(8,128)(2,1)S(1)}, u32[]{:S(2)}, u32[]{:S(2)}) collective-permute-start(bf16[256,1024]{1,0:T(8,128)(2,1)S(1)} %add_convert_fusion.3), channel_id=1, source_target_pairs={{2,3},{1,0},{6,7},{5,4},{10,11},{9,8},{14,15},{13,12},{18,19},{17,... | collective-permute-start | bytes 1572872 | tf_op jit(solution)/shard_map/ppermute | solution.py:498
  88.4 9.9 %collective-permute-start.19 = (f32[512]{0:T(512)S(1)}, f32[512]{0:T(512)S(1)}, u32[]{:S(2)}, u32[]{:S(2)}) collective-permute-start(f32[512]{0:T(512)S(1)} %bitcast.22), channel_id=1, source_target_pairs={{0,3},{1,0},{2,1},{3,2},{4,7},{5,4},{6,5},{7,6},{8,11},{9,8},{10,9... | collective-permute-start | bytes 6152 | tf_op jit(solution)/shard_map/ppermute | solution.py:630
  89.3 14.7 %collective-permute-start.21 = (bf16[2432,128]{1,0:T(8,128)(2,1)S(1)}, bf16[2432,128]{1,0:T(8,128)(2,1)S(1)}, u32[]{:S(2)}, u32[]{:S(2)}) collective-permute-start(bf16[2432,128]{1,0:T(8,128)(2,1)S(1)} %route.1), channel_id=1, source_target_pairs={{0,4},{4,0},{8,12},{12,8},{1,5},{5,1},{9,13},{13,9},{2,6},{6,2},{1... | collective-permute-start | bytes 1867784 | tf_op jit(solution)/shard_map/ppermute | solution.py:634
  98.4 9.3 %collective-permute-start.11 = (bf16[256,1024]{1,0:T(8,128)(2,1)S(1)}, bf16[256,1024]{1,0:T(8,128)(2,1)S(1)}, u32[]{:S(2)}, u32[]{:S(2)}) collective-permute-start(bf16[256,1024]{1,0:T(8,128)(2,1)S(1)} %get-tuple-element.58), channel_id=1, source_target_pairs={{0,1},{3,2},{4,5},{7,6},{8,9},{11,10},{12,13},{15,14},{16,17},{19,... | collective-permute-start | bytes 1572872 | tf_op jit(solution)/shard_map/ppermute | solution.py:498
  101.0 6.6 %collective-permute-start.13 = (bf16[256,1024]{1,0:T(8,128)(2,1)S(1)}, bf16[256,1024]{1,0:T(8,128)(2,1)S(1)}, u32[]{:S(2)}, u32[]{:S(2)}) collective-permute-start(bf16[256,1024]{1,0:T(8,128)(2,1)S(1)} %add_convert_fusion.2), channel_id=1, source_target_pairs={{1,2},{2,1},{5,6},{6,5},{9,10},{10,9},{13,14},{14,13},{17,18},{18,... | collective-permute-start | bytes 1572872 | tf_op jit(solution)/shard_map/ppermute | solution.py:498
  101.7 11.1 %collective-permute-start.16 = (bf16[256,1024]{1,0:T(8,128)(2,1)S(1)}, bf16[256,1024]{1,0:T(8,128)(2,1)S(1)}, u32[]{:S(2)}, u32[]{:S(2)}) collective-permute-start(bf16[256,1024]{1,0:T(8,128)(2,1)S(1)} %add_convert_fusion), channel_id=1, source_target_pairs={{2,3},{1,0},{6,7},{5,4},{10,11},{9,8},{14,15},{13,12},{18,19},{17,... | collective-permute-start | bytes 1572872 | tf_op jit(solution)/shard_map/ppermute | solution.py:498
  (12 other events, 23.9 us)
